TPU v7x, 32 devices: a whole 2x2x4 slice. The times are simulated.
32 devices in a mesh: groups: 1, sector: 32 (over z, y, x, core).
Axes of the slice: x: 2, y: 2, z: 4, core: 2. Of those that a mesh axis runs over, the one named last changes fastest.
Arguments:
- wavefunction: bfloat16 [512, 128, 128], P(('groups', 'sector')), may hold values from -16 to 16
- onsite_energy: float32 [512], P(('groups', 'sector')), may hold values from 0.3 to 5
- left_env: bfloat16 [128, 32, 128, 128], P(('groups', 'sector')), may hold values from -0.09375 to 0.09375
- right_env: bfloat16 [128, 32, 128, 128], P(('groups', 'sector')), may hold values from -0.5 to 0.5
- source_device: int32 [512, 16], P(('groups', 'sector')), may hold values from 0 to 31, all different within a row; in each aligned block of 16 rows (0 to 15, 16 to 31, ...) at most 8 rows name the same one
- source_block: int32 [512, 16], P(('groups', 'sector')), may hold values from 0 to 15
Outputs:
- applied: bfloat16 [512, 128, 128], P(('groups', 'sector'))
- residual: bfloat16 [512, 128, 128], P(('groups', 'sector'))
- quotient: float32 [1], P('groups')
Inputs may be any that keep to these rules, and one draw needn't show every extreme that they name: `source_device`: each row names 16 different devices; among the 16 rows of one device every device is named by exactly 8 rows.
All inputs are finite; a program needn't handle non-finite values.
Results may differ from a plain program's by a relative error of at most 0.004.
Values may be sent and summed in bfloat16 or wider, within the bound.
No kernel may reach another device: no remote copies, remote signals or barrier semaphores. Data moves between devices by JAX's collectives and lax.ppermute only.
A program may use at most 128 MiB of HBM per device.

v0:
```python
import jax
import jax.numpy as jnp
from jax import lax
from jax.sharding import PartitionSpec as P


def earlier_count(targets):
    length = targets.shape[0]
    row_iota = lax.broadcasted_iota(jnp.int32, (length, length), 0)
    col_iota = lax.broadcasted_iota(jnp.int32, (length, length), 1)
    earlier = (targets[:, None] == targets[None, :]) & (col_iota < row_iota)
    return jnp.sum(earlier.astype(jnp.int32), axis=1)


def local(wavefunction, onsite_energy, left_env, right_env, source_device, source_block):
    owners = lax.axis_size("sector")
    sec_dev = wavefunction.shape[0]
    block_size = wavefunction.shape[1]
    left_count = left_env.shape[0]
    right_count = right_env.shape[0]
    channels = left_env.shape[1]
    hop_count = source_device.shape[1]
    local_count = channels - hop_count
    capacity = sec_dev * hop_count // owners
    targets = source_device.reshape(-1)
    wanted = source_block.reshape(-1)
    slot_index = targets * capacity + earlier_count(targets)
    asked_for = jnp.zeros((owners * capacity,), jnp.int32).at[slot_index].set(wanted)
    asked_for = asked_for.reshape(owners, capacity)
    received = lax.all_to_all(
        wavefunction[lax.all_to_all(asked_for, "sector", split_axis=0, concat_axis=0, tiled=True)],
        "sector",
        split_axis=0,
        concat_axis=0,
        tiled=True,
    )
    fetched = received.reshape(owners * capacity, block_size, block_size)[slot_index]
    fetched = fetched.reshape(left_count, right_count, hop_count, block_size, block_size)
    blocks_grid = wavefunction.reshape(left_count, right_count, block_size, block_size)
    spread_out = jnp.broadcast_to(
        blocks_grid[:, :, None], (left_count, right_count, local_count, block_size, block_size)
    )
    inputs_all = jnp.concatenate([spread_out, fetched], axis=2)
    middle = jnp.einsum(
        "ijhab,jhbc->ijhac", inputs_all, right_env, preferred_element_type=jnp.float32
    ).astype(jnp.bfloat16)
    summed = jnp.einsum("ihxa,ijhac->ijxc", left_env, middle, preferred_element_type=jnp.float32)
    psi_float = wavefunction.astype(jnp.float32)
    hpsi = (
        summed.reshape(sec_dev, block_size, block_size) + onsite_energy[:, None, None] * psi_float
    )
    numerator, denominator = lax.psum(
        (jnp.sum(psi_float * hpsi), jnp.sum(psi_float * psi_float)), "sector"
    )
    quotient = numerator / denominator
    residual = (hpsi - quotient * psi_float).astype(jnp.bfloat16)
    return (hpsi.astype(jnp.bfloat16), residual, quotient.reshape(1))


def solution(mesh):
    return jax.shard_map(
        local,
        mesh=mesh,
        in_specs=(
            P(("groups", "sector"), None, None),
            P(("groups", "sector")),
            P(("groups", "sector"), None, None, None),
            P(("groups", "sector"), None, None, None),
            P(("groups", "sector"), None),
            P(("groups", "sector"), None),
        ),
        out_specs=(
            P(("groups", "sector"), None, None),
            P(("groups", "sector"), None, None),
            P("groups"),
        ),
        check_vma=False,
    )
```

profile of v0, /device:TPU:0, one launch (start us, length us, event | category | flops | bytes accessed | tf_op | source)
XLA Modules:
  0.0 292.3 jit_solution(8924627581809581193)
XLA Ops:
  0.6 0.8 eq.15
  1.4 0.7 broadcast_multiply_fusion
  2.1 0.8 reshape.111
  2.9 0.2 convert_reduce_fusion
  3.1 0.1 mul.38
  3.2 1.4 scatter_custom_fusion
  4.6 0.1 all_to_all.11
  4.6 14.3 %all_to_all.17 = s32[32,1,8]{2,1,0:T(1,128)S(1)} all-to-all(s32[32,1,8]{2,1,0:T(1,128)S(1)} %bitcast.34), channel_id=1, replica_groups=mesh['groups'=1,'sector'=32] {'sector'}, dimensions={0} | all-to-all | bytes 2048 | tf_op jit(solution)/shard_map/all_to_all | solution.py:31
  18.9 0.1 reshape.93
  19.0 9.6 %gather_fusion = bf16[256,128,128]{2,1,0:T(8,128)(2,1)} fusion(bf16[16,128,128]{2,1,0:T(8,128)(2,1)} %param.6, s32[1024]{0:T(1024)S(1)} %pad_clamp_fusion.1), kind=kCustom, calls=%fused_computation | custom fusion | bytes 16778240 | tf_op jit(solution)/shard_map/gather | solution.py:31
  28.6 3.7 %all-to-all-start.1 = ((bf16[32,8,128,128]{3,2,1,0:T(8,128)(2,1)}), bf16[32,8,128,128]{3,2,1,0:T(8,128)(2,1)}, u32[]{:S(2)}, u32[]{:S(2)}) async-start(bf16[32,8,128,128]{3,2,1,0:T(8,128)(2,1)} %bitcast.31), calls=%async_computation.1 | async-start | bytes 16777216 | tf_op jit(solution)/shard_map/all_to_all | solution.py:30
  32.3 186.1 %all-to-all-done.1 = bf16[32,8,128,128]{3,2,1,0:T(8,128)(2,1)} async-done(((bf16[32,8,128,128]{3,2,1,0:T(8,128)(2,1)}), bf16[32,8,128,128]{3,2,1,0:T(8,128)(2,1)}, u32[]{:S(2)}, u32[]{:S(2)}) %all-to-all-start.1) | async-done | bytes 8388640 | tf_op jit(solution)/shard_map/all_to_all | solution.py:30
  218.5 0.0 copy-start
  218.5 12.0 %gather_fusion.1 = bf16[256,128,128]{2,1,0:T(8,128)(2,1)} fusion(bf16[256,128,128]{2,1,0:T(8,128)(2,1)} %bitcast.6, s32[1024]{0:T(1024)S(1)} %pad_clamp_fusion), kind=kCustom, calls=%fused_computation.1 | custom fusion | bytes 16778240 | tf_op jit(solution)/shard_map/gather | solution.py:37
  230.5 0.0 copy-done
  230.5 5.3 %broadcast_in_dim.5 = bf16[4,4,16,128,128]{4,3,2,1,0:T(8,128)(2,1)} broadcast(bf16[4,4,128,128]{3,2,1,0:T(8,128)(2,1)S(1)} %bitcast.30), dimensions={0,1,3,4} | broadcast | bytes 8912896 | tf_op jit(solution)/shard_map/broadcast_in_dim | solution.py:40
  235.9 0.0 copy-start.1
  235.9 14.0 %fusion.4 = f32[4,4,128,128,1]{3,2,4,1,0:T(8,128)S(1)} fusion(bf16[4,4,16,128,128]{4,3,2,1,0:T(8,128)(2,1)} %bitcast.32, bf16[4,4,16,128,128]{4,3,2,1,0:T(8,128)(2,1)} %broadcast_in_dim.5, bf16[4,32,128,128]{3,2,1,0:T(8,128)(2,1)} %param.8, bf16[4,32,128,128]{3,2,1,0:T(8,128)(2,1)} %param.9), kind=kOutput, calls=%fused_computation.7 | convolution fusion | flops 4311744512 | bytes 26214400 | tf_op jit(solution)/shard_map/ihxa,ijhac->ijxc/dot_general | solution.py:47
  249.9 0.3 copy.16
  250.2 0.0 copy-done.1
  250.2 1.1 fusion.16
  251.3 37.1 %all-reduce = (f32[]{:T(128)}, f32[]{:T(128)}) all-reduce(f32[]{:T(128)} %get-tuple-element.4, f32[]{:T(128)} %get-tuple-element.3), channel_id=1, replica_groups=mesh['groups'=1,'sector'=32] {'sector'}, use_global_device_ids=true, to_apply=%region_3.0 | all-reduce | flops 2 | bytes 16 | tf_op jit(solution)/shard_map/psum | solution.py:52
  289.8 1.3 fusion.18
  (4 shorter events, 0.0 us)
Async XLA Ops:
  28.6 189.8 %all-to-all-start.1 = ((bf16[32,8,128,128]{3,2,1,0:T(8,128)(2,1)}), bf16[32,8,128,128]{3,2,1,0:T(8,128)(2,1)}, u32[]{:S(2)}, u32[]{:S(2)}) async-start(bf16[32,8,128,128]{3,2,1,0:T(8,128)(2,1)} %bitcast.31), calls=%async_computation.1 | async-start | bytes 16777216 | tf_op jit(solution)/shard_map/all_to_all | solution.py:30
  218.5 12.1 %copy-start = (bf16[16,128,128]{2,1,0:T(8,128)(2,1)S(1)}, bf16[16,128,128]{2,1,0:T(8,128)(2,1)}, u32[]{:S(2)}) copy-start(bf16[16,128,128]{2,1,0:T(8,128)(2,1)} %param.6) | copy-start | bytes 1572868
  235.9 14.4 %copy-start.1 = (f32[16]{0:T(128)S(1)}, f32[16]{0:T(128)}, u32[]{:S(2)}) copy-start(f32[16]{0:T(128)} %param.7) | copy-start | bytes 196
where the time goes:
time: 294 us; the launch traced here: 292 us
  waiting for transfers between devices  186 us (63%)
  blocking collectives  51.4 us (17%)
  local copies, waits for them, and re-layouts  30.6 us (10%)
  matrix products  14 us (5%)
  starting transfers between devices  3.67 us (1%)
  other arithmetic  3.31 us (1%)
  between operations  3.17 us (1%)
    all_to_all x1, waiting for transfers between devices, local(): lax.all_to_all(wavefunction[lax.all_to_all(asked_for, 'sector', split_axi...  186 us
    psum x1, blocking collectives, local(): lax.psum((jnp.sum(psi_float * hpsi), jnp.sum(psi_float * psi_float)), 'se...  37.1 us
    all_to_all x1, blocking collectives, local(): lax.all_to_all(asked_for, 'sector', split_axis=0, concat_axis=0, tiled=True)  14.3 us
    dot_general x1, matrix products, local(): jnp.einsum('ihxa,ijhac->ijxc', left_env, middle, preferred_element_type=j...  14 us
    gather x1, local copies, waits for them, and re-layouts, local(): received.reshape(owners * capacity, block_size, block_size)[slot_index]  12 us
    gather x1, local copies, waits for them, and re-layouts, local(): wavefunction[lax.all_to_all(asked_for, 'sector', split_axis=0, concat_axi...  9.63 us
  transfers between devices with their start and end apart: 1, of which 1 were waited for; matrix products, arithmetic and copies ran while one was open for 0% of the time, Pallas kernels for 0%

commit v1 on v0

v1 whole, which is shorter than its diff:
```python
import functools

import jax
import jax.numpy as jnp
from jax import lax
from jax.experimental import pallas as pl
from jax.experimental.pallas import tpu as pltpu
from jax.sharding import PartitionSpec as P

F32 = jnp.float32
BF16 = jnp.bfloat16
VMEM_BYTES = 48 * 1024 * 1024
ANY = pl.BlockSpec(memory_space=pl.ANY)
VMEM = pl.BlockSpec(memory_space=pltpu.VMEM)
SMEM = pl.BlockSpec(memory_space=pltpu.SMEM)
TOKEN = jax.ShapeDtypeStruct((8, 128), F32)


def dot(a, b):
    return jnp.dot(a, b, preferred_element_type=F32)


def earlier_count(targets):
    length = targets.shape[0]
    row_iota = lax.broadcasted_iota(jnp.int32, (length, length), 0)
    col_iota = lax.broadcasted_iota(jnp.int32, (length, length), 1)
    earlier = (targets[:, None] == targets[None, :]) & (col_iota < row_iota)
    return jnp.sum(earlier.astype(jnp.int32), axis=1)


def ask_and_send(wavefunction, onsite_energy, left_env, right_env, source_device, source_block):
    owners = lax.axis_size("sector")
    sec_dev, block_size = wavefunction.shape[:2]
    left_count, channels = left_env.shape[:2]
    right_count = right_env.shape[0]
    hop_count = source_device.shape[1]
    local_count = channels - hop_count
    capacity = sec_dev * hop_count // owners
    targets = source_device.reshape(-1)
    slot_index = targets * capacity + earlier_count(targets)
    asked_for = jnp.zeros((owners * capacity,), jnp.int32).at[slot_index].set(source_block.reshape(-1))
    asked_for = lax.all_to_all(asked_for.reshape(owners, capacity), "sector", 0, 0, tiled=True)
    received = lax.all_to_all(wavefunction[asked_for], "sector", 0, 0, tiled=True)
    fetched = received.reshape(owners * capacity, block_size, block_size)[slot_index]
    fetched = fetched.reshape(left_count, right_count, hop_count, block_size, block_size)
    grid = wavefunction.reshape(left_count, right_count, 1, block_size, block_size)
    spread_out = jnp.broadcast_to(grid, (left_count, right_count, local_count, block_size, block_size))
    inputs_all = jnp.concatenate([spread_out, fetched], axis=2)
    middle = jnp.einsum("ijhab,jhbc->ijhac", inputs_all, right_env, preferred_element_type=F32).astype(BF16)
    summed = jnp.einsum("ihxa,ijhac->ijxc", left_env, middle, preferred_element_type=F32)
    psi_float = wavefunction.astype(F32)
    hpsi = summed.reshape(sec_dev, block_size, block_size) + onsite_energy[:, None, None] * psi_float
    numerator, denominator = lax.psum((jnp.sum(psi_float * hpsi), jnp.sum(psi_float * psi_float)), "sector")
    quotient = numerator / denominator
    residual = (hpsi - quotient * psi_float).astype(BF16)
    return hpsi.astype(BF16), residual, quotient.reshape(1)


def local_kernel(onsite, psi, right, left, acc, square, token, r_buf, l_buf, middle, sems):
    token[...] = jnp.zeros(token.shape, F32)
    rows, cols, size = psi.shape[0], psi.shape[1], psi.shape[2]
    chans = r_buf.shape[1]
    r_copy = [pltpu.make_async_copy(right.at[j, pl.ds(0, chans)], r_buf.at[j], sems.at[0, j]) for j in range(cols)]
    l_copy = [pltpu.make_async_copy(left.at[i, pl.ds(0, chans)], l_buf.at[i], sems.at[1, i]) for i in range(rows)]
    for copy in r_copy + l_copy:
        copy.start()
    for j in range(cols):
        r_copy[j].wait()
        column = psi[:, j].reshape(rows * size, size)
        for h in range(chans):
            product = dot(column, r_buf[j, h]).astype(BF16)
            for i in range(rows):
                middle[i, pl.ds(h * size, size), pl.ds(j * size, size)] = product[i * size : (i + 1) * size]
    total = jnp.zeros((size, size), F32)
    for i in range(rows):
        l_copy[i].wait()
        wide = jnp.concatenate([l_buf[i, h] for h in range(chans)], axis=1)
        summed = dot(wide, middle[i])
        for j in range(cols):
            block = psi[i, j].astype(F32)
            acc[i * cols + j] = summed[:, j * size : (j + 1) * size] + onsite[i * cols + j] * block
            total += block * block
    square[...] = total


def local_call(onsite, psi, right, left, hops):
    sec, size = psi.shape[:2]
    rows, chans = left.shape[0], left.shape[1] - hops
    cols = right.shape[0]
    return pl.pallas_call(
        local_kernel,
        out_shape=(jax.ShapeDtypeStruct((sec, size, size), F32), jax.ShapeDtypeStruct((size, size), F32), TOKEN),
        in_specs=[SMEM, VMEM, ANY, ANY],
        out_specs=(VMEM, VMEM, VMEM),
        scratch_shapes=[
            pltpu.VMEM((cols, chans, size, size), BF16),
            pltpu.VMEM((rows, chans, size, size), BF16),
            pltpu.VMEM((rows, chans * size, cols * size), BF16),
            pltpu.SemaphoreType.DMA((2, max(rows, cols))),
        ],
        compiler_params=pltpu.CompilerParams(vmem_limit_bytes=VMEM_BYTES),
        cost_estimate=pl.CostEstimate(
            flops=4 * sec * chans * size**3, bytes_accessed=4 * (rows + cols) * chans * size * size, transcendentals=0
        ),
        name="local_channels",
    )(onsite, psi.reshape(rows, cols, size, size), right, left)


def hop_kernel(plan, first, last, capacity, hops, *refs):
    refs = list(refs)
    take = lambda n: [refs.pop(0) for _ in range(n)]
    order, *terms = take(3)
    envs = take(4)
    acc_in = take(1 if first else 2)
    base, pieces = plan
    bufs = take(1 + max(p[0] for owner in pieces for p in owner))
    psis = take(2) if last else []
    square = take(1)[0] if last else None
    acc_out = take(2)
    sums = take(1)[0]
    psi, r_buf, l_buf, acc, psi_sem, env_sem, acc_sem = refs
    count = len(pieces)
    skip = envs[0].shape[1] - hops
    env_copies = []
    for e in range(2):
        for f, buf in enumerate((r_buf, l_buf)):
            src = envs[2 * e + f]
            src = src.at[:, pl.ds(skip, hops)]
            env_copies.append(pltpu.make_async_copy(src, buf.at[e], env_sem.at[2 * e + f]))
    psi_copies = []
    for s, owner in enumerate(pieces):
        for operand, rows, at in owner:
            sem = psi_sem.at[len(psi_copies)]
            psi_copies.append(pltpu.make_async_copy(bufs[operand], psi.at[s, pl.ds(at, rows)], sem))
    acc_copies = [pltpu.make_async_copy(ref, acc.at[e], acc_sem.at[e]) for e, ref in enumerate(acc_in)]
    for copy in psi_copies + env_copies[:2] + acc_copies[:1] + env_copies[2:] + acc_copies[1:]:
        copy.start()
    if first:
        acc[1] = jnp.zeros(acc.shape[1:], F32)
    outs = [pltpu.make_async_copy(acc.at[e], acc_out[e], acc_sem.at[e]) for e in range(2)]
    rcols = r_buf.shape[2]
    for e in range(2):
        if e == 0:
            for copy in psi_copies:
                copy.wait()
        for copy in env_copies[2 * e : 2 * e + 2]:
            copy.wait()
        if e < len(acc_copies):
            acc_copies[e].wait()

        def owner_step(s, carry, e=e):
            slot = order[base + s] * capacity
            words = [terms[e][slot + r] for r in range(capacity)]
            mids = []
            for w in words:
                rr = (w >> 16) & 255
                mids.append(dot(psi[s, w & 255], r_buf[e, rr // rcols, rr % rcols]).astype(BF16))
            parts = []
            for w, mid in zip(words, mids):
                ll = w >> 24
                parts.append(dot(l_buf[e, ll // rcols, ll % rcols], mid))
            for w, part in zip(words, parts):
                t = (w >> 8) & 255
                acc[e, t] = acc[e, t] + part
            return carry

        lax.fori_loop(0, count, owner_step, 0)
        outs[e].start()
    if last:
        total = jnp.zeros(acc.shape[2:], F32)
        for e in range(2):
            total = lax.fori_loop(
                0, acc.shape[1], lambda t, v, e=e: v + psis[e][t].astype(F32) * acc[e, t], total
            )
        lanes = lax.broadcasted_iota(jnp.int32, sums.shape, 1)
        sums[...] = jnp.where(lanes < sums.shape[1] // 2, jnp.sum(total), jnp.sum(square[...]))
    else:
        sums[...] = jnp.zeros(sums.shape, F32)
    for copy in outs:
        copy.wait()


def hop_call(name, order, terms, envs, accs, plan, bufs, last_args, owners, capacity, hops):
    sec, size = accs[0].shape[:2]
    first, last = len(accs) == 1, bool(last_args)
    count = len(plan[1])
    n_pieces = sum(len(owner) for owner in plan[1])
    rcols = hops
    acc_shape = jax.ShapeDtypeStruct((sec, size, size), F32)
    out_shape = (acc_shape, acc_shape)
    out_specs = (ANY, ANY)
    out_shape += (jax.ShapeDtypeStruct((owners, size), F32) if last else TOKEN,)
    out_specs += (VMEM,)
    n_front = 3 + len(envs)
    return pl.pallas_call(
        functools.partial(hop_kernel, plan, first, last, capacity, hops),
        out_shape=out_shape,
        in_specs=[SMEM] * 3 + [ANY] * (len(envs) + len(accs) + len(bufs)) + [VMEM] * len(last_args),
        out_specs=out_specs,
        scratch_shapes=[
            pltpu.VMEM((count, sec, size, size), BF16),
            pltpu.VMEM((2, envs[0].shape[0], rcols, size, size), BF16),
            pltpu.VMEM((2, envs[1].shape[0], rcols, size, size), BF16),
            pltpu.VMEM((2, sec, size, size), F32),
            pltpu.SemaphoreType.DMA((n_pieces,)),
            pltpu.SemaphoreType.DMA((4,)),
            pltpu.SemaphoreType.DMA((2,)),
        ],
        input_output_aliases={n_front + i: i for i in range(len(accs))},
        compiler_params=pltpu.CompilerParams(vmem_limit_bytes=VMEM_BYTES),
        cost_estimate=pl.CostEstimate(
            flops=8 * count * capacity * size**3, bytes_accessed=12 * 1024 * 1024, transcendentals=0
        ),
        name=name,
    )(order, *terms, *envs, *accs, *bufs, *last_args)


def finish_kernel(sums, psi, mine, theirs, applied, residual, quotient):
    lanes = lax.broadcasted_iota(jnp.int32, sums.shape, 1)
    half = sums.shape[1] // 2
    ratio = jnp.sum(jnp.where(lanes == 0, sums[...], 0.0)) / jnp.sum(jnp.where(lanes == half, sums[...], 0.0))
    hpsi = mine[...] + theirs[...]
    applied[...] = hpsi.astype(BF16)
    residual[...] = (hpsi - ratio * psi[...].astype(F32)).astype(BF16)
    quotient[0] = ratio


def finish_call(sums, psi, mine, theirs):
    sec, size = psi.shape[:2]
    step = sec // 4 if sec % 4 == 0 else sec
    block = pl.BlockSpec((step, size, size), lambda g: (g, 0, 0))
    return pl.pallas_call(
        finish_kernel,
        grid=(sec // step,),
        out_shape=(
            jax.ShapeDtypeStruct(psi.shape, BF16),
            jax.ShapeDtypeStruct(psi.shape, BF16),
            jax.ShapeDtypeStruct((1,), F32),
        ),
        in_specs=[pl.BlockSpec(sums.shape, lambda g: (0, 0)), block, block, block],
        out_specs=(block, block, SMEM),
        name="finish",
    )(sums, psi, mine, theirs)


def term_words(source_device, source_block, rows, cols, capacity):
    sec, hops = source_device.shape
    targets = source_device.reshape(-1)
    slots = targets * capacity + earlier_count(targets)
    index = jnp.arange(sec * hops, dtype=jnp.int32)
    t, k = index // hops, index % hops
    words = source_block.reshape(-1) | (t << 8) | (((t % cols) * hops + k) << 16) | (((t // cols) * hops + k) << 24)
    hit = slots[None, :] == index[:, None]
    return jnp.sum(jnp.where(hit, words[None, :], 0), axis=1)


def tie(value, *after):
    return lax.optimization_barrier((value,) + after)[0]


def spread_everywhere(wavefunction, onsite_energy, left_env, right_env, source_device, source_block):
    owners = lax.axis_size("sector")
    sec = wavefunction.shape[0]
    rows, cols = left_env.shape[0], right_env.shape[0]
    hops = source_device.shape[1]
    chans = left_env.shape[1] - hops
    capacity = sec * hops // owners

    def swap(value, mask):
        return lax.ppermute(value, "sector", [(i, i ^ mask) for i in range(owners)])

    core, x, y = 1, 2, 4
    far_masks = list(range(8, owners, 8))
    far = [swap(wavefunction, mask) for mask in far_masks]
    terms = term_words(source_device, source_block, rows, cols, capacity)
    terms_sib = swap(terms, core)
    psi_sib = swap(wavefunction, core)
    right_sib = swap(right_env, core)
    left_sib = swap(left_env, core)
    acc, square, token = local_call(onsite_energy, wavefunction, right_env, left_env, hops)
    accs = (acc,)
    envs = (right_env, left_env, right_sib, left_sib)
    blocks = list(zip([0] + far_masks, [wavefunction] + far))
    tokens = [token]
    out = None

    def run(group, last_args=(), ahead=None):
        nonlocal accs, out
        masks = jnp.array([mask for mask, _ in group], jnp.int32)
        order = lax.axis_index("sector") ^ masks
        if ahead is not None:
            order = tie(order, ahead)
        plan = (0, [[(s, sec, 0)] for s in range(len(group))])
        bufs = tuple(value for _, value in group)
        name = f"hops_{len(tokens)}"
        out = hop_call(name, order, (terms, terms_sib), envs, accs, plan, bufs, last_args, owners, capacity, hops)
        accs = out[:2]
        tokens.append(out[2])

    late = []
    tail = []
    arrived = []
    for g, (mask, block) in enumerate(blocks):
        final = g >= len(blocks) - 2
        if g == 1:
            block = tie(block, tokens[0])
        elif g > 1:
            block = tie(block, *arrived[g - 2], tokens[g - 2])
        from_x, from_y = swap(block, x), swap(block, y)
        relay = from_y if g % 2 == 0 else from_x
        if final:
            relay = tie(relay, tokens[len(blocks) - 2])
        diag = swap(relay, x if g % 2 == 0 else y)
        arrived.append((from_x, from_y))
        near = [(mask, block), (mask ^ x, from_x), (mask ^ y, from_y)]
        if final:
            late += near
            tail.append((mask ^ x ^ y, diag))
        else:
            run(near + [(mask ^ x ^ y, diag)], (), blocks[g + 2][1])
    run(late)
    run(tail, (wavefunction, psi_sib, square))
    sums = lax.all_to_all(out[2], "sector", 0, 0, tiled=True)
    theirs = swap(accs[1], core)
    return finish_call(sums, wavefunction, accs[0], theirs)


def local(wavefunction, onsite_energy, left_env, right_env, source_device, source_block):
    owners = lax.axis_size("sector")
    sec, hops = source_device.shape
    fits = owners >= 32 and owners & (owners - 1) == 0 and sec % 2 == 0 and sec < 128
    fits = fits and max(left_env.shape[0], right_env.shape[0]) * hops < 128
    plan = spread_everywhere if fits and 2 * (sec * hops // owners) >= sec else ask_and_send
    return plan(wavefunction, onsite_energy, left_env, right_env, source_device, source_block)


def solution(mesh):
    return jax.shard_map(
        local,
        mesh=mesh,
        in_specs=(
            P(("groups", "sector"), None, None),
            P(("groups", "sector")),
            P(("groups", "sector"), None, None, None),
            P(("groups", "sector"), None, None, None),
            P(("groups", "sector"), None),
            P(("groups", "sector"), None),
        ),
        out_specs=(
            P(("groups", "sector"), None, None),
            P(("groups", "sector"), None, None),
            P("groups"),
        ),
        check_vma=False,
    )
```

time: 294 us -> 138 us (0.47)
  waiting for transfers between devices: 186 us -> 42 us
  Pallas kernels: 0 us -> 38 us
  blocking collectives: 51.4 us -> 19.2 us
  starting transfers between devices: 3.67 us -> 23.4 us
  local copies, waits for them, and re-layouts: 30.6 us -> 13.7 us
  matrix products: 14 us -> 0 us
  other arithmetic: 3.31 us -> 0.32 us
    all_to_all x1 -> x0, waiting for transfers between devices: 186 us -> none  [local(): lax.all_to_all(wavefunction[lax.all_to_all(asked_for, 'sector', split_axi...]
    ppermute x0 -> x20, waiting for transfers between devices: none -> 42 us  [swap(): return lax.ppermute(value, 'sector', [(i, i ^ mask) for i in range(owners)])]
    pallas_call x0 -> x6, Pallas kernels: none -> 38 us  [the longest x4 28.3 us: hop_call(): pl.pallas_call(functools.partial(hop_kernel, plan, first, last, capacity,...]
    psum x1 -> x0, blocking collectives: 37.1 us -> none  [local(): lax.psum((jnp.sum(psi_float * hpsi), jnp.sum(psi_float * psi_float)), 'se...]
    ppermute x0 -> x20, starting transfers between devices: none -> 23.4 us  [swap(): return lax.ppermute(value, 'sector', [(i, i ^ mask) for i in range(owners)])]
    gather x2 -> x0, local copies, waits for them, and re-layouts: 21.7 us -> none  [the longest x1 12 us: local(): received.reshape(owners * capacity, block_size, block_size)[slot_index]]
    dot_general x1 -> x0, matrix products: 14 us -> none  [local(): jnp.einsum('ihxa,ijhac->ijxc', left_env, middle, preferred_element_type=j...]
    unnamed x4 -> x34, local copies, waits for them, and re-layouts: 0.01 us -> 12.1 us
  transfers between devices with their start and end apart: 1 -> 20, of which waited for: 1 -> 7; matrix products, arithmetic and copies ran while one was open for 0% -> 1% of each run, Pallas kernels for 0% -> 21%
where the time goes in v1:
time: 138 us; the launch traced here: 137 us
  waiting for transfers between devices  42 us (30%)
  Pallas kernels  38 us (28%)
  starting transfers between devices  23.4 us (17%)
  blocking collectives  19.2 us (14%)
  local copies, waits for them, and re-layouts  13.7 us (10%)
    ppermute x20, waiting for transfers between devices, swap(): return lax.ppermute(value, 'sector', [(i, i ^ mask) for i in range(owners)])  42 us
    pallas_call x4, Pallas kernels, hop_call(): pl.pallas_call(functools.partial(hop_kernel, plan, first, last, capacity,...  28.3 us
    ppermute x20, starting transfers between devices, swap(): return lax.ppermute(value, 'sector', [(i, i ^ mask) for i in range(owners)])  23.4 us
    all_to_all x1, blocking collectives, spread_everywhere(): sums = lax.all_to_all(out[2], 'sector', 0, 0, tiled=True)  19.2 us
    unnamed x34, local copies, waits for them, and re-layouts  12.1 us
    pallas_call x1, Pallas kernels, local_call(): pl.pallas_call(local_kernel, out_shape=(jax.ShapeDtypeStruct((sec, size,...  5.83 us
    pallas_call x1, Pallas kernels, finish_call(): pl.pallas_call(finish_kernel, grid=(sec // step,), out_shape=(jax.ShapeDt...  3.94 us
  transfers between devices with their start and end apart: 20, of which 7 were waited for; matrix products, arithmetic and copies ran while one was open for 1% of the time, Pallas kernels for 21%

profile of v1, /device:TPU:0, one launch (start us, length us, event | category | flops | bytes accessed | tf_op | source)
XLA Modules:
  0.0 137.4 jit_solution(10179016777816123276)
XLA Ops:
  0.6 0.5 collective-permute-start.1
  1.1 0.1 collective-permute-start.2
  1.2 4.0 %collective-permute-start.4 = (bf16[16,128,128]{2,1,0:T(8,128)(2,1)}, bf16[16,128,128]{2,1,0:T(8,128)(2,1)S(1)}, u32[]{:S(2)}, u32[]{:S(2)}) collective-permute-start(bf16[16,128,128]{2,1,0:T(8,128)(2,1)} %psi.1), channel_id=1, source_target_pairs={{0,16},{1,17},{2,18},{3,19},{4,20},{5,21},{6,22},{7,23},{8,24},{9,... | collective-permute-start | bytes 1572872 | tf_op jit(solution)/shard_map/ppermute | solution.py:270
  5.2 1.6 %collective-permute-start.8 = (bf16[16,128,128]{2,1,0:T(8,128)(2,1)}, bf16[16,128,128]{2,1,0:T(8,128)(2,1)S(1)}, u32[]{:S(2)}, u32[]{:S(2)}) collective-permute-start(bf16[16,128,128]{2,1,0:T(8,128)(2,1)} %psi.1), channel_id=1, source_target_pairs={{0,8},{1,9},{2,10},{3,11},{4,12},{5,13},{6,14},{7,15},{8,0},{9,1},... | collective-permute-start | bytes 1572872 | tf_op jit(solution)/shard_map/ppermute | solution.py:270
  6.8 0.8 reshape.87
  7.6 0.8 reshape.88
  8.4 0.2 convert_reduce_fusion
  8.6 0.1 select_reduce_fusion.refs_1_
  8.7 0.1 collective-permute-start
  8.8 5.2 %collective-permute-done.refs_2_ = s32[256]{0:T(256)S(1)} collective-permute-done((s32[256]{0:T(256)S(1)}, s32[256]{0:T(256)S(1)}, u32[]{:S(2)}, u32[]{:S(2)}) %collective-permute-start) | collective-permute-done | bytes 1056 | tf_op jit(solution)/shard_map/ppermute | solution.py:270
  13.9 2.9 %collective-permute-start.6 = (bf16[16,128,128]{2,1,0:T(8,128)(2,1)}, bf16[16,128,128]{2,1,0:T(8,128)(2,1)S(1)}, u32[]{:S(2)}, u32[]{:S(2)}) collective-permute-start(bf16[16,128,128]{2,1,0:T(8,128)(2,1)} %psi.1), channel_id=1, source_target_pairs={{0,4},{1,5},{2,6},{3,7},{4,0},{5,1},{6,2},{7,3},{8,12},{9,13},{10,... | collective-permute-start | bytes 1572872 | tf_op jit(solution)/shard_map/ppermute | solution.py:270
  16.8 2.2 %copy-done = bf16[4,32,128,128]{3,2,1,0:T(8,128)(2,1)S(1)} copy-done((bf16[4,32,128,128]{3,2,1,0:T(8,128)(2,1)S(1)}, bf16[4,32,128,128]{3,2,1,0:T(8,128)(2,1)}, u32[]{:S(2)}) %copy-start) | copy-done | bytes 4194328
  19.0 1.0 copy-done.2
  20.0 0.7 copy-done.12
  20.7 5.8 %local_channels.1 = (f32[16,128,128]{2,1,0:T(8,128)S(1)}, f32[128,128]{1,0:T(8,128)S(1)}, f32[8,128]{1,0:T(8,128)}) custom-call(f32[16]{0:T(128)S(1)} %copy-done.12, bf16[4,4,128,128]{3,2,1,0:T(8,128)(2,1)S(1)} %bitcast.5, bf16[4,32,128,128]{3,2,1,0:T(8,128)(2,1)S(1)} %copy-done, bf16[4,32,128,128]{3,2,1,0:T(8,128)(2,1)} %refs_4_.7), custom_call_target="tpu_custom_call" | custom-call | flops 2147483648 | bytes 8388608 | tf_op jit(solution)/shard_map/local_channels/pallas_call | solution.py:90
  26.5 2.6 %collective-permute-done.8.refs_9_ = bf16[16,128,128]{2,1,0:T(8,128)(2,1)S(1)} collective-permute-done((bf16[16,128,128]{2,1,0:T(8,128)(2,1)}, bf16[16,128,128]{2,1,0:T(8,128)(2,1)S(1)}, u32[]{:S(2)}, u32[]{:S(2)}) %collective-permute-start.8) | collective-permute-done | bytes 524320 | tf_op jit(solution)/shard_map/ppermute | solution.py:270
  29.2 0.5 collective-permute-start.3
  29.6 0.0 collective-permute-done.4.refs_9_
  29.6 1.5 %collective-permute-start.9 = (bf16[16,128,128]{2,1,0:T(8,128)(2,1)S(1)}, bf16[16,128,128]{2,1,0:T(8,128)(2,1)}, u32[]{:S(2)}, u32[]{:S(2)}) collective-permute-start(bf16[16,128,128]{2,1,0:T(8,128)(2,1)S(1)} %collective-permute-done.8.refs_9_), channel_id=1, source_target_pairs={{0,2},{1,3},{2,0},{3,1},{4,6},{5,7},{6,4},{7,5},{8,10},{9,11},{10,... | collective-permute-start | bytes 1572872 | tf_op jit(solution)/shard_map/ppermute | solution.py:270
  31.1 0.0 collective-permute-done.6.refs_10_
  31.1 1.5 %collective-permute-start.10 = (bf16[16,128,128]{2,1,0:T(8,128)(2,1)S(1)}, bf16[16,128,128]{2,1,0:T(8,128)(2,1)S(1)}, u32[]{:S(2)}, u32[]{:S(2)}) collective-permute-start(bf16[16,128,128]{2,1,0:T(8,128)(2,1)S(1)} %collective-permute-done.8.refs_9_), channel_id=1, source_target_pairs={{0,4},{1,5},{2,6},{3,7},{4,0},{5,1},{6,2},{7,3},{8,12},{9,13},{10,... | collective-permute-start | bytes 1572872 | tf_op jit(solution)/shard_map/ppermute | solution.py:270
  32.6 10.6 %collective-permute-done.3.refs_12_ = bf16[16,128,128]{2,1,0:T(8,128)(2,1)S(1)} collective-permute-done((bf16[16,128,128]{2,1,0:T(8,128)(2,1)S(1)}, bf16[16,128,128]{2,1,0:T(8,128)(2,1)S(1)}, u32[]{:S(2)}, u32[]{:S(2)}) %collective-permute-start.3) | collective-permute-done | bytes 524320 | tf_op jit(solution)/shard_map/ppermute | solution.py:270
  43.2 1.5 %collective-permute-start.5 = (bf16[16,128,128]{2,1,0:T(8,128)(2,1)S(1)}, bf16[16,128,128]{2,1,0:T(8,128)(2,1)S(1)}, u32[]{:S(2)}, u32[]{:S(2)}) collective-permute-start(bf16[16,128,128]{2,1,0:T(8,128)(2,1)S(1)} %copy-done.2), channel_id=1, source_target_pairs={{0,2},{1,3},{2,0},{3,1},{4,6},{5,7},{6,4},{7,5},{8,10},{9,11},{10,... | collective-permute-start | bytes 1572872 | tf_op jit(solution)/shard_map/ppermute | solution.py:270
  44.7 0.0 collective-permute-done.9.refs_10_
  44.7 0.5 collective-permute-start.7
  45.3 0.8 copy-done.4
  46.1 0.0 collective-permute-done.10.refs_11_
  46.1 0.8 copy-done.6
  46.9 1.5 %collective-permute-start.11 = (bf16[16,128,128]{2,1,0:T(8,128)(2,1)}, bf16[16,128,128]{2,1,0:T(8,128)(2,1)}, u32[]{:S(2)}, u32[]{:S(2)}) collective-permute-start(bf16[16,128,128]{2,1,0:T(8,128)(2,1)} %collective-permute-done.9.refs_10_), channel_id=1, source_target_pairs={{0,4},{1,5},{2,6},{3,7},{4,0},{5,1},{6,2},{7,3},{8,12},{9,13},{10,... | collective-permute-start | bytes 1572872 | tf_op jit(solution)/shard_map/ppermute | solution.py:270
  48.4 9.7 %collective-permute-done.5.refs_9_ = bf16[16,128,128]{2,1,0:T(8,128)(2,1)S(1)} collective-permute-done((bf16[16,128,128]{2,1,0:T(8,128)(2,1)S(1)}, bf16[16,128,128]{2,1,0:T(8,128)(2,1)S(1)}, u32[]{:S(2)}, u32[]{:S(2)}) %collective-permute-start.5) | collective-permute-done | bytes 524320 | tf_op jit(solution)/shard_map/ppermute | solution.py:270
  58.1 0.8 copy-done.8
  58.9 1.5 %collective-permute-start.14 = (bf16[16,128,128]{2,1,0:T(8,128)(2,1)S(1)}, bf16[16,128,128]{2,1,0:T(8,128)(2,1)}, u32[]{:S(2)}, u32[]{:S(2)}) collective-permute-start(bf16[16,128,128]{2,1,0:T(8,128)(2,1)S(1)} %collective-permute-done.3.refs_12_), channel_id=1, source_target_pairs={{0,2},{1,3},{2,0},{3,1},{4,6},{5,7},{6,4},{7,5},{8,10},{9,11},{10,... | collective-permute-start | bytes 1572872 | tf_op jit(solution)/shard_map/ppermute | solution.py:270
  60.4 9.0 %collective-permute-done.7.refs_11_ = bf16[16,128,128]{2,1,0:T(8,128)(2,1)S(1)} collective-permute-done((bf16[16,128,128]{2,1,0:T(8,128)(2,1)S(1)}, bf16[16,128,128]{2,1,0:T(8,128)(2,1)S(1)}, u32[]{:S(2)}, u32[]{:S(2)}) %collective-permute-start.7) | collective-permute-done | bytes 524320 | tf_op jit(solution)/shard_map/ppermute | solution.py:270
  69.3 0.8 copy-done.10
  70.1 1.5 %collective-permute-start.13 = (bf16[16,128,128]{2,1,0:T(8,128)(2,1)S(1)}, bf16[16,128,128]{2,1,0:T(8,128)(2,1)}, u32[]{:S(2)}, u32[]{:S(2)}) collective-permute-start(bf16[16,128,128]{2,1,0:T(8,128)(2,1)S(1)} %collective-permute-done.4.refs_9_), channel_id=1, source_target_pairs={{0,4},{1,5},{2,6},{3,7},{4,0},{5,1},{6,2},{7,3},{8,12},{9,13},{10,... | collective-permute-start | bytes 1572872 | tf_op jit(solution)/shard_map/ppermute | solution.py:270
  71.6 0.0 collective-permute-done.1.refs_5_
  71.7 1.6 %collective-permute-start.12 = (bf16[16,128,128]{2,1,0:T(8,128)(2,1)S(1)}, bf16[16,128,128]{2,1,0:T(8,128)(2,1)S(1)}, u32[]{:S(2)}, u32[]{:S(2)}) collective-permute-start(bf16[16,128,128]{2,1,0:T(8,128)(2,1)S(1)} %collective-permute-done.4.refs_9_), channel_id=1, source_target_pairs={{0,2},{1,3},{2,0},{3,1},{4,6},{5,7},{6,4},{7,5},{8,10},{9,11},{10,... | collective-permute-start | bytes 1572872 | tf_op jit(solution)/shard_map/ppermute | solution.py:270
  73.2 0.0 collective-permute-done.2.refs_6_
  73.2 0.5 collective-permute-start.15
  73.7 1.0 copy-done.5
  74.8 1.0 copy-done.9
  75.8 1.0 copy-done.11
  76.9 6.9 %hops_1.1 = (f32[16,128,128]{2,1,0:T(8,128)S(1)}, f32[16,128,128]{2,1,0:T(8,128)S(1)}, f32[8,128]{1,0:T(8,128)}) custom-call(s32[4]{0:T(128)S(1)} %multiply_xor_fusion.refs_0_, s32[256]{0:T(256)S(1)} %select_reduce_fusion.refs_1_, s32[256]{0:T(256)S(1)} %collective-permute-done.refs_2_, ...), custom_call_target="tpu_custom_call", output_to_operand_aliasing={{0}: (7, {})} | custom-call | flops 536870912 | bytes 12582912 | tf_op jit(solution)/shard_map/hops_1/pallas_call | solution.py:195
  83.7 0.0 collective-permute-done.11.refs_12_
  83.7 0.1 collective-permute-start.18
  83.8 0.0 copy-start.15
  83.8 0.0 copy-start.14
  83.8 7.1 %hops_2.1 = (f32[16,128,128]{2,1,0:T(8,128)S(1)}, f32[16,128,128]{2,1,0:T(8,128)S(1)}, f32[8,128]{1,0:T(8,128)}) custom-call(s32[4]{0:T(128)S(1)} %broadcast_xor_fusion.refs_0_, s32[256]{0:T(256)S(1)} %select_reduce_fusion.refs_1_, s32[256]{0:T(256)S(1)} %collective-permute-done.refs_2_, ...), custom_call_target="tpu_custom_call", output_to_operand_aliasing={{0}: (7, {}), {1}: (8, {})} | custom-call | flops 536870912 | bytes 12582912 | tf_op jit(solution)/shard_map/hops_2/pallas_call | solution.py:195
  91.0 0.0 collective-permute-done.14.refs_13_
  91.0 1.6 %collective-permute-start.17 = (bf16[16,128,128]{2,1,0:T(8,128)(2,1)}, bf16[16,128,128]{2,1,0:T(8,128)(2,1)S(1)}, u32[]{:S(2)}, u32[]{:S(2)}) collective-permute-start(bf16[16,128,128]{2,1,0:T(8,128)(2,1)} %collective-permute-done.14.refs_13_), channel_id=1, source_target_pairs={{0,4},{1,5},{2,6},{3,7},{4,0},{5,1},{6,2},{7,3},{8,12},{9,13},{10,... | collective-permute-start | bytes 1572872 | tf_op jit(solution)/shard_map/ppermute | solution.py:270
  92.6 0.0 collective-permute-done.13.refs_11_
  92.6 0.5 collective-permute-start.16
  93.1 0.0 collective-permute-done.12.refs_10_
  93.1 0.0 collective-permute-done.15.refs_14_
  93.1 8.7 %hops_3.1 = (f32[16,128,128]{2,1,0:T(8,128)S(1)}, f32[16,128,128]{2,1,0:T(8,128)S(1)}, f32[8,128]{1,0:T(8,128)}) custom-call(s32[6]{0:T(128)S(1)} %broadcast_xor_fusion.1.refs_0_, s32[256]{0:T(256)S(1)} %select_reduce_fusion.refs_1_, s32[256]{0:T(256)S(1)} %collective-permute-done.refs_2_, ...), custom_call_target="tpu_custom_call", output_to_operand_aliasing={{0}: (7, {}), {1}: (8, {})} | custom-call | flops 805306368 | bytes 12582912 | tf_op jit(solution)/shard_map/hops_3/pallas_call | solution.py:195
  101.9 3.7 %collective-permute-done.17.refs_10_ = bf16[16,128,128]{2,1,0:T(8,128)(2,1)S(1)} collective-permute-done((bf16[16,128,128]{2,1,0:T(8,128)(2,1)}, bf16[16,128,128]{2,1,0:T(8,128)(2,1)S(1)}, u32[]{:S(2)}, u32[]{:S(2)}) %collective-permute-start.17) | collective-permute-done | bytes 524320 | tf_op jit(solution)/shard_map/ppermute | solution.py:270
  105.5 1.3 collective-permute-done.16.refs_9_
  106.8 5.6 %hops_4.1 = (f32[16,128,128]{2,1,0:T(8,128)S(1)}, f32[16,128,128]{2,1,0:T(8,128)S(1)}, f32[32,128]{1,0:T(8,128)S(1)}) custom-call(s32[2]{0:T(128)S(1)} %broadcast_xor_fusion.2.refs_0_, s32[256]{0:T(256)S(1)} %select_reduce_fusion.refs_1_, s32[256]{0:T(256)S(1)} %collective-permute-done.refs_2_, ...), custom_call_target="tpu_custom_call", output_to_operand_aliasing={{0}: (7, {}), {1}: (8, {})} | custom-call | flops 268435456 | bytes 12582912 | tf_op jit(solution)/shard_map/hops_4/pallas_call | solution.py:195
  112.4 1.0 copy-done.1
  113.4 0.0 collective-permute-start.19
  113.4 19.2 %all_to_all.11 = f32[32,1,128]{2,1,0:T(1,128)} all-to-all(f32[32,1,128]{2,1,0:T(1,128)S(1)} %bitcast.6), channel_id=1, replica_groups=mesh['groups'=1,'sector'=32] {'sector'}, dimensions={0} | all-to-all | bytes 32768 | tf_op jit(solution)/shard_map/all_to_all | solution.py:323
  132.5 0.0 collective-permute-done.19.theirs
  132.5 1.0 copy-done.13
  133.5 3.9 %finish.1 = (bf16[16,128,128]{2,1,0:T(8,128)(2,1)}, bf16[16,128,128]{2,1,0:T(8,128)(2,1)}, f32[1]{0:T(128)}) custom-call(f32[32,128]{1,0:T(8,128)} %bitcast.7, bf16[16,128,128]{2,1,0:T(8,128)(2,1)} %psi.1, f32[16,128,128]{2,1,0:T(8,128)} %copy-done.1, f32[16,128,128]{2,1,0:T(8,128)} %copy-done.13), custom_call_target="tpu_custom_call" | custom-call | tf_op jit(solution)/shard_map/finish/pallas_call | solution.py:232
  (26 shorter events, 0.1 us)
Async XLA Ops:
  0.6 71.0 %collective-permute-start.1 = (bf16[4,32,128,128]{3,2,1,0:T(8,128)(2,1)}, bf16[4,32,128,128]{3,2,1,0:T(8,128)(2,1)}, u32[]{:S(2)}, u32[]{:S(2)}) collective-permute-start(bf16[4,32,128,128]{3,2,1,0:T(8,128)(2,1)} %refs_3_.7), channel_id=1, source_target_pairs={{0,1},{1,0},{2,3},{3,2},{4,5},{5,4},{6,7},{7,6},{8,9},{9,8},{10,11... | collective-permute-start | bytes 12582920 | tf_op jit(solution)/shard_map/ppermute | solution.py:270
  1.1 72.1 %collective-permute-start.2 = (bf16[4,32,128,128]{3,2,1,0:T(8,128)(2,1)}, bf16[4,32,128,128]{3,2,1,0:T(8,128)(2,1)}, u32[]{:S(2)}, u32[]{:S(2)}) collective-permute-start(bf16[4,32,128,128]{3,2,1,0:T(8,128)(2,1)} %refs_4_.7), channel_id=1, source_target_pairs={{0,1},{1,0},{2,3},{3,2},{4,5},{5,4},{6,7},{7,6},{8,9},{9,8},{10,11... | collective-permute-start | bytes 12582920 | tf_op jit(solution)/shard_map/ppermute | solution.py:270
  1.2 28.4 %collective-permute-start.4 = (bf16[16,128,128]{2,1,0:T(8,128)(2,1)}, bf16[16,128,128]{2,1,0:T(8,128)(2,1)S(1)}, u32[]{:S(2)}, u32[]{:S(2)}) collective-permute-start(bf16[16,128,128]{2,1,0:T(8,128)(2,1)} %psi.1), channel_id=1, source_target_pairs={{0,16},{1,17},{2,18},{3,19},{4,20},{5,21},{6,22},{7,23},{8,24},{9,... | collective-permute-start | bytes 1572872 | tf_op jit(solution)/shard_map/ppermute | solution.py:270
  5.2 23.9 %collective-permute-start.8 = (bf16[16,128,128]{2,1,0:T(8,128)(2,1)}, bf16[16,128,128]{2,1,0:T(8,128)(2,1)S(1)}, u32[]{:S(2)}, u32[]{:S(2)}) collective-permute-start(bf16[16,128,128]{2,1,0:T(8,128)(2,1)} %psi.1), channel_id=1, source_target_pairs={{0,8},{1,9},{2,10},{3,11},{4,12},{5,13},{6,14},{7,15},{8,0},{9,1},... | collective-permute-start | bytes 1572872 | tf_op jit(solution)/shard_map/ppermute | solution.py:270
  8.7 5.2 %collective-permute-start = (s32[256]{0:T(256)S(1)}, s32[256]{0:T(256)S(1)}, u32[]{:S(2)}, u32[]{:S(2)}) collective-permute-start(s32[256]{0:T(256)S(1)} %select_reduce_fusion.refs_1_), channel_id=1, source_target_pairs={{0,1},{1,0},{2,3},{3,2},{4,5},{5,4},{6,7},{7,6},{8,9},{9,8},{10,11... | collective-permute-start | bytes 3080 | tf_op jit(solution)/shard_map/ppermute | solution.py:270
  13.9 17.2 %collective-permute-start.6 = (bf16[16,128,128]{2,1,0:T(8,128)(2,1)}, bf16[16,128,128]{2,1,0:T(8,128)(2,1)S(1)}, u32[]{:S(2)}, u32[]{:S(2)}) collective-permute-start(bf16[16,128,128]{2,1,0:T(8,128)(2,1)} %psi.1), channel_id=1, source_target_pairs={{0,4},{1,5},{2,6},{3,7},{4,0},{5,1},{6,2},{7,3},{8,12},{9,13},{10,... | collective-permute-start | bytes 1572872 | tf_op jit(solution)/shard_map/ppermute | solution.py:270
  16.8 2.2 %copy-start = (bf16[4,32,128,128]{3,2,1,0:T(8,128)(2,1)S(1)}, bf16[4,32,128,128]{3,2,1,0:T(8,128)(2,1)}, u32[]{:S(2)}) copy-start(bf16[4,32,128,128]{3,2,1,0:T(8,128)(2,1)} %refs_3_.7) | copy-start | bytes 12582916
  19.0 1.0 copy-start.2
  20.0 0.7 copy-start.12
  20.7 51.0 %copy-start.16 = (s32[4]{0:T(128)S(1)}, s32[4]{0:T(128)}, u32[]{:S(2)}) copy-start(s32[4]{0:T(128)} %constant.70.clone) | copy-start | bytes 52
  20.7 53.0 %copy-start.3 = (bf16[16,128,128]{2,1,0:T(8,128)(2,1)S(1)}, bf16[16,128,128]{2,1,0:T(8,128)(2,1)}, u32[]{:S(2)}) copy-start(bf16[16,128,128]{2,1,0:T(8,128)(2,1)} %psi.1) | copy-start | bytes 1572868
  29.2 14.1 %collective-permute-start.3 = (bf16[16,128,128]{2,1,0:T(8,128)(2,1)S(1)}, bf16[16,128,128]{2,1,0:T(8,128)(2,1)S(1)}, u32[]{:S(2)}, u32[]{:S(2)}) collective-permute-start(bf16[16,128,128]{2,1,0:T(8,128)(2,1)S(1)} %copy-done.2), channel_id=1, source_target_pairs={{0,24},{1,25},{2,26},{3,27},{4,28},{5,29},{6,30},{7,31},{8,16},{9,... | collective-permute-start | bytes 1572872 | tf_op jit(solution)/shard_map/ppermute | solution.py:270
  29.6 15.1 %collective-permute-start.9 = (bf16[16,128,128]{2,1,0:T(8,128)(2,1)S(1)}, bf16[16,128,128]{2,1,0:T(8,128)(2,1)}, u32[]{:S(2)}, u32[]{:S(2)}) collective-permute-start(bf16[16,128,128]{2,1,0:T(8,128)(2,1)S(1)} %collective-permute-done.8.refs_9_), channel_id=1, source_target_pairs={{0,2},{1,3},{2,0},{3,1},{4,6},{5,7},{6,4},{7,5},{8,10},{9,11},{10,... | collective-permute-start | bytes 1572872 | tf_op jit(solution)/shard_map/ppermute | solution.py:270
  31.1 15.0 %collective-permute-start.10 = (bf16[16,128,128]{2,1,0:T(8,128)(2,1)S(1)}, bf16[16,128,128]{2,1,0:T(8,128)(2,1)S(1)}, u32[]{:S(2)}, u32[]{:S(2)}) collective-permute-start(bf16[16,128,128]{2,1,0:T(8,128)(2,1)S(1)} %collective-permute-done.8.refs_9_), channel_id=1, source_target_pairs={{0,4},{1,5},{2,6},{3,7},{4,0},{5,1},{6,2},{7,3},{8,12},{9,13},{10,... | collective-permute-start | bytes 1572872 | tf_op jit(solution)/shard_map/ppermute | solution.py:270
  43.2 14.9 %collective-permute-start.5 = (bf16[16,128,128]{2,1,0:T(8,128)(2,1)S(1)}, bf16[16,128,128]{2,1,0:T(8,128)(2,1)S(1)}, u32[]{:S(2)}, u32[]{:S(2)}) collective-permute-start(bf16[16,128,128]{2,1,0:T(8,128)(2,1)S(1)} %copy-done.2), channel_id=1, source_target_pairs={{0,2},{1,3},{2,0},{3,1},{4,6},{5,7},{6,4},{7,5},{8,10},{9,11},{10,... | collective-permute-start | bytes 1572872 | tf_op jit(solution)/shard_map/ppermute | solution.py:270
  44.7 24.6 %collective-permute-start.7 = (bf16[16,128,128]{2,1,0:T(8,128)(2,1)S(1)}, bf16[16,128,128]{2,1,0:T(8,128)(2,1)S(1)}, u32[]{:S(2)}, u32[]{:S(2)}) collective-permute-start(bf16[16,128,128]{2,1,0:T(8,128)(2,1)S(1)} %collective-permute-done.6.refs_10_), channel_id=1, source_target_pairs={{0,2},{1,3},{2,0},{3,1},{4,6},{5,7},{6,4},{7,5},{8,10},{9,11},{10,... | collective-permute-start | bytes 1572872 | tf_op jit(solution)/shard_map/ppermute | solution.py:270
  45.3 0.8 copy-start.4
  46.1 0.8 copy-start.6
  46.9 36.8 %collective-permute-start.11 = (bf16[16,128,128]{2,1,0:T(8,128)(2,1)}, bf16[16,128,128]{2,1,0:T(8,128)(2,1)}, u32[]{:S(2)}, u32[]{:S(2)}) collective-permute-start(bf16[16,128,128]{2,1,0:T(8,128)(2,1)} %collective-permute-done.9.refs_10_), channel_id=1, source_target_pairs={{0,4},{1,5},{2,6},{3,7},{4,0},{5,1},{6,2},{7,3},{8,12},{9,13},{10,... | collective-permute-start | bytes 1572872 | tf_op jit(solution)/shard_map/ppermute | solution.py:270
  58.1 0.8 copy-start.8
  58.9 32.1 %collective-permute-start.14 = (bf16[16,128,128]{2,1,0:T(8,128)(2,1)S(1)}, bf16[16,128,128]{2,1,0:T(8,128)(2,1)}, u32[]{:S(2)}, u32[]{:S(2)}) collective-permute-start(bf16[16,128,128]{2,1,0:T(8,128)(2,1)S(1)} %collective-permute-done.3.refs_12_), channel_id=1, source_target_pairs={{0,2},{1,3},{2,0},{3,1},{4,6},{5,7},{6,4},{7,5},{8,10},{9,11},{10,... | collective-permute-start | bytes 1572872 | tf_op jit(solution)/shard_map/ppermute | solution.py:270
  69.3 0.8 copy-start.10
  70.1 22.4 %collective-permute-start.13 = (bf16[16,128,128]{2,1,0:T(8,128)(2,1)S(1)}, bf16[16,128,128]{2,1,0:T(8,128)(2,1)}, u32[]{:S(2)}, u32[]{:S(2)}) collective-permute-start(bf16[16,128,128]{2,1,0:T(8,128)(2,1)S(1)} %collective-permute-done.4.refs_9_), channel_id=1, source_target_pairs={{0,4},{1,5},{2,6},{3,7},{4,0},{5,1},{6,2},{7,3},{8,12},{9,13},{10,... | collective-permute-start | bytes 1572872 | tf_op jit(solution)/shard_map/ppermute | solution.py:270
  71.7 21.5 %collective-permute-start.12 = (bf16[16,128,128]{2,1,0:T(8,128)(2,1)S(1)}, bf16[16,128,128]{2,1,0:T(8,128)(2,1)S(1)}, u32[]{:S(2)}, u32[]{:S(2)}) collective-permute-start(bf16[16,128,128]{2,1,0:T(8,128)(2,1)S(1)} %collective-permute-done.4.refs_9_), channel_id=1, source_target_pairs={{0,2},{1,3},{2,0},{3,1},{4,6},{5,7},{6,4},{7,5},{8,10},{9,11},{10,... | collective-permute-start | bytes 1572872 | tf_op jit(solution)/shard_map/ppermute | solution.py:270
  73.2 19.9 %collective-permute-start.15 = (bf16[16,128,128]{2,1,0:T(8,128)(2,1)S(1)}, bf16[16,128,128]{2,1,0:T(8,128)(2,1)S(1)}, u32[]{:S(2)}, u32[]{:S(2)}) collective-permute-start(bf16[16,128,128]{2,1,0:T(8,128)(2,1)S(1)} %collective-permute-done.3.refs_12_), channel_id=1, source_target_pairs={{0,4},{1,5},{2,6},{3,7},{4,0},{5,1},{6,2},{7,3},{8,12},{9,13},{10,... | collective-permute-start | bytes 1572872 | tf_op jit(solution)/shard_map/ppermute | solution.py:270
  73.7 1.0 copy-start.5
  74.8 1.0 copy-start.9
  75.8 1.0 copy-start.11
  76.9 7.0 %copy-start.7 = (bf16[16,128,128]{2,1,0:T(8,128)(2,1)S(1)}, bf16[16,128,128]{2,1,0:T(8,128)(2,1)}, u32[]{:S(2)}) copy-start(bf16[16,128,128]{2,1,0:T(8,128)(2,1)} %copy-done.6) | copy-start | bytes 1572868
  83.7 18.1 %collective-permute-start.18 = (bf16[16,128,128]{2,1,0:T(8,128)(2,1)S(1)}, bf16[16,128,128]{2,1,0:T(8,128)(2,1)S(1)}, u32[]{:S(2)}, u32[]{:S(2)}) collective-permute-start(bf16[16,128,128]{2,1,0:T(8,128)(2,1)S(1)} %copy-done.3), channel_id=1, source_target_pairs={{0,1},{1,0},{2,3},{3,2},{4,5},{5,4},{6,7},{7,6},{8,9},{9,8},{10,11... | collective-permute-start | bytes 1572872 | tf_op jit(solution)/shard_map/ppermute | solution.py:270
  83.8 9.3 %copy-start.15 = (s32[6]{0:T(128)S(1)}, s32[6]{0:T(128)}, u32[]{:S(2)}) copy-start(s32[6]{0:T(128)} %constant.71.clone) | copy-start | bytes 76
  83.8 9.3 %copy-start.14 = (s32[2]{0:T(128)S(1)}, s32[2]{0:T(128)}, u32[]{:S(2)}) copy-start(s32[2]{0:T(128)} %constant.72.clone) | copy-start | bytes 28
  91.0 14.6 %collective-permute-start.17 = (bf16[16,128,128]{2,1,0:T(8,128)(2,1)}, bf16[16,128,128]{2,1,0:T(8,128)(2,1)S(1)}, u32[]{:S(2)}, u32[]{:S(2)}) collective-permute-start(bf16[16,128,128]{2,1,0:T(8,128)(2,1)} %collective-permute-done.14.refs_13_), channel_id=1, source_target_pairs={{0,4},{1,5},{2,6},{3,7},{4,0},{5,1},{6,2},{7,3},{8,12},{9,13},{10,... | collective-permute-start | bytes 1572872 | tf_op jit(solution)/shard_map/ppermute | solution.py:270
  92.6 14.2 %collective-permute-start.16 = (bf16[16,128,128]{2,1,0:T(8,128)(2,1)}, bf16[16,128,128]{2,1,0:T(8,128)(2,1)S(1)}, u32[]{:S(2)}, u32[]{:S(2)}) collective-permute-start(bf16[16,128,128]{2,1,0:T(8,128)(2,1)} %collective-permute-done.13.refs_11_), channel_id=1, source_target_pairs={{0,2},{1,3},{2,0},{3,1},{4,6},{5,7},{6,4},{7,5},{8,10},{9,11},{10,... | collective-permute-start | bytes 1572872 | tf_op jit(solution)/shard_map/ppermute | solution.py:270
  112.4 1.0 copy-start.1
  113.4 19.2 %collective-permute-start.19 = (f32[16,128,128]{2,1,0:T(8,128)S(1)}, f32[16,128,128]{2,1,0:T(8,128)S(1)}, u32[]{:S(2)}, u32[]{:S(2)}) collective-permute-start(f32[16,128,128]{2,1,0:T(8,128)S(1)} %get-tuple-element.42), channel_id=1, source_target_pairs={{0,1},{1,0},{2,3},{3,2},{4,5},{5,4},{6,7},{7,6},{8,9},{9,8},{10,11... | collective-permute-start | bytes 3145736 | tf_op jit(solution)/shard_map/ppermute | solution.py:270
  132.5 1.0 copy-start.13

commit v2 on v1

v2 whole, which is shorter than its diff:
```python
import functools

import jax
import jax.numpy as jnp
from jax import lax
from jax.experimental import pallas as pl
from jax.experimental.pallas import tpu as pltpu
from jax.sharding import PartitionSpec as P

F32 = jnp.float32
BF16 = jnp.bfloat16
VMEM_BYTES = 16 * 1024 * 1024
LOCAL_BYTES = 48 * 1024 * 1024
FIRST_BYTES = 24 * 1024 * 1024
COST = pl.CostEstimate(flops=1, bytes_accessed=1, transcendentals=0)
ANY = pl.BlockSpec(memory_space=pl.ANY)
VMEM = pl.BlockSpec(memory_space=pltpu.VMEM)
HBM = pl.BlockSpec(memory_space=pltpu.HBM)
SMEM = pl.BlockSpec(memory_space=pltpu.SMEM)
TOKEN = jax.ShapeDtypeStruct((8, 128), F32)


def dot(a, b):
    return jnp.dot(a, b, preferred_element_type=F32)


def earlier_count(targets):
    length = targets.shape[0]
    row_iota = lax.broadcasted_iota(jnp.int32, (length, length), 0)
    col_iota = lax.broadcasted_iota(jnp.int32, (length, length), 1)
    earlier = (targets[:, None] == targets[None, :]) & (col_iota < row_iota)
    return jnp.sum(earlier.astype(jnp.int32), axis=1)


def ask_and_send(wavefunction, onsite_energy, left_env, right_env, source_device, source_block):
    owners = lax.axis_size("sector")
    sec_dev, block_size = wavefunction.shape[:2]
    left_count, channels = left_env.shape[:2]
    right_count = right_env.shape[0]
    hop_count = source_device.shape[1]
    local_count = channels - hop_count
    capacity = sec_dev * hop_count // owners
    targets = source_device.reshape(-1)
    slot_index = targets * capacity + earlier_count(targets)
    asked_for = jnp.zeros((owners * capacity,), jnp.int32).at[slot_index].set(source_block.reshape(-1))
    asked_for = lax.all_to_all(asked_for.reshape(owners, capacity), "sector", 0, 0, tiled=True)
    received = lax.all_to_all(wavefunction[asked_for], "sector", 0, 0, tiled=True)
    fetched = received.reshape(owners * capacity, block_size, block_size)[slot_index]
    fetched = fetched.reshape(left_count, right_count, hop_count, block_size, block_size)
    grid = wavefunction.reshape(left_count, right_count, 1, block_size, block_size)
    spread_out = jnp.broadcast_to(grid, (left_count, right_count, local_count, block_size, block_size))
    inputs_all = jnp.concatenate([spread_out, fetched], axis=2)
    middle = jnp.einsum("ijhab,jhbc->ijhac", inputs_all, right_env, preferred_element_type=F32).astype(BF16)
    summed = jnp.einsum("ihxa,ijhac->ijxc", left_env, middle, preferred_element_type=F32)
    psi_float = wavefunction.astype(F32)
    hpsi = summed.reshape(sec_dev, block_size, block_size) + onsite_energy[:, None, None] * psi_float
    numerator, denominator = lax.psum((jnp.sum(psi_float * hpsi), jnp.sum(psi_float * psi_float)), "sector")
    quotient = numerator / denominator
    residual = (hpsi - quotient * psi_float).astype(BF16)
    return hpsi.astype(BF16), residual, quotient.reshape(1)


def local_kernel(onsite, psi, right, left, acc, square, hop_env, r_buf, l_buf, middle, sems):
    rows, cols, size = psi.shape[0], psi.shape[1], psi.shape[2]
    chans = r_buf.shape[1]
    r_copy = [pltpu.make_async_copy(right.at[j, pl.ds(0, chans)], r_buf.at[j], sems.at[0, j]) for j in range(cols)]
    l_copy = [pltpu.make_async_copy(left.at[i, pl.ds(0, chans)], l_buf.at[i], sems.at[1, i]) for i in range(rows)]
    hop_copy = []
    for n in range(cols + rows):
        env, row = (right, n) if n < cols else (left, n - cols)
        src = env.at[row, pl.ds(chans, hop_env.shape[1])]
        hop_copy.append(pltpu.make_async_copy(src, hop_env.at[n], sems.at[2 + n // cols, n % cols]))
    for copy in r_copy + l_copy + hop_copy:
        copy.start()
    for j in range(cols):
        r_copy[j].wait()
        column = psi[:, j].reshape(rows * size, size)
        for h in range(chans):
            product = dot(column, r_buf[j, h]).astype(BF16)
            for i in range(rows):
                middle[i, pl.ds(h * size, size), pl.ds(j * size, size)] = product[i * size : (i + 1) * size]
    total = jnp.zeros((size, size), F32)
    for i in range(rows):
        l_copy[i].wait()
        wide = jnp.concatenate([l_buf[i, h] for h in range(chans)], axis=1)
        summed = dot(wide, middle[i])
        for j in range(cols):
            block = psi[i, j].astype(F32)
            acc[i * cols + j] = summed[:, j * size : (j + 1) * size] + onsite[i * cols + j] * block
            total += block * block
    square[...] = total
    for copy in hop_copy:
        copy.wait()


def local_call(onsite, psi, right, left, hops):
    sec, size = psi.shape[:2]
    rows, cols, chans = left.shape[0], right.shape[0], left.shape[1] - hops
    return pl.pallas_call(
        local_kernel,
        out_shape=(
            jax.ShapeDtypeStruct((sec, size, size), F32),
            jax.ShapeDtypeStruct((size, size), F32),
            jax.ShapeDtypeStruct((cols + rows, hops, size, size), BF16),
        ),
        in_specs=[SMEM, VMEM, HBM, HBM],
        out_specs=[VMEM] * 3,
        scratch_shapes=[
            pltpu.VMEM((cols, chans, size, size), BF16),
            pltpu.VMEM((rows, chans, size, size), BF16),
            pltpu.VMEM((rows, chans * size, cols * size), BF16),
            pltpu.SemaphoreType.DMA((4, max(rows, cols))),
        ],
        compiler_params=pltpu.CompilerParams(vmem_limit_bytes=LOCAL_BYTES),
        cost_estimate=COST,
        name="local_channels",
    )(onsite, psi.reshape(rows, cols, size, size), right, left)


def hop_kernel(base, count, first, last, capacity, *refs):
    refs = list(refs)
    take = lambda n: [refs.pop(0) for _ in range(n)]
    order, *terms = take(3)
    envs = take(2) if first else take(1)
    acc_in = take(1 if first else 2)
    bufs = take(count)
    psis = take(2) if last else []
    square = take(1)[0] if last else None
    acc = take(2)
    sums = take(1)[0]
    env = take(1)[0] if first else envs[0]
    psi, sems, env_sems = refs
    hops, rows = env.shape[2], env.shape[1] // 2
    copies = [pltpu.make_async_copy(buf, psi.at[s], sems.at[s]) for s, buf in enumerate(bufs)]
    fills = []
    if first:
        for e in range(2):
            for f in range(2):
                half = pl.ds(f * rows, rows)
                fills.append(pltpu.make_async_copy(envs[e].at[half], env.at[e, half], env_sems.at[2 * e + f]))
    for copy in copies + fills:
        copy.start()
    for e in range(2):
        acc[e][...] = acc_in[e][...] if e < len(acc_in) else jnp.zeros(acc[e].shape, F32)
    for copy in copies:
        copy.wait()
    for e in range(2):
        for fill in fills[2 * e : 2 * e + 2]:
            fill.wait()

        def owner_step(s, carry, e=e):
            slot = order[base + s] * capacity
            words = [terms[e][slot + r] for r in range(capacity)]
            mids = []
            for w in words:
                right = (w >> 16) & 255
                mids.append(dot(psi[s, w & 255], env[e, right // hops, right % hops]).astype(BF16))
            parts = []
            for w, mid in zip(words, mids):
                left = w >> 24
                parts.append(dot(env[e, left // hops, left % hops], mid))
            for w, part in zip(words, parts):
                t = (w >> 8) & 255
                acc[e][t] = acc[e][t] + part
            return carry

        lax.fori_loop(0, count, owner_step, 0)
    if last:
        total = jnp.zeros(acc[0].shape[1:], F32)
        for e in range(2):
            total = lax.fori_loop(
                0, acc[e].shape[0], lambda t, v, e=e: v + psis[e][t].astype(F32) * acc[e][t], total
            )
        lanes = lax.broadcasted_iota(jnp.int32, sums.shape, 1)
        sums[...] = jnp.where(lanes < sums.shape[1] // 2, jnp.sum(total), jnp.sum(square[...]))
    else:
        sums[...] = jnp.zeros(sums.shape, F32)


def hop_call(name, order, base, terms, envs, accs, bufs, last_args, owners, capacity):
    sec, size = accs[0].shape[:2]
    first, last = len(accs) == 1, bool(last_args)
    count = len(bufs)
    acc_shape = jax.ShapeDtypeStruct((sec, size, size), F32)
    out_shape = [acc_shape, acc_shape, jax.ShapeDtypeStruct((owners, size), F32) if last else TOKEN]
    if first:
        out_shape.append(jax.ShapeDtypeStruct((2,) + envs[0].shape, BF16))
    return pl.pallas_call(
        functools.partial(hop_kernel, base, count, first, last, capacity),
        out_shape=out_shape,
        in_specs=[SMEM] * 3
        + [HBM if first else VMEM] * len(envs)
        + [VMEM] * len(accs)
        + [ANY] * count
        + [VMEM] * len(last_args),
        out_specs=[VMEM] * len(out_shape),
        scratch_shapes=[
            pltpu.VMEM((count, sec, size, size), BF16),
            pltpu.SemaphoreType.DMA((count,)),
            pltpu.SemaphoreType.DMA((4,)),
        ],
        compiler_params=pltpu.CompilerParams(vmem_limit_bytes=FIRST_BYTES if first else VMEM_BYTES),
        cost_estimate=COST,
        name=name,
    )(order, *terms, *envs, *accs, *bufs, *last_args)


def hold_until(values, tokens):
    count = len(values)
    return pl.pallas_call(
        lambda *refs: None,
        out_shape=[jax.ShapeDtypeStruct(value.shape, value.dtype) for value in values],
        in_specs=[ANY] * (count + len(tokens)),
        out_specs=[ANY] * count,
        input_output_aliases={n: n for n in range(count)},
        compiler_params=pltpu.CompilerParams(vmem_limit_bytes=VMEM_BYTES),
        cost_estimate=COST,
        name="hold",
    )(*values, *tokens)


def finish_kernel(sums, psi, mine, theirs, applied, residual, quotient):
    lanes = lax.broadcasted_iota(jnp.int32, sums.shape, 1)
    half = sums.shape[1] // 2
    ratio = jnp.sum(jnp.where(lanes == 0, sums[...], 0.0)) / jnp.sum(jnp.where(lanes == half, sums[...], 0.0))
    quotient[0] = ratio
    for t in range(psi.shape[0]):
        hpsi = mine[t] + theirs[t]
        applied[t] = hpsi.astype(BF16)
        residual[t] = (hpsi - ratio * psi[t].astype(F32)).astype(BF16)


def finish_call(sums, psi, mine, theirs):
    shape = jax.ShapeDtypeStruct(psi.shape, BF16)
    return pl.pallas_call(
        finish_kernel,
        out_shape=(shape, shape, jax.ShapeDtypeStruct((1,), F32)),
        in_specs=[VMEM] * 4,
        out_specs=(VMEM, VMEM, SMEM),
        compiler_params=pltpu.CompilerParams(vmem_limit_bytes=VMEM_BYTES),
        name="finish",
    )(sums, psi, mine, theirs)


def term_words(source_device, source_block, cols, capacity):
    sec, hops = source_device.shape
    targets = source_device.reshape(-1)
    slots = targets * capacity + earlier_count(targets)
    index = jnp.arange(sec * hops, dtype=jnp.int32)
    t, k = index // hops, index % hops
    right, left = (t % cols) * hops + k, (cols + t // cols) * hops + k
    words = source_block.reshape(-1) | (t << 8) | (right << 16) | (left << 24)
    hit = slots[None, :] == index[:, None]
    return jnp.sum(jnp.where(hit, words[None, :], 0), axis=1)


def spread_everywhere(wavefunction, onsite_energy, left_env, right_env, source_device, source_block):
    owners = lax.axis_size("sector")
    sec = wavefunction.shape[0]
    hops = source_device.shape[1]
    capacity = sec * hops // owners
    core, x, y, z = 1, 2, 4, 8
    xy = x ^ y
    layers = owners // z

    def swap(value, mask):
        return lax.ppermute(value, "sector", [(i, i ^ mask) for i in range(owners)])

    def swap_middle(value):
        pairs = []
        for i in range(owners):
            layer = i // z
            to = layers - 1 - layer if layer in (1, 2) else layer
            pairs.append((i, to * z + i % z))
        return lax.ppermute(value, "sector", pairs)

    me = lax.axis_index("sector")
    outer = (me < z) | (me >= owners - z)
    layer_masks = [0, z, jnp.where(outer, 2 * z, 3 * z), jnp.where(outer, 3 * z, 2 * z)]
    groups = [
        [(0, 0), (0, x), (0, y), (1, 0)],
        [(1, x), (1, y)],
        [(0, xy), (1, xy), (2, 0)],
        [(2, x), (2, y), (3, 0)],
        [(3, x), (3, y)],
        [(2, xy), (3, xy)],
    ]
    order = jnp.stack([me ^ layer_masks[b] ^ bits for group in groups for b, bits in group])

    held = {(0, 0): wavefunction}
    state = {"base": 0}

    def hold(keys, *tokens):
        held.update(zip(keys, hold_until([held[key] for key in keys], tokens)))

    def run(group, last_args=()):
        first = len(state["accs"]) == 1
        out = hop_call(
            f"hops_{group}", order, state["base"], terms, state["envs"], state["accs"],
            tuple(held[key] for key in groups[group]), last_args, owners, capacity,
        )
        state["accs"] = out[:2]
        state["base"] += len(groups[group])
        if first:
            state["envs"] = out[3:]
        return out[2]

    held[1, 0] = swap(wavefunction, z)
    held["middle"] = swap_middle(wavefunction)
    held[0, x], held[0, y] = swap(wavefunction, x), swap(wavefunction, y)
    terms = term_words(source_device, source_block, right_env.shape[0], capacity)
    terms = (terms, swap(terms, core))
    acc, square, held["env"] = local_call(onsite_energy, wavefunction, right_env, left_env, hops)
    hold([(1, 0), "middle", (0, x), (0, y), "env"], terms[1])

    for link in (x, y):
        held[1, link] = swap(held[1, 0], link)
    held["outer"] = swap(held["middle"], z)
    held["middle_2"] = swap_middle(held[1, 0])
    env_sib = swap(held["env"], core)
    hold([(0, y)], env_sib)
    state["accs"], state["envs"] = (acc,), (held["env"], env_sib)

    held[0, xy] = swap(held[0, y], x)
    done = run(0)
    hold([(1, x), (1, y), "outer", "middle_2"], done)
    held[1, xy] = swap(held[1, x], y)
    held["outer_2"] = swap(held["middle_2"], z)
    held[2, 0] = jnp.where(outer, held["outer"], held["middle"])
    for link in (x, y):
        held[2, link] = swap(held[2, 0], link)
    done = run(1)
    hold([(0, xy), (1, xy), "outer_2"], done)
    held[3, 0] = jnp.where(outer, held["outer_2"], held["middle_2"])
    for link in (x, y):
        held[3, link] = swap(held[3, 0], link)
    done = run(2)
    hold([(2, x), (2, y)], done)
    held[2, xy] = swap(held[2, y], x)
    done = run(3)
    hold([(3, x)], done)
    held[3, xy] = swap(held[3, x], y)
    run(4)
    psi_sib = swap(wavefunction, core)
    sums = run(5, (wavefunction, psi_sib, square))
    sums = lax.all_to_all(sums, "sector", 0, 0, tiled=True)
    mine, theirs = state["accs"]
    return finish_call(sums, wavefunction, mine, swap(theirs, core))


def local(wavefunction, onsite_energy, left_env, right_env, source_device, source_block):
    owners = lax.axis_size("sector")
    sec, hops = source_device.shape
    fits = owners == 32 and sec <= 256 and (left_env.shape[0] + right_env.shape[0]) * hops <= 128
    plan = spread_everywhere if fits and 2 * (sec * hops // owners) >= sec else ask_and_send
    return plan(wavefunction, onsite_energy, left_env, right_env, source_device, source_block)


def solution(mesh):
    return jax.shard_map(
        local,
        mesh=mesh,
        in_specs=(
            P(("groups", "sector"), None, None),
            P(("groups", "sector")),
            P(("groups", "sector"), None, None, None),
            P(("groups", "sector"), None, None, None),
            P(("groups", "sector"), None),
            P(("groups", "sector"), None),
        ),
        out_specs=(
            P(("groups", "sector"), None, None),
            P(("groups", "sector"), None, None),
            P("groups"),
        ),
        check_vma=False,
    )
```

time: 138 us -> 107 us (0.78)
  waiting for transfers between devices: 42 us -> 31 us
  blocking collectives: 19.2 us -> 11.3 us
  local copies, waits for them, and re-layouts: 13.7 us -> 6 us
  Pallas kernels: 38 us -> 31.2 us
  starting transfers between devices: 23.4 us -> 25.7 us
    ppermute x20 -> x19, waiting for transfers between devices: 42 us -> 30.9 us  [swap(): return lax.ppermute(value, 'sector', [(i, i ^ mask) for i in range(owners)])]
    pallas_call x5 -> x13, Pallas kernels: 32.2 us -> 22.8 us  [the longest x6 21.5 us: hop_call(): pl.pallas_call(functools.partial(hop_kernel, base, count, first, last, ca...]
    all_to_all x1, blocking collectives: 19.2 us -> 11.3 us  [spread_everywhere(): sums = lax.all_to_all(sums, 'sector', 0, 0, tiled=True)]
    unnamed x34 -> x18, local copies, waits for them, and re-layouts: 12.1 us -> 4.36 us
    ppermute x0 -> x2, starting transfers between devices: none -> 3.38 us  [swap_middle(): return lax.ppermute(value, 'sector', pairs)]
    pallas_call x1, Pallas kernels: 5.83 us -> 8.33 us  [local_call(): pl.pallas_call(local_kernel, out_shape=(jax.ShapeDtypeStruct((sec, size,...]
    ppermute x20 -> x19, starting transfers between devices: 23.4 us -> 22.3 us  [swap(): return lax.ppermute(value, 'sector', [(i, i ^ mask) for i in range(owners)])]
  transfers between devices with their start and end apart: 20 -> 21, of which waited for: 7 -> 8; matrix products, arithmetic and copies ran while one was open for 1% -> 2% of each run, Pallas kernels for 21% -> 25%
where the time goes in v2:
time: 107 us; the launch traced here: 106 us
  Pallas kernels  31.2 us (29%)
  waiting for transfers between devices  31 us (29%)
  starting transfers between devices  25.7 us (24%)
  blocking collectives  11.3 us (11%)
  local copies, waits for them, and re-layouts  6 us (6%)
    ppermute x19, waiting for transfers between devices, swap(): return lax.ppermute(value, 'sector', [(i, i ^ mask) for i in range(owners)])  30.9 us
    ppermute x19, starting transfers between devices, swap(): return lax.ppermute(value, 'sector', [(i, i ^ mask) for i in range(owners)])  22.3 us
    pallas_call x6, Pallas kernels, hop_call(): pl.pallas_call(functools.partial(hop_kernel, base, count, first, last, ca...  21.5 us
    all_to_all x1, blocking collectives, spread_everywhere(): sums = lax.all_to_all(sums, 'sector', 0, 0, tiled=True)  11.3 us
    pallas_call x1, Pallas kernels, local_call(): pl.pallas_call(local_kernel, out_shape=(jax.ShapeDtypeStruct((sec, size,...  8.33 us
    unnamed x18, local copies, waits for them, and re-layouts  4.36 us
    ppermute x2, starting transfers between devices, swap_middle(): return lax.ppermute(value, 'sector', pairs)  3.38 us
  transfers between devices with their start and end apart: 21, of which 8 were waited for; matrix products, arithmetic and copies ran while one was open for 2% of the time, Pallas kernels for 25%

profile of v2, /device:TPU:0, one launch (start us, length us, event | category | flops | bytes accessed | tf_op | source)
XLA Modules:
  0.0 106.4 jit_solution(10019353319247153054)
XLA Ops:
  0.6 3.1 %collective-permute-start.1 = (bf16[16,128,128]{2,1,0:T(8,128)(2,1)}, bf16[16,128,128]{2,1,0:T(8,128)(2,1)}, u32[]{:S(2)}, u32[]{:S(2)}) collective-permute-start(bf16[16,128,128]{2,1,0:T(8,128)(2,1)} %psi.1), channel_id=1, source_target_pairs={{0,8},{1,9},{2,10},{3,11},{4,12},{5,13},{6,14},{7,15},{8,0},{9,1},... | collective-permute-start | bytes 1572872 | tf_op jit(solution)/shard_map/ppermute | solution.py:267
  3.7 1.7 %collective-permute-start.2 = (bf16[16,128,128]{2,1,0:T(8,128)(2,1)}, bf16[16,128,128]{2,1,0:T(8,128)(2,1)S(1)}, u32[]{:S(2)}, u32[]{:S(2)}) collective-permute-start(bf16[16,128,128]{2,1,0:T(8,128)(2,1)} %psi.1), channel_id=1, source_target_pairs={{0,0},{1,1},{2,2},{3,3},{4,4},{5,5},{6,6},{7,7},{8,16},{9,17},{10,... | collective-permute-start | bytes 1572872 | tf_op jit(solution)/shard_map/ppermute | solution.py:275
  5.4 1.5 %collective-permute-start.3 = (bf16[16,128,128]{2,1,0:T(8,128)(2,1)}, bf16[16,128,128]{2,1,0:T(8,128)(2,1)S(1)}, u32[]{:S(2)}, u32[]{:S(2)}) collective-permute-start(bf16[16,128,128]{2,1,0:T(8,128)(2,1)} %psi.1), channel_id=1, source_target_pairs={{0,2},{1,3},{2,0},{3,1},{4,6},{5,7},{6,4},{7,5},{8,10},{9,11},{10,... | collective-permute-start | bytes 1572872 | tf_op jit(solution)/shard_map/ppermute | solution.py:267
  6.9 1.5 %collective-permute-start.4 = (bf16[16,128,128]{2,1,0:T(8,128)(2,1)}, bf16[16,128,128]{2,1,0:T(8,128)(2,1)S(1)}, u32[]{:S(2)}, u32[]{:S(2)}) collective-permute-start(bf16[16,128,128]{2,1,0:T(8,128)(2,1)} %psi.1), channel_id=1, source_target_pairs={{0,4},{1,5},{2,6},{3,7},{4,0},{5,1},{6,2},{7,3},{8,12},{9,13},{10,... | collective-permute-start | bytes 1572872 | tf_op jit(solution)/shard_map/ppermute | solution.py:267
  8.4 0.8 reshape.88
  9.2 0.8 reshape.89
  10.0 0.2 convert_reduce_fusion
  10.2 0.1 select_reduce_fusion.refs_1_
  10.3 0.1 collective-permute-start
  10.4 0.0 copy-start
  10.4 1.0 copy-done
  11.4 0.7 copy-done.8
  12.1 8.3 %local_channels.1 = (f32[16,128,128]{2,1,0:T(8,128)S(1)}, f32[128,128]{1,0:T(8,128)S(1)}, bf16[8,16,128,128]{3,2,1,0:T(8,128)(2,1)}) custom-call(f32[16]{0:T(128)S(1)} %copy-done.8, bf16[4,4,128,128]{3,2,1,0:T(8,128)(2,1)S(1)} %bitcast.21, bf16[4,32,128,128]{3,2,1,0:T(8,128)(2,1)} %right.1, bf16[4,32,128,128]{3,2,1,0:T(8,128)(2,1)} %left.1), custom_call_target="tpu_custom_call" | custom-call | flops 1 | bytes 1 | tf_op jit(solution)/shard_map/local_channels/pallas_call | solution.py:99
  20.4 0.0 collective-permute-done.refs_5_.refs_2_
  20.4 0.0 collective-permute-done.1.refs_0_
  20.4 0.0 collective-permute-done.2.refs_1_
  20.5 0.0 collective-permute-done.3.refs_2_
  20.5 0.0 collective-permute-done.4.refs_3_
  20.5 0.0 copy-start.2
  20.5 0.9 copy-done.2
  21.4 0.8 copy-done.4
  22.2 0.5 collective-permute-start.5
  22.7 0.5 collective-permute-start.6
  23.2 0.7 collective-permute-start.7
  23.9 1.7 %collective-permute-start.9 = (bf16[16,128,128]{2,1,0:T(8,128)(2,1)}, bf16[16,128,128]{2,1,0:T(8,128)(2,1)S(1)}, u32[]{:S(2)}, u32[]{:S(2)}) collective-permute-start(bf16[16,128,128]{2,1,0:T(8,128)(2,1)} %get-tuple-element.43.refs_9_), channel_id=1, source_target_pairs={{0,0},{1,1},{2,2},{3,3},{4,4},{5,5},{6,6},{7,7},{8,16},{9,17},{10,... | collective-permute-start | bytes 1572872 | tf_op jit(solution)/shard_map/ppermute | solution.py:275
  25.6 3.7 %collective-permute-start.8 = (bf16[16,128,128]{2,1,0:T(8,128)(2,1)}, bf16[16,128,128]{2,1,0:T(8,128)(2,1)S(1)}, u32[]{:S(2)}, u32[]{:S(2)}) collective-permute-start(bf16[16,128,128]{2,1,0:T(8,128)(2,1)} %copy-done.4), channel_id=1, source_target_pairs={{0,8},{1,9},{2,10},{3,11},{4,12},{5,13},{6,14},{7,15},{8,0},{9,1},... | collective-permute-start | bytes 1572872 | tf_op jit(solution)/shard_map/ppermute | solution.py:267
  29.3 0.1 stack.67.refs_0_
  29.4 0.0 copy-start.3
  29.4 0.4 collective-permute-done.5.refs_1_.refs_4_
  29.8 0.6 copy-done.3
  30.4 0.3 copy-done.7
  30.8 6.7 %hops_0.1 = (f32[16,128,128]{2,1,0:T(8,128)S(1)}, f32[16,128,128]{2,1,0:T(8,128)S(1)}, f32[8,128]{1,0:T(8,128)S(1)}, bf16[2,8,16,128,128]{4,3,2,1,0:T(8,128)(2,1)S(1)}) custom-call(s32[16]{0:T(128)S(1)} %stack.67.refs_0_, s32[256]{0:T(256)S(1)} %select_reduce_fusion.refs_1_, s32[256]{0:T(256)S(1)} %collective-permute-done.refs_5_.refs_2_, ...), custom_call_target="tpu_custom_call" | custom-call | flops 1 | bytes 1 | tf_op jit(solution)/shard_map/hops_0/pallas_call | solution.py:188
  37.5 0.0 collective-permute-done.6.refs_0_
  37.5 0.0 collective-permute-done.7.refs_1_
  37.5 0.0 collective-permute-done.9.refs_3_
  37.6 3.7 %collective-permute-done.8.refs_2_ = bf16[16,128,128]{2,1,0:T(8,128)(2,1)S(1)} collective-permute-done((bf16[16,128,128]{2,1,0:T(8,128)(2,1)}, bf16[16,128,128]{2,1,0:T(8,128)(2,1)S(1)}, u32[]{:S(2)}, u32[]{:S(2)}) %collective-permute-start.8) | collective-permute-done | bytes 524320 | tf_op jit(solution)/shard_map/ppermute | solution.py:267
  41.3 1.2 %collective-permute-start.11 = (bf16[16,128,128]{2,1,0:T(8,128)(2,1)S(1)}, bf16[16,128,128]{2,1,0:T(8,128)(2,1)S(1)}, u32[]{:S(2)}, u32[]{:S(2)}) collective-permute-start(bf16[16,128,128]{2,1,0:T(8,128)(2,1)S(1)} %get-tuple-element.49.refs_6_), channel_id=1, source_target_pairs={{0,4},{1,5},{2,6},{3,7},{4,0},{5,1},{6,2},{7,3},{8,12},{9,13},{10,... | collective-permute-start | bytes 1572872 | tf_op jit(solution)/shard_map/ppermute | solution.py:267
  42.4 1.7 %collective-permute-start.12 = (bf16[16,128,128]{2,1,0:T(8,128)(2,1)S(1)}, bf16[16,128,128]{2,1,0:T(8,128)(2,1)S(1)}, u32[]{:S(2)}, u32[]{:S(2)}) collective-permute-start(bf16[16,128,128]{2,1,0:T(8,128)(2,1)S(1)} %get-tuple-element.53), channel_id=1, source_target_pairs={{0,8},{1,9},{2,10},{3,11},{4,12},{5,13},{6,14},{7,15},{8,0},{9,1},... | collective-permute-start | bytes 1572872 | tf_op jit(solution)/shard_map/ppermute | solution.py:267
  44.2 1.5 %collective-permute-start.10 = (bf16[16,128,128]{2,1,0:T(8,128)(2,1)S(1)}, bf16[16,128,128]{2,1,0:T(8,128)(2,1)S(1)}, u32[]{:S(2)}, u32[]{:S(2)}) collective-permute-start(bf16[16,128,128]{2,1,0:T(8,128)(2,1)S(1)} %hold.7.refs_8_), channel_id=1, source_target_pairs={{0,2},{1,3},{2,0},{3,1},{4,6},{5,7},{6,4},{7,5},{8,10},{9,11},{10,... | collective-permute-start | bytes 1572872 | tf_op jit(solution)/shard_map/ppermute | solution.py:267
  45.6 0.1 broadcast_select_fusion.1.refs_8_
  45.7 0.6 collective-permute-start.13
  46.3 0.9 collective-permute-start.14
  47.2 2.4 %hops_1.1 = (f32[16,128,128]{2,1,0:T(8,128)S(1)}, f32[16,128,128]{2,1,0:T(8,128)S(1)}, f32[8,128]{1,0:T(8,128)S(1)}) custom-call(s32[16]{0:T(128)S(1)} %stack.67.refs_0_, s32[256]{0:T(256)S(1)} %select_reduce_fusion.refs_1_, s32[256]{0:T(256)S(1)} %collective-permute-done.refs_5_.refs_2_, bf16[2,8,16,128,128]{4,3,2,1,0:T(8,128)(2,1)S(1)} %get-tuple-element.44.refs_3_, ...), custom_call_target="tpu_custom_call" | custom-call | flops 1 | bytes 1 | tf_op jit(solution)/shard_map/hops_1/pallas_call | solution.py:188
  49.6 6.6 %collective-permute-done.11.refs_1_ = bf16[16,128,128]{2,1,0:T(8,128)(2,1)S(1)} collective-permute-done((bf16[16,128,128]{2,1,0:T(8,128)(2,1)S(1)}, bf16[16,128,128]{2,1,0:T(8,128)(2,1)S(1)}, u32[]{:S(2)}, u32[]{:S(2)}) %collective-permute-start.11) | collective-permute-done | bytes 524320 | tf_op jit(solution)/shard_map/ppermute | solution.py:267
  56.1 2.9 %collective-permute-done.10.refs_0_ = bf16[16,128,128]{2,1,0:T(8,128)(2,1)S(1)} collective-permute-done((bf16[16,128,128]{2,1,0:T(8,128)(2,1)S(1)}, bf16[16,128,128]{2,1,0:T(8,128)(2,1)S(1)}, u32[]{:S(2)}, u32[]{:S(2)}) %collective-permute-start.10) | collective-permute-done | bytes 524320 | tf_op jit(solution)/shard_map/ppermute | solution.py:267
  59.0 0.1 broadcast_select_fusion.refs_8_
  59.1 1.6 %collective-permute-start.15 = (bf16[16,128,128]{2,1,0:T(8,128)(2,1)S(1)}, bf16[16,128,128]{2,1,0:T(8,128)(2,1)S(1)}, u32[]{:S(2)}, u32[]{:S(2)}) collective-permute-start(bf16[16,128,128]{2,1,0:T(8,128)(2,1)S(1)} %broadcast_select_fusion.refs_8_), channel_id=1, source_target_pairs={{0,2},{1,3},{2,0},{3,1},{4,6},{5,7},{6,4},{7,5},{8,10},{9,11},{10,... | collective-permute-start | bytes 1572872 | tf_op jit(solution)/shard_map/ppermute | solution.py:267
  60.6 0.9 collective-permute-start.16
  61.5 3.2 %hops_2.1 = (f32[16,128,128]{2,1,0:T(8,128)S(1)}, f32[16,128,128]{2,1,0:T(8,128)S(1)}, f32[8,128]{1,0:T(8,128)S(1)}) custom-call(s32[16]{0:T(128)S(1)} %stack.67.refs_0_, s32[256]{0:T(256)S(1)} %select_reduce_fusion.refs_1_, s32[256]{0:T(256)S(1)} %collective-permute-done.refs_5_.refs_2_, bf16[2,8,16,128,128]{4,3,2,1,0:T(8,128)(2,1)S(1)} %get-tuple-element.44.refs_3_, ...), custom_call_target="tpu_custom_call" | custom-call | flops 1 | bytes 1 | tf_op jit(solution)/shard_map/hops_2/pallas_call | solution.py:188
  64.7 5.5 %collective-permute-done.13.refs_0_ = bf16[16,128,128]{2,1,0:T(8,128)(2,1)S(1)} collective-permute-done((bf16[16,128,128]{2,1,0:T(8,128)(2,1)S(1)}, bf16[16,128,128]{2,1,0:T(8,128)(2,1)S(1)}, u32[]{:S(2)}, u32[]{:S(2)}) %collective-permute-start.13) | collective-permute-done | bytes 524320 | tf_op jit(solution)/shard_map/ppermute | solution.py:267
  70.3 1.5 %collective-permute-start.17 = (bf16[16,128,128]{2,1,0:T(8,128)(2,1)S(1)}, bf16[16,128,128]{2,1,0:T(8,128)(2,1)S(1)}, u32[]{:S(2)}, u32[]{:S(2)}) collective-permute-start(bf16[16,128,128]{2,1,0:T(8,128)(2,1)S(1)} %get-tuple-element.62.refs_7_), channel_id=1, source_target_pairs={{0,2},{1,3},{2,0},{3,1},{4,6},{5,7},{6,4},{7,5},{8,10},{9,11},{10,... | collective-permute-start | bytes 1572872 | tf_op jit(solution)/shard_map/ppermute | solution.py:267
  71.7 3.2 %hops_3.1 = (f32[16,128,128]{2,1,0:T(8,128)S(1)}, f32[16,128,128]{2,1,0:T(8,128)S(1)}, f32[8,128]{1,0:T(8,128)S(1)}) custom-call(s32[16]{0:T(128)S(1)} %stack.67.refs_0_, s32[256]{0:T(256)S(1)} %select_reduce_fusion.refs_1_, s32[256]{0:T(256)S(1)} %collective-permute-done.refs_5_.refs_2_, bf16[2,8,16,128,128]{4,3,2,1,0:T(8,128)(2,1)S(1)} %get-tuple-element.44.refs_3_, ...), custom_call_target="tpu_custom_call" | custom-call | flops 1 | bytes 1 | tf_op jit(solution)/shard_map/hops_3/pallas_call | solution.py:188
  75.0 6.5 %collective-permute-done.15.refs_0_ = bf16[16,128,128]{2,1,0:T(8,128)(2,1)S(1)} collective-permute-done((bf16[16,128,128]{2,1,0:T(8,128)(2,1)S(1)}, bf16[16,128,128]{2,1,0:T(8,128)(2,1)S(1)}, u32[]{:S(2)}, u32[]{:S(2)}) %collective-permute-start.15) | collective-permute-done | bytes 524320 | tf_op jit(solution)/shard_map/ppermute | solution.py:267
  81.5 0.9 collective-permute-start.18
  82.4 0.0 collective-permute-done.16.refs_7_
  82.4 3.0 %hops_4.1 = (f32[16,128,128]{2,1,0:T(8,128)S(1)}, f32[16,128,128]{2,1,0:T(8,128)S(1)}, f32[8,128]{1,0:T(8,128)}) custom-call(s32[16]{0:T(128)S(1)} %stack.67.refs_0_, s32[256]{0:T(256)S(1)} %select_reduce_fusion.refs_1_, s32[256]{0:T(256)S(1)} %collective-permute-done.refs_5_.refs_2_, bf16[2,8,16,128,128]{4,3,2,1,0:T(8,128)(2,1)S(1)} %get-tuple-element.44.refs_3_, ...), custom_call_target="tpu_custom_call" | custom-call | flops 1 | bytes 1 | tf_op jit(solution)/shard_map/hops_4/pallas_call | solution.py:188
  85.3 0.0 collective-permute-done.19.refs_9_
  85.4 4.3 %collective-permute-done.17.refs_6_ = bf16[16,128,128]{2,1,0:T(8,128)(2,1)S(1)} collective-permute-done((bf16[16,128,128]{2,1,0:T(8,128)(2,1)S(1)}, bf16[16,128,128]{2,1,0:T(8,128)(2,1)S(1)}, u32[]{:S(2)}, u32[]{:S(2)}) %collective-permute-start.17) | collective-permute-done | bytes 524320 | tf_op jit(solution)/shard_map/ppermute | solution.py:267
  89.7 1.0 collective-permute-done.18.refs_7_
  90.7 3.1 %hops_5.1 = (f32[16,128,128]{2,1,0:T(8,128)S(1)}, f32[16,128,128]{2,1,0:T(8,128)S(1)}, f32[32,128]{1,0:T(8,128)S(1)}) custom-call(s32[16]{0:T(128)S(1)} %stack.67.refs_0_, s32[256]{0:T(256)S(1)} %select_reduce_fusion.refs_1_, s32[256]{0:T(256)S(1)} %collective-permute-done.refs_5_.refs_2_, bf16[2,8,16,128,128]{4,3,2,1,0:T(8,128)(2,1)S(1)} %get-tuple-element.44.refs_3_, ...), custom_call_target="tpu_custom_call" | custom-call | flops 1 | bytes 1 | tf_op jit(solution)/shard_map/hops_5/pallas_call | solution.py:188
  93.7 0.1 collective-permute-start.20
  93.8 11.3 %all_to_all.11 = f32[32,1,128]{2,1,0:T(1,128)S(1)} all-to-all(f32[32,1,128]{2,1,0:T(1,128)S(1)} %bitcast.23), channel_id=1, replica_groups=mesh['groups'=1,'sector'=32] {'sector'}, dimensions={0} | all-to-all | bytes 32768 | tf_op jit(solution)/shard_map/all_to_all | solution.py:346
  105.1 0.0 collective-permute-done.20.theirs
  105.1 1.3 %finish.1 = (bf16[16,128,128]{2,1,0:T(8,128)(2,1)}, bf16[16,128,128]{2,1,0:T(8,128)(2,1)}, f32[1]{0:T(128)}) custom-call(f32[32,128]{1,0:T(8,128)S(1)} %bitcast.22, bf16[16,128,128]{2,1,0:T(8,128)(2,1)S(1)} %copy-done.1, f32[16,128,128]{2,1,0:T(8,128)S(1)} %get-tuple-element.71.mine, f32[16,128,128]{2,1,0:T(8,128)S(1)} %collective-permute-done.20.theirs), custom_call_target="tpu_custom_call" | custom-call | tf_op jit(solution)/shard_map/finish/pallas_call | solution.py:235
  (19 shorter events, 0.0 us)
Async XLA Ops:
  0.6 19.8 %collective-permute-start.1 = (bf16[16,128,128]{2,1,0:T(8,128)(2,1)}, bf16[16,128,128]{2,1,0:T(8,128)(2,1)}, u32[]{:S(2)}, u32[]{:S(2)}) collective-permute-start(bf16[16,128,128]{2,1,0:T(8,128)(2,1)} %psi.1), channel_id=1, source_target_pairs={{0,8},{1,9},{2,10},{3,11},{4,12},{5,13},{6,14},{7,15},{8,0},{9,1},... | collective-permute-start | bytes 1572872 | tf_op jit(solution)/shard_map/ppermute | solution.py:267
  3.7 16.7 %collective-permute-start.2 = (bf16[16,128,128]{2,1,0:T(8,128)(2,1)}, bf16[16,128,128]{2,1,0:T(8,128)(2,1)S(1)}, u32[]{:S(2)}, u32[]{:S(2)}) collective-permute-start(bf16[16,128,128]{2,1,0:T(8,128)(2,1)} %psi.1), channel_id=1, source_target_pairs={{0,0},{1,1},{2,2},{3,3},{4,4},{5,5},{6,6},{7,7},{8,16},{9,17},{10,... | collective-permute-start | bytes 1572872 | tf_op jit(solution)/shard_map/ppermute | solution.py:275
  5.4 15.0 %collective-permute-start.3 = (bf16[16,128,128]{2,1,0:T(8,128)(2,1)}, bf16[16,128,128]{2,1,0:T(8,128)(2,1)S(1)}, u32[]{:S(2)}, u32[]{:S(2)}) collective-permute-start(bf16[16,128,128]{2,1,0:T(8,128)(2,1)} %psi.1), channel_id=1, source_target_pairs={{0,2},{1,3},{2,0},{3,1},{4,6},{5,7},{6,4},{7,5},{8,10},{9,11},{10,... | collective-permute-start | bytes 1572872 | tf_op jit(solution)/shard_map/ppermute | solution.py:267
  6.9 13.6 %collective-permute-start.4 = (bf16[16,128,128]{2,1,0:T(8,128)(2,1)}, bf16[16,128,128]{2,1,0:T(8,128)(2,1)S(1)}, u32[]{:S(2)}, u32[]{:S(2)}) collective-permute-start(bf16[16,128,128]{2,1,0:T(8,128)(2,1)} %psi.1), channel_id=1, source_target_pairs={{0,4},{1,5},{2,6},{3,7},{4,0},{5,1},{6,2},{7,3},{8,12},{9,13},{10,... | collective-permute-start | bytes 1572872 | tf_op jit(solution)/shard_map/ppermute | solution.py:267
  10.3 10.1 %collective-permute-start = (s32[256]{0:T(256)S(1)}, s32[256]{0:T(256)S(1)}, u32[]{:S(2)}, u32[]{:S(2)}) collective-permute-start(s32[256]{0:T(256)S(1)} %select_reduce_fusion.refs_1_), channel_id=1, source_target_pairs={{0,1},{1,0},{2,3},{3,2},{4,5},{5,4},{6,7},{7,6},{8,9},{9,8},{10,11... | collective-permute-start | bytes 3080 | tf_op jit(solution)/shard_map/ppermute | solution.py:267
  10.4 1.0 copy-start
  11.4 0.7 copy-start.8
  20.4 5.1 %copy-start.6 = (f32[16,128,128]{2,1,0:T(8,128)}, f32[16,128,128]{2,1,0:T(8,128)S(1)}, u32[]{:S(2)}) copy-start(f32[16,128,128]{2,1,0:T(8,128)S(1)} %get-tuple-element.40.refs_5_) | copy-start | bytes 3145732
  20.5 0.9 copy-start.2
  21.4 0.8 copy-start.4
  22.2 7.6 %copy-start.1 = (bf16[16,128,128]{2,1,0:T(8,128)(2,1)S(1)}, bf16[16,128,128]{2,1,0:T(8,128)(2,1)}, u32[]{:S(2)}) copy-start(bf16[16,128,128]{2,1,0:T(8,128)(2,1)} %psi.1) | copy-start | bytes 1572868
  22.2 7.6 %collective-permute-start.5 = (bf16[8,16,128,128]{3,2,1,0:T(8,128)(2,1)}, bf16[8,16,128,128]{3,2,1,0:T(8,128)(2,1)}, u32[]{:S(2)}, u32[]{:S(2)}) collective-permute-start(bf16[8,16,128,128]{3,2,1,0:T(8,128)(2,1)} %get-tuple-element.39.refs_3_), channel_id=1, source_target_pairs={{0,1},{1,0},{2,3},{3,2},{4,5},{5,4},{6,7},{7,6},{8,9},{9,8},{10,11... | collective-permute-start | bytes 12582920 | tf_op jit(solution)/shard_map/ppermute | solution.py:267
  22.7 14.9 %collective-permute-start.6 = (bf16[16,128,128]{2,1,0:T(8,128)(2,1)}, bf16[16,128,128]{2,1,0:T(8,128)(2,1)S(1)}, u32[]{:S(2)}, u32[]{:S(2)}) collective-permute-start(bf16[16,128,128]{2,1,0:T(8,128)(2,1)} %get-tuple-element.43.refs_9_), channel_id=1, source_target_pairs={{0,2},{1,3},{2,0},{3,1},{4,6},{5,7},{6,4},{7,5},{8,10},{9,11},{10,... | collective-permute-start | bytes 1572872 | tf_op jit(solution)/shard_map/ppermute | solution.py:267
  23.2 14.3 %collective-permute-start.7 = (bf16[16,128,128]{2,1,0:T(8,128)(2,1)}, bf16[16,128,128]{2,1,0:T(8,128)(2,1)S(1)}, u32[]{:S(2)}, u32[]{:S(2)}) collective-permute-start(bf16[16,128,128]{2,1,0:T(8,128)(2,1)} %get-tuple-element.43.refs_9_), channel_id=1, source_target_pairs={{0,4},{1,5},{2,6},{3,7},{4,0},{5,1},{6,2},{7,3},{8,12},{9,13},{10,... | collective-permute-start | bytes 1572872 | tf_op jit(solution)/shard_map/ppermute | solution.py:267
  23.9 13.7 %collective-permute-start.9 = (bf16[16,128,128]{2,1,0:T(8,128)(2,1)}, bf16[16,128,128]{2,1,0:T(8,128)(2,1)S(1)}, u32[]{:S(2)}, u32[]{:S(2)}) collective-permute-start(bf16[16,128,128]{2,1,0:T(8,128)(2,1)} %get-tuple-element.43.refs_9_), channel_id=1, source_target_pairs={{0,0},{1,1},{2,2},{3,3},{4,4},{5,5},{6,6},{7,7},{8,16},{9,17},{10,... | collective-permute-start | bytes 1572872 | tf_op jit(solution)/shard_map/ppermute | solution.py:275
  25.6 15.7 %collective-permute-start.8 = (bf16[16,128,128]{2,1,0:T(8,128)(2,1)}, bf16[16,128,128]{2,1,0:T(8,128)(2,1)S(1)}, u32[]{:S(2)}, u32[]{:S(2)}) collective-permute-start(bf16[16,128,128]{2,1,0:T(8,128)(2,1)} %copy-done.4), channel_id=1, source_target_pairs={{0,8},{1,9},{2,10},{3,11},{4,12},{5,13},{6,14},{7,15},{8,0},{9,1},... | collective-permute-start | bytes 1572872 | tf_op jit(solution)/shard_map/ppermute | solution.py:267
  29.4 1.0 copy-start.3
  29.4 1.4 %copy-start.7 = (f32[16,128,128]{2,1,0:T(8,128)S(1)}, f32[16,128,128]{2,1,0:T(8,128)}, u32[]{:S(2)}) copy-start(f32[16,128,128]{2,1,0:T(8,128)} %copy-done.6) | copy-start | bytes 3145732
  30.8 14.9 %copy-start.5 = (bf16[16,128,128]{2,1,0:T(8,128)(2,1)S(1)}, bf16[16,128,128]{2,1,0:T(8,128)(2,1)}, u32[]{:S(2)}) copy-start(bf16[16,128,128]{2,1,0:T(8,128)(2,1)} %copy-done.4) | copy-start | bytes 1572868
  41.3 14.9 %collective-permute-start.11 = (bf16[16,128,128]{2,1,0:T(8,128)(2,1)S(1)}, bf16[16,128,128]{2,1,0:T(8,128)(2,1)S(1)}, u32[]{:S(2)}, u32[]{:S(2)}) collective-permute-start(bf16[16,128,128]{2,1,0:T(8,128)(2,1)S(1)} %get-tuple-element.49.refs_6_), channel_id=1, source_target_pairs={{0,4},{1,5},{2,6},{3,7},{4,0},{5,1},{6,2},{7,3},{8,12},{9,13},{10,... | collective-permute-start | bytes 1572872 | tf_op jit(solution)/shard_map/ppermute | solution.py:267
  42.4 13.7 %collective-permute-start.12 = (bf16[16,128,128]{2,1,0:T(8,128)(2,1)S(1)}, bf16[16,128,128]{2,1,0:T(8,128)(2,1)S(1)}, u32[]{:S(2)}, u32[]{:S(2)}) collective-permute-start(bf16[16,128,128]{2,1,0:T(8,128)(2,1)S(1)} %get-tuple-element.53), channel_id=1, source_target_pairs={{0,8},{1,9},{2,10},{3,11},{4,12},{5,13},{6,14},{7,15},{8,0},{9,1},... | collective-permute-start | bytes 1572872 | tf_op jit(solution)/shard_map/ppermute | solution.py:267
  44.2 14.9 %collective-permute-start.10 = (bf16[16,128,128]{2,1,0:T(8,128)(2,1)S(1)}, bf16[16,128,128]{2,1,0:T(8,128)(2,1)S(1)}, u32[]{:S(2)}, u32[]{:S(2)}) collective-permute-start(bf16[16,128,128]{2,1,0:T(8,128)(2,1)S(1)} %hold.7.refs_8_), channel_id=1, source_target_pairs={{0,2},{1,3},{2,0},{3,1},{4,6},{5,7},{6,4},{7,5},{8,10},{9,11},{10,... | collective-permute-start | bytes 1572872 | tf_op jit(solution)/shard_map/ppermute | solution.py:267
  45.7 24.5 %collective-permute-start.13 = (bf16[16,128,128]{2,1,0:T(8,128)(2,1)S(1)}, bf16[16,128,128]{2,1,0:T(8,128)(2,1)S(1)}, u32[]{:S(2)}, u32[]{:S(2)}) collective-permute-start(bf16[16,128,128]{2,1,0:T(8,128)(2,1)S(1)} %broadcast_select_fusion.1.refs_8_), channel_id=1, source_target_pairs={{0,2},{1,3},{2,0},{3,1},{4,6},{5,7},{6,4},{7,5},{8,10},{9,11},{10,... | collective-permute-start | bytes 1572872 | tf_op jit(solution)/shard_map/ppermute | solution.py:267
  46.3 23.9 %collective-permute-start.14 = (bf16[16,128,128]{2,1,0:T(8,128)(2,1)S(1)}, bf16[16,128,128]{2,1,0:T(8,128)(2,1)S(1)}, u32[]{:S(2)}, u32[]{:S(2)}) collective-permute-start(bf16[16,128,128]{2,1,0:T(8,128)(2,1)S(1)} %broadcast_select_fusion.1.refs_8_), channel_id=1, source_target_pairs={{0,4},{1,5},{2,6},{3,7},{4,0},{5,1},{6,2},{7,3},{8,12},{9,13},{10,... | collective-permute-start | bytes 1572872 | tf_op jit(solution)/shard_map/ppermute | solution.py:267
  59.1 22.4 %collective-permute-start.15 = (bf16[16,128,128]{2,1,0:T(8,128)(2,1)S(1)}, bf16[16,128,128]{2,1,0:T(8,128)(2,1)S(1)}, u32[]{:S(2)}, u32[]{:S(2)}) collective-permute-start(bf16[16,128,128]{2,1,0:T(8,128)(2,1)S(1)} %broadcast_select_fusion.refs_8_), channel_id=1, source_target_pairs={{0,2},{1,3},{2,0},{3,1},{4,6},{5,7},{6,4},{7,5},{8,10},{9,11},{10,... | collective-permute-start | bytes 1572872 | tf_op jit(solution)/shard_map/ppermute | solution.py:267
  60.6 24.7 %collective-permute-start.19 = (bf16[16,128,128]{2,1,0:T(8,128)(2,1)S(1)}, bf16[16,128,128]{2,1,0:T(8,128)(2,1)S(1)}, u32[]{:S(2)}, u32[]{:S(2)}) collective-permute-start(bf16[16,128,128]{2,1,0:T(8,128)(2,1)S(1)} %copy-done.1), channel_id=1, source_target_pairs={{0,1},{1,0},{2,3},{3,2},{4,5},{5,4},{6,7},{7,6},{8,9},{9,8},{10,11... | collective-permute-start | bytes 1572872 | tf_op jit(solution)/shard_map/ppermute | solution.py:267
  60.6 21.7 %collective-permute-start.16 = (bf16[16,128,128]{2,1,0:T(8,128)(2,1)S(1)}, bf16[16,128,128]{2,1,0:T(8,128)(2,1)S(1)}, u32[]{:S(2)}, u32[]{:S(2)}) collective-permute-start(bf16[16,128,128]{2,1,0:T(8,128)(2,1)S(1)} %broadcast_select_fusion.refs_8_), channel_id=1, source_target_pairs={{0,4},{1,5},{2,6},{3,7},{4,0},{5,1},{6,2},{7,3},{8,12},{9,13},{10,... | collective-permute-start | bytes 1572872 | tf_op jit(solution)/shard_map/ppermute | solution.py:267
  70.3 19.4 %collective-permute-start.17 = (bf16[16,128,128]{2,1,0:T(8,128)(2,1)S(1)}, bf16[16,128,128]{2,1,0:T(8,128)(2,1)S(1)}, u32[]{:S(2)}, u32[]{:S(2)}) collective-permute-start(bf16[16,128,128]{2,1,0:T(8,128)(2,1)S(1)} %get-tuple-element.62.refs_7_), channel_id=1, source_target_pairs={{0,2},{1,3},{2,0},{3,1},{4,6},{5,7},{6,4},{7,5},{8,10},{9,11},{10,... | collective-permute-start | bytes 1572872 | tf_op jit(solution)/shard_map/ppermute | solution.py:267
  81.5 9.2 %collective-permute-start.18 = (bf16[16,128,128]{2,1,0:T(8,128)(2,1)S(1)}, bf16[16,128,128]{2,1,0:T(8,128)(2,1)S(1)}, u32[]{:S(2)}, u32[]{:S(2)}) collective-permute-start(bf16[16,128,128]{2,1,0:T(8,128)(2,1)S(1)} %hold.11.refs_6_), channel_id=1, source_target_pairs={{0,4},{1,5},{2,6},{3,7},{4,0},{5,1},{6,2},{7,3},{8,12},{9,13},{10,... | collective-permute-start | bytes 1572872 | tf_op jit(solution)/shard_map/ppermute | solution.py:267
  93.7 11.4 %collective-permute-start.20 = (f32[16,128,128]{2,1,0:T(8,128)S(1)}, f32[16,128,128]{2,1,0:T(8,128)S(1)}, u32[]{:S(2)}, u32[]{:S(2)}) collective-permute-start(f32[16,128,128]{2,1,0:T(8,128)S(1)} %get-tuple-element.72), channel_id=1, source_target_pairs={{0,1},{1,0},{2,3},{3,2},{4,5},{5,4},{6,7},{7,6},{8,9},{9,8},{10,11... | collective-permute-start | bytes 3145736 | tf_op jit(solution)/shard_map/ppermute | solution.py:267

commit v3 on v2

--- a/solution.py
+++ b/solution.py
@@ -10,8 +10,7 @@
 F32 = jnp.float32
 BF16 = jnp.bfloat16
 VMEM_BYTES = 16 * 1024 * 1024
-LOCAL_BYTES = 48 * 1024 * 1024
-FIRST_BYTES = 24 * 1024 * 1024
+LOCAL_BYTES = 50 * 1024 * 1024
 COST = pl.CostEstimate(flops=1, bytes_accessed=1, transcendentals=0)
 ANY = pl.BlockSpec(memory_space=pl.ANY)
 VMEM = pl.BlockSpec(memory_space=pltpu.VMEM)
@@ -60,37 +59,47 @@
     return hpsi.astype(BF16), residual, quotient.reshape(1)
 
 
-def local_kernel(onsite, psi, right, left, acc, square, hop_env, r_buf, l_buf, middle, sems):
+def local_kernel(onsite, psi, right, left, acc, square, moved, onsite_buf, psi_buf, r_buf, l_buf, middle, sems, moved_sems):
     rows, cols, size = psi.shape[0], psi.shape[1], psi.shape[2]
     chans = r_buf.shape[1]
-    r_copy = [pltpu.make_async_copy(right.at[j, pl.ds(0, chans)], r_buf.at[j], sems.at[0, j]) for j in range(cols)]
-    l_copy = [pltpu.make_async_copy(left.at[i, pl.ds(0, chans)], l_buf.at[i], sems.at[1, i]) for i in range(rows)]
-    hop_copy = []
-    for n in range(cols + rows):
-        env, row = (right, n) if n < cols else (left, n - cols)
-        src = env.at[row, pl.ds(chans, hop_env.shape[1])]
-        hop_copy.append(pltpu.make_async_copy(src, hop_env.at[n], sems.at[2 + n // cols, n % cols]))
-    for copy in r_copy + l_copy + hop_copy:
+    hops = right.shape[1] - chans
+    copies = [pltpu.make_async_copy(psi, psi_buf, sems.at[0, 0]), pltpu.make_async_copy(onsite, onsite_buf, sems.at[0, 1])]
+    r_copy = [pltpu.make_async_copy(right.at[j, pl.ds(0, chans)], r_buf.at[j], sems.at[1, j]) for j in range(cols)]
+    l_copy = [pltpu.make_async_copy(left.at[i, pl.ds(0, chans)], l_buf.at[i], sems.at[2, i]) for i in range(rows)]
+    parts = [right.at[j, pl.ds(chans, hops)] for j in range(cols)] + [left.at[i, pl.ds(chans, hops)] for i in range(rows)]
+    for n, part in enumerate(parts):
+        parts[n] = pltpu.make_async_copy(part, moved.at[pl.ds(n * hops, hops)], moved_sems.at[n])
+    for copy in copies + r_copy + l_copy:
         copy.start()
+    for copy in copies:
+        copy.wait()
     for j in range(cols):
         r_copy[j].wait()
-        column = psi[:, j].reshape(rows * size, size)
-        for h in range(chans):
-            product = dot(column, r_buf[j, h]).astype(BF16)
+        if j == 1:
+            for part in parts:
+                part.start()
+        column = psi_buf[:, j].reshape(rows * size, size)
+        for h in range(0, chans, 2):
+            pair = jnp.concatenate([r_buf[j, h], r_buf[j, h + 1]], axis=1)
+            product = dot(column, pair).astype(BF16)
             for i in range(rows):
-                middle[i, pl.ds(h * size, size), pl.ds(j * size, size)] = product[i * size : (i + 1) * size]
+                for g in range(2):
+                    block = product[i * size : (i + 1) * size, g * size : (g + 1) * size]
+                    middle[i, pl.ds((h + g) * size, size), pl.ds(j * size, size)] = block
     total = jnp.zeros((size, size), F32)
+    first = (rows + cols) * hops
     for i in range(rows):
         l_copy[i].wait()
         wide = jnp.concatenate([l_buf[i, h] for h in range(chans)], axis=1)
         summed = dot(wide, middle[i])
         for j in range(cols):
-            block = psi[i, j].astype(F32)
-            acc[i * cols + j] = summed[:, j * size : (j + 1) * size] + onsite[i * cols + j] * block
+            moved[first + i * cols + j] = psi_buf[i, j]
+            block = psi_buf[i, j].astype(F32)
+            acc[i * cols + j] = summed[:, j * size : (j + 1) * size] + onsite_buf[i * cols + j] * block
             total += block * block
     square[...] = total
-    for copy in hop_copy:
-        copy.wait()
+    for part in parts:
+        part.wait()
 
 
 def local_call(onsite, psi, right, left, hops):
@@ -101,15 +110,18 @@
         out_shape=(
             jax.ShapeDtypeStruct((sec, size, size), F32),
             jax.ShapeDtypeStruct((size, size), F32),
-            jax.ShapeDtypeStruct((cols + rows, hops, size, size), BF16),
+            jax.ShapeDtypeStruct(((rows + cols) * hops + sec, size, size), BF16),
         ),
-        in_specs=[SMEM, VMEM, HBM, HBM],
+        in_specs=[HBM] * 4,
         out_specs=[VMEM] * 3,
         scratch_shapes=[
+            pltpu.SMEM((sec,), F32),
+            pltpu.VMEM((rows, cols, size, size), BF16),
             pltpu.VMEM((cols, chans, size, size), BF16),
             pltpu.VMEM((rows, chans, size, size), BF16),
             pltpu.VMEM((rows, chans * size, cols * size), BF16),
-            pltpu.SemaphoreType.DMA((4, max(rows, cols))),
+            pltpu.SemaphoreType.DMA((3, max(rows, cols, 2))),
+            pltpu.SemaphoreType.DMA((rows + cols,)),
         ],
         compiler_params=pltpu.CompilerParams(vmem_limit_bytes=LOCAL_BYTES),
         cost_estimate=COST,
@@ -121,56 +133,47 @@
     refs = list(refs)
     take = lambda n: [refs.pop(0) for _ in range(n)]
     order, *terms = take(3)
-    envs = take(2) if first else take(1)
+    envs = take(2 if first else 1)
     acc_in = take(1 if first else 2)
     bufs = take(count)
-    psis = take(2) if last else []
     square = take(1)[0] if last else None
     acc = take(2)
     sums = take(1)[0]
     env = take(1)[0] if first else envs[0]
     psi, sems, env_sems = refs
-    hops, rows = env.shape[2], env.shape[1] // 2
     copies = [pltpu.make_async_copy(buf, psi.at[s], sems.at[s]) for s, buf in enumerate(bufs)]
-    fills = []
-    if first:
-        for e in range(2):
-            for f in range(2):
-                half = pl.ds(f * rows, rows)
-                fills.append(pltpu.make_async_copy(envs[e].at[half], env.at[e, half], env_sems.at[2 * e + f]))
+    fills = [pltpu.make_async_copy(envs[e], env.at[e], env_sems.at[e]) for e in range(2)] if first else []
     for copy in copies + fills:
         copy.start()
-    for e in range(2):
-        acc[e][...] = acc_in[e][...] if e < len(acc_in) else jnp.zeros(acc[e].shape, F32)
+    if first:
+        copies.append(pltpu.make_async_copy(acc_in[0], acc[0], env_sems.at[2]))
+        copies[-1].start()
+        acc[1][...] = jnp.zeros(acc[1].shape, F32)
+    else:
+        for e in range(2):
+            acc[e][...] = acc_in[e][...]
     for copy in copies:
         copy.wait()
-    for e in range(2):
-        for fill in fills[2 * e : 2 * e + 2]:
-            fill.wait()
-
-        def owner_step(s, carry, e=e):
-            slot = order[base + s] * capacity
-            words = [terms[e][slot + r] for r in range(capacity)]
-            mids = []
-            for w in words:
-                right = (w >> 16) & 255
-                mids.append(dot(psi[s, w & 255], env[e, right // hops, right % hops]).astype(BF16))
-            parts = []
-            for w, mid in zip(words, mids):
-                left = w >> 24
-                parts.append(dot(env[e, left // hops, left % hops], mid))
-            for w, part in zip(words, parts):
-                t = (w >> 8) & 255
-                acc[e][t] = acc[e][t] + part
-            return carry
-
-        lax.fori_loop(0, count, owner_step, 0)
+    for fill in fills:
+        fill.wait()
+
+    def owner_step(s, carry):
+        slot = order[base + s] * capacity
+        words = [(e, terms[e][slot + r]) for e in range(2) for r in range(capacity)]
+        mids = [dot(psi[s, w & 255], env[e, (w >> 16) & 255]).astype(BF16) for e, w in words]
+        parts = [dot(env[e, w >> 24], mid) for (e, w), mid in zip(words, mids)]
+        for (e, w), part in zip(words, parts):
+            t = (w >> 8) & 255
+            acc[e][t] = acc[e][t] + part
+        return carry
+
+    lax.fori_loop(0, count, owner_step, 0, unroll=2)
     if last:
         total = jnp.zeros(acc[0].shape[1:], F32)
+        sec = acc[0].shape[0]
+        first_psi = env.shape[1] - sec
         for e in range(2):
-            total = lax.fori_loop(
-                0, acc[e].shape[0], lambda t, v, e=e: v + psis[e][t].astype(F32) * acc[e][t], total
-            )
+            total = lax.fori_loop(0, sec, lambda t, v, e=e: v + env[e, first_psi + t].astype(F32) * acc[e][t], total)
         lanes = lax.broadcasted_iota(jnp.int32, sums.shape, 1)
         sums[...] = jnp.where(lanes < sums.shape[1] // 2, jnp.sum(total), jnp.sum(square[...]))
     else:
@@ -189,17 +192,16 @@
         functools.partial(hop_kernel, base, count, first, last, capacity),
         out_shape=out_shape,
         in_specs=[SMEM] * 3
-        + [HBM if first else VMEM] * len(envs)
-        + [VMEM] * len(accs)
+        + [ANY if first else VMEM] * (len(envs) + len(accs))
         + [ANY] * count
         + [VMEM] * len(last_args),
         out_specs=[VMEM] * len(out_shape),
         scratch_shapes=[
             pltpu.VMEM((count, sec, size, size), BF16),
             pltpu.SemaphoreType.DMA((count,)),
-            pltpu.SemaphoreType.DMA((4,)),
+            pltpu.SemaphoreType.DMA((3,)),
         ],
-        compiler_params=pltpu.CompilerParams(vmem_limit_bytes=FIRST_BYTES if first else VMEM_BYTES),
+        compiler_params=pltpu.CompilerParams(vmem_limit_bytes=VMEM_BYTES),
         cost_estimate=COST,
         name=name,
     )(order, *terms, *envs, *accs, *bufs, *last_args)
@@ -270,8 +272,7 @@
         pairs = []
         for i in range(owners):
             layer = i // z
-            to = layers - 1 - layer if layer in (1, 2) else layer
-            pairs.append((i, to * z + i % z))
+            pairs.append((i, (layers - 1 - layer) * z + i % z if layer in (1, 2) else i ^ core))
         return lax.ppermute(value, "sector", pairs)
 
     me = lax.axis_index("sector")
@@ -279,11 +280,9 @@
     layer_masks = [0, z, jnp.where(outer, 2 * z, 3 * z), jnp.where(outer, 3 * z, 2 * z)]
     groups = [
         [(0, 0), (0, x), (0, y), (1, 0)],
-        [(1, x), (1, y)],
-        [(0, xy), (1, xy), (2, 0)],
-        [(2, x), (2, y), (3, 0)],
-        [(3, x), (3, y)],
-        [(2, xy), (3, xy)],
+        [(0, xy), (1, y), (2, 0), (2, x), (2, y), (3, 0)],
+        [(3, x), (3, y), (1, x)],
+        [(2, xy), (3, xy), (1, xy)],
     ]
     order = jnp.stack([me ^ layer_masks[b] ^ bits for group in groups for b, bits in group])
 
@@ -294,55 +293,49 @@
         held.update(zip(keys, hold_until([held[key] for key in keys], tokens)))
 
     def run(group, last_args=()):
-        first = len(state["accs"]) == 1
         out = hop_call(
             f"hops_{group}", order, state["base"], terms, state["envs"], state["accs"],
             tuple(held[key] for key in groups[group]), last_args, owners, capacity,
         )
         state["accs"] = out[:2]
+        if group == 0:
+            state["envs"] = out[3:]
         state["base"] += len(groups[group])
-        if first:
-            state["envs"] = out[3:]
         return out[2]
 
+    held[0, x], held[0, y] = swap(wavefunction, x), swap(wavefunction, y)
     held[1, 0] = swap(wavefunction, z)
     held["middle"] = swap_middle(wavefunction)
-    held[0, x], held[0, y] = swap(wavefunction, x), swap(wavefunction, y)
     terms = term_words(source_device, source_block, right_env.shape[0], capacity)
     terms = (terms, swap(terms, core))
     acc, square, held["env"] = local_call(onsite_energy, wavefunction, right_env, left_env, hops)
-    hold([(1, 0), "middle", (0, x), (0, y), "env"], terms[1])
-
-    for link in (x, y):
-        held[1, link] = swap(held[1, 0], link)
+    hold([(0, x), (0, y), (1, 0), "middle", "env"], terms[1])
+
+    held[0, xy] = swap(held[0, y], x)
+    held[1, y] = swap(held[1, 0], y)
     held["outer"] = swap(held["middle"], z)
     held["middle_2"] = swap_middle(held[1, 0])
-    env_sib = swap(held["env"], core)
-    hold([(0, y)], env_sib)
-    state["accs"], state["envs"] = (acc,), (held["env"], env_sib)
-
-    held[0, xy] = swap(held[0, y], x)
+    held["env_sib"] = swap(held["env"], core)
+    hold([(0, xy), (1, y), "outer", "middle_2", "env_sib"])
+
+    held[2, 0] = jnp.where(outer, held["outer"], held["middle"])
+    held[2, x], held[2, y] = swap(held[2, 0], x), swap(held[2, 0], y)
+    held["outer_2"] = swap(held["middle_2"], z)
+    state["accs"], state["envs"] = (acc,), (held["env"], held["env_sib"])
     done = run(0)
-    hold([(1, x), (1, y), "outer", "middle_2"], done)
-    held[1, xy] = swap(held[1, x], y)
-    held["outer_2"] = swap(held["middle_2"], z)
-    held[2, 0] = jnp.where(outer, held["outer"], held["middle"])
-    for link in (x, y):
-        held[2, link] = swap(held[2, 0], link)
+    hold([(2, x), (2, y), "outer_2", (0, x)], done)
+
+    held[3, 0] = jnp.where(outer, held["outer_2"], held["middle_2"])
+    held[3, x], held[3, y] = swap(held[3, 0], x), swap(held[3, 0], y)
+    held[1, x] = swap(held[0, x], z)
     done = run(1)
-    hold([(0, xy), (1, xy), "outer_2"], done)
-    held[3, 0] = jnp.where(outer, held["outer_2"], held["middle_2"])
-    for link in (x, y):
-        held[3, link] = swap(held[3, 0], link)
-    done = run(2)
-    hold([(2, x), (2, y)], done)
+    hold([(3, x), (3, y), (1, x), (2, y), (0, xy)], done)
+
     held[2, xy] = swap(held[2, y], x)
-    done = run(3)
-    hold([(3, x)], done)
     held[3, xy] = swap(held[3, x], y)
-    run(4)
-    psi_sib = swap(wavefunction, core)
-    sums = run(5, (wavefunction, psi_sib, square))
+    held[1, xy] = swap(held[0, xy], z)
+    run(2)
+    sums = run(3, (square,))
     sums = lax.all_to_all(sums, "sector", 0, 0, tiled=True)
     mine, theirs = state["accs"]
     return finish_call(sums, wavefunction, mine, swap(theirs, core))
@@ -352,6 +345,7 @@
     owners = lax.axis_size("sector")
     sec, hops = source_device.shape
     fits = owners == 32 and sec <= 256 and (left_env.shape[0] + right_env.shape[0]) * hops <= 128
+    fits = fits and (left_env.shape[1] - hops) % 2 == 0
     plan = spread_everywhere if fits and 2 * (sec * hops // owners) >= sec else ask_and_send
     return plan(wavefunction, onsite_energy, left_env, right_env, source_device, source_block)
 

time: 107 us -> 94 us (0.88)
  starting transfers between devices: 25.7 us -> 17.9 us
  Pallas kernels: 31.2 us -> 23.6 us
  waiting for transfers between devices: 31 us -> 33.1 us
    pallas_call x6 -> x4, Pallas kernels: 21.5 us -> 14.2 us  [hop_call(): pl.pallas_call(functools.partial(hop_kernel, base, count, first, last, ca...]
    ppermute x19 -> x18, starting transfers between devices: 22.3 us -> 17.4 us  [swap(): return lax.ppermute(value, 'sector', [(i, i ^ mask) for i in range(owners)])]
    ppermute x2, starting transfers between devices: 3.38 us -> 0.52 us  [swap_middle(): return lax.ppermute(value, 'sector', pairs)]
    ppermute x19 -> x18, waiting for transfers between devices: 30.9 us -> 33.1 us  [swap(): return lax.ppermute(value, 'sector', [(i, i ^ mask) for i in range(owners)])]
    unnamed x18 -> x14, local copies, waits for them, and re-layouts: 4.36 us -> 3.72 us
  transfers between devices with their start and end apart: 21 -> 20, of which waited for: 8 -> 11; matrix products, arithmetic and copies ran while one was open for 2% -> 2% of each run, Pallas kernels for 25% -> 21%
where the time goes in v3:
time: 94 us; the launch traced here: 93.6 us
  waiting for transfers between devices  33.1 us (35%)
  Pallas kernels  23.6 us (25%)
  starting transfers between devices  17.9 us (19%)
  blocking collectives  11.4 us (12%)
  local copies, waits for them, and re-layouts  5.36 us (6%)
  other arithmetic  1.47 us (2%)
    ppermute x18, waiting for transfers between devices, swap(): return lax.ppermute(value, 'sector', [(i, i ^ mask) for i in range(owners)])  33.1 us
    ppermute x18, starting transfers between devices, swap(): return lax.ppermute(value, 'sector', [(i, i ^ mask) for i in range(owners)])  17.4 us
    pallas_call x4, Pallas kernels, hop_call(): pl.pallas_call(functools.partial(hop_kernel, base, count, first, last, ca...  14.2 us
    all_to_all x1, blocking collectives, spread_everywhere(): sums = lax.all_to_all(sums, 'sector', 0, 0, tiled=True)  11.4 us
    pallas_call x1, Pallas kernels, local_call(): pl.pallas_call(local_kernel, out_shape=(jax.ShapeDtypeStruct((sec, size,...  8.01 us
    unnamed x14, local copies, waits for them, and re-layouts  3.72 us
  transfers between devices with their start and end apart: 20, of which 11 were waited for; matrix products, arithmetic and copies ran while one was open for 2% of the time, Pallas kernels for 21%

profile of v3, /device:TPU:0, one launch (start us, length us, event | category | flops | bytes accessed | tf_op | source)
XLA Modules:
  0.0 93.6 jit_solution(6704718685128308933)
XLA Ops:
  0.6 0.5 collective-permute-start.4
  1.1 4.1 %collective-permute-start.3 = (bf16[16,128,128]{2,1,0:T(8,128)(2,1)}, bf16[16,128,128]{2,1,0:T(8,128)(2,1)}, u32[]{:S(2)}, u32[]{:S(2)}) collective-permute-start(bf16[16,128,128]{2,1,0:T(8,128)(2,1)} %psi.1), channel_id=1, source_target_pairs={{0,8},{1,9},{2,10},{3,11},{4,12},{5,13},{6,14},{7,15},{8,0},{9,1},... | collective-permute-start | bytes 1572872 | tf_op jit(solution)/shard_map/ppermute | solution.py:269
  5.3 1.5 %collective-permute-start.2 = (bf16[16,128,128]{2,1,0:T(8,128)(2,1)}, bf16[16,128,128]{2,1,0:T(8,128)(2,1)}, u32[]{:S(2)}, u32[]{:S(2)}) collective-permute-start(bf16[16,128,128]{2,1,0:T(8,128)(2,1)} %psi.1), channel_id=1, source_target_pairs={{0,4},{1,5},{2,6},{3,7},{4,0},{5,1},{6,2},{7,3},{8,12},{9,13},{10,... | collective-permute-start | bytes 1572872 | tf_op jit(solution)/shard_map/ppermute | solution.py:269
  6.8 1.5 %collective-permute-start.1 = (bf16[16,128,128]{2,1,0:T(8,128)(2,1)}, bf16[16,128,128]{2,1,0:T(8,128)(2,1)S(1)}, u32[]{:S(2)}, u32[]{:S(2)}) collective-permute-start(bf16[16,128,128]{2,1,0:T(8,128)(2,1)} %psi.1), channel_id=1, source_target_pairs={{0,2},{1,3},{2,0},{3,1},{4,6},{5,7},{6,4},{7,5},{8,10},{9,11},{10,... | collective-permute-start | bytes 1572872 | tf_op jit(solution)/shard_map/ppermute | solution.py:269
  8.3 0.8 reshape.88
  9.1 0.8 reshape.89
  9.9 0.2 convert_reduce_fusion
  10.1 0.1 select_reduce_fusion.refs_1_
  10.2 0.1 collective-permute-start
  10.3 0.0 copy-start
  10.3 1.0 %copy-done = bf16[16,128,128]{2,1,0:T(8,128)(2,1)S(1)} copy-done((bf16[16,128,128]{2,1,0:T(8,128)(2,1)S(1)}, bf16[16,128,128]{2,1,0:T(8,128)(2,1)}, u32[]{:S(2)}) %copy-start) | copy-done | bytes 524312
  11.3 0.7 copy-done.6
  12.0 8.0 %local_channels.1 = (f32[16,128,128]{2,1,0:T(8,128)S(1)}, f32[128,128]{1,0:T(8,128)S(1)}, bf16[144,128,128]{2,1,0:T(8,128)(2,1)}) custom-call(f32[16]{0:T(128)S(1)} %copy-done.6, bf16[4,4,128,128]{3,2,1,0:T(8,128)(2,1)S(1)} %bitcast.21, bf16[4,32,128,128]{3,2,1,0:T(8,128)(2,1)} %right.1, bf16[4,32,128,128]{3,2,1,0:T(8,128)(2,1)} %left.1), custom_call_target="tpu_custom_call" | custom-call | flops 1 | bytes 1 | tf_op jit(solution)/shard_map/local_channels/pallas_call | solution.py:108
  20.0 0.0 copy-start.4
  20.0 0.0 collective-permute-done.refs_5_.refs_2_
  20.0 0.0 collective-permute-done.4.refs_3_
  20.0 0.0 collective-permute-done.3.refs_2_
  20.0 0.0 collective-permute-done.2.refs_1_
  20.0 0.0 collective-permute-done.1.refs_0_
  20.1 0.0 copy-start.1
  20.1 0.6 collective-permute-start.9
  20.6 0.7 collective-permute-start.5
  21.3 0.3 collective-permute-start.7
  21.6 0.0 copy-done.4
  21.6 0.0 collective-permute-start.8
  21.6 0.6 collective-permute-start.6
  22.2 12.6 %collective-permute-done.5.refs_0_ = bf16[16,128,128]{2,1,0:T(8,128)(2,1)S(1)} collective-permute-done((bf16[16,128,128]{2,1,0:T(8,128)(2,1)}, bf16[16,128,128]{2,1,0:T(8,128)(2,1)S(1)}, u32[]{:S(2)}, u32[]{:S(2)}) %collective-permute-start.5) | collective-permute-done | bytes 524320 | tf_op jit(solution)/shard_map/ppermute | solution.py:269
  34.8 0.6 collective-permute-done.7.refs_2_
  35.4 0.0 collective-permute-done.8.refs_3_
  35.4 0.8 collective-permute-done.6.refs_1_
  36.2 0.0 collective-permute-done.9.refs_4_
  36.2 0.8 copy-done.2
  37.0 0.1 broadcast_select_fusion.1.refs_8_
  37.0 0.6 collective-permute-start.11
  37.7 1.0 %collective-permute-start.10 = (bf16[16,128,128]{2,1,0:T(8,128)(2,1)S(1)}, bf16[16,128,128]{2,1,0:T(8,128)(2,1)S(1)}, u32[]{:S(2)}, u32[]{:S(2)}) collective-permute-start(bf16[16,128,128]{2,1,0:T(8,128)(2,1)S(1)} %broadcast_select_fusion.1.refs_8_), channel_id=1, source_target_pairs={{0,2},{1,3},{2,0},{3,1},{4,6},{5,7},{6,4},{7,5},{8,10},{9,11},{10,... | collective-permute-start | bytes 1572872 | tf_op jit(solution)/shard_map/ppermute | solution.py:269
  38.6 1.2 %collective-permute-start.12 = (bf16[16,128,128]{2,1,0:T(8,128)(2,1)}, bf16[16,128,128]{2,1,0:T(8,128)(2,1)}, u32[]{:S(2)}, u32[]{:S(2)}) collective-permute-start(bf16[16,128,128]{2,1,0:T(8,128)(2,1)} %get-tuple-element.51), channel_id=1, source_target_pairs={{0,8},{1,9},{2,10},{3,11},{4,12},{5,13},{6,14},{7,15},{8,0},{9,1},... | collective-permute-start | bytes 1572872 | tf_op jit(solution)/shard_map/ppermute | solution.py:269
  39.9 0.1 stack.67.refs_0_
  39.9 0.0 copy-done.1
  40.0 0.0 copy-start.5
  40.0 1.2 %copy-done.5 = f32[16,128,128]{2,1,0:T(8,128)S(1)} copy-done((f32[16,128,128]{2,1,0:T(8,128)S(1)}, f32[16,128,128]{2,1,0:T(8,128)}, u32[]{:S(2)}) %copy-start.5) | copy-done | bytes 1048600
  41.2 6.2 %hops_0.1 = (f32[16,128,128]{2,1,0:T(8,128)S(1)}, f32[16,128,128]{2,1,0:T(8,128)S(1)}, f32[8,128]{1,0:T(8,128)S(1)}, bf16[2,144,128,128]{3,2,1,0:T(8,128)(2,1)S(1)}) custom-call(s32[16]{0:T(128)S(1)} %stack.67.refs_0_, s32[256]{0:T(256)S(1)} %select_reduce_fusion.refs_1_, s32[256]{0:T(256)S(1)} %collective-permute-done.refs_5_.refs_2_, ...), custom_call_target="tpu_custom_call" | custom-call | flops 1 | bytes 1 | tf_op jit(solution)/shard_map/hops_0/pallas_call | solution.py:191
  47.4 3.3 %collective-permute-done.11.refs_1_ = bf16[16,128,128]{2,1,0:T(8,128)(2,1)S(1)} collective-permute-done((bf16[16,128,128]{2,1,0:T(8,128)(2,1)S(1)}, bf16[16,128,128]{2,1,0:T(8,128)(2,1)S(1)}, u32[]{:S(2)}, u32[]{:S(2)}) %collective-permute-start.11) | collective-permute-done | bytes 524320 | tf_op jit(solution)/shard_map/ppermute | solution.py:269
  50.7 0.3 collective-permute-done.10.refs_0_
  50.9 0.9 %collective-permute-done.12.refs_2_ = bf16[16,128,128]{2,1,0:T(8,128)(2,1)} collective-permute-done((bf16[16,128,128]{2,1,0:T(8,128)(2,1)}, bf16[16,128,128]{2,1,0:T(8,128)(2,1)}, u32[]{:S(2)}, u32[]{:S(2)}) %collective-permute-start.12) | collective-permute-done | bytes 524320 | tf_op jit(solution)/shard_map/ppermute | solution.py:269
  51.9 1.1 %broadcast_select_fusion.refs_11_ = bf16[16,128,128]{2,1,0:T(8,128)(2,1)S(1)} fusion(bf16[16,128,128]{2,1,0:T(8,128)(2,1)} %get-tuple-element.55, bf16[16,128,128]{2,1,0:T(8,128)(2,1)} %get-tuple-element.51, pred[]{:T(512)S(6)} %or.24), kind=kLoop, calls=%fused_computation | loop fusion | flops 262144 | bytes 1572865 | tf_op jit(solution)/shard_map/jit(_where)/select_n | solution.py:328
  53.0 1.6 %collective-permute-start.14 = (bf16[16,128,128]{2,1,0:T(8,128)(2,1)S(1)}, bf16[16,128,128]{2,1,0:T(8,128)(2,1)S(1)}, u32[]{:S(2)}, u32[]{:S(2)}) collective-permute-start(bf16[16,128,128]{2,1,0:T(8,128)(2,1)S(1)} %broadcast_select_fusion.refs_11_), channel_id=1, source_target_pairs={{0,4},{1,5},{2,6},{3,7},{4,0},{5,1},{6,2},{7,3},{8,12},{9,13},{10,... | collective-permute-start | bytes 1572872 | tf_op jit(solution)/shard_map/ppermute | solution.py:269
  54.6 1.1 %collective-permute-start.13 = (bf16[16,128,128]{2,1,0:T(8,128)(2,1)S(1)}, bf16[16,128,128]{2,1,0:T(8,128)(2,1)S(1)}, u32[]{:S(2)}, u32[]{:S(2)}) collective-permute-start(bf16[16,128,128]{2,1,0:T(8,128)(2,1)S(1)} %broadcast_select_fusion.refs_11_), channel_id=1, source_target_pairs={{0,2},{1,3},{2,0},{3,1},{4,6},{5,7},{6,4},{7,5},{8,10},{9,11},{10,... | collective-permute-start | bytes 1572872 | tf_op jit(solution)/shard_map/ppermute | solution.py:269
  55.6 0.9 collective-permute-start.15
  56.5 3.2 %hops_1.1 = (f32[16,128,128]{2,1,0:T(8,128)S(1)}, f32[16,128,128]{2,1,0:T(8,128)S(1)}, f32[8,128]{1,0:T(8,128)S(1)}) custom-call(s32[16]{0:T(128)S(1)} %stack.67.refs_0_, s32[256]{0:T(256)S(1)} %select_reduce_fusion.refs_1_, s32[256]{0:T(256)S(1)} %collective-permute-done.refs_5_.refs_2_, bf16[2,144,128,128]{3,2,1,0:T(8,128)(2,1)S(1)} %get-tuple-element.45.refs_3_, ...), custom_call_target="tpu_custom_call" | custom-call | flops 1 | bytes 1 | tf_op jit(solution)/shard_map/hops_1/pallas_call | solution.py:191
  59.7 5.3 %collective-permute-done.14.refs_1_ = bf16[16,128,128]{2,1,0:T(8,128)(2,1)S(1)} collective-permute-done((bf16[16,128,128]{2,1,0:T(8,128)(2,1)S(1)}, bf16[16,128,128]{2,1,0:T(8,128)(2,1)S(1)}, u32[]{:S(2)}, u32[]{:S(2)}) %collective-permute-start.14) | collective-permute-done | bytes 524320 | tf_op jit(solution)/shard_map/ppermute | solution.py:269
  65.0 1.3 %collective-permute-done.13.refs_0_ = bf16[16,128,128]{2,1,0:T(8,128)(2,1)S(1)} collective-permute-done((bf16[16,128,128]{2,1,0:T(8,128)(2,1)S(1)}, bf16[16,128,128]{2,1,0:T(8,128)(2,1)S(1)}, u32[]{:S(2)}, u32[]{:S(2)}) %collective-permute-start.13) | collective-permute-done | bytes 524320 | tf_op jit(solution)/shard_map/ppermute | solution.py:269
  66.3 0.9 collective-permute-done.15.refs_2_
  67.2 0.8 collective-permute-start.16
  68.0 0.3 collective-permute-start.18
  68.3 0.5 collective-permute-start.17
  68.8 2.4 %hops_2.1 = (f32[16,128,128]{2,1,0:T(8,128)S(1)}, f32[16,128,128]{2,1,0:T(8,128)S(1)}, f32[8,128]{1,0:T(8,128)}) custom-call(s32[16]{0:T(128)S(1)} %stack.67.refs_0_, s32[256]{0:T(256)S(1)} %select_reduce_fusion.refs_1_, s32[256]{0:T(256)S(1)} %collective-permute-done.refs_5_.refs_2_, bf16[2,144,128,128]{3,2,1,0:T(8,128)(2,1)S(1)} %get-tuple-element.45.refs_3_, ...), custom_call_target="tpu_custom_call" | custom-call | flops 1 | bytes 1 | tf_op jit(solution)/shard_map/hops_2/pallas_call | solution.py:191
  71.2 6.5 %collective-permute-done.16.refs_6_ = bf16[16,128,128]{2,1,0:T(8,128)(2,1)S(1)} collective-permute-done((bf16[16,128,128]{2,1,0:T(8,128)(2,1)S(1)}, bf16[16,128,128]{2,1,0:T(8,128)(2,1)S(1)}, u32[]{:S(2)}, u32[]{:S(2)}) %collective-permute-start.16) | collective-permute-done | bytes 524320 | tf_op jit(solution)/shard_map/ppermute | solution.py:269
  77.8 0.6 collective-permute-done.18.refs_8_
  78.4 0.0 collective-permute-done.17.refs_7_
  78.4 2.4 %hops_3.1 = (f32[16,128,128]{2,1,0:T(8,128)S(1)}, f32[16,128,128]{2,1,0:T(8,128)S(1)}, f32[32,128]{1,0:T(8,128)S(1)}) custom-call(s32[16]{0:T(128)S(1)} %stack.67.refs_0_, s32[256]{0:T(256)S(1)} %select_reduce_fusion.refs_1_, s32[256]{0:T(256)S(1)} %collective-permute-done.refs_5_.refs_2_, bf16[2,144,128,128]{3,2,1,0:T(8,128)(2,1)S(1)} %get-tuple-element.45.refs_3_, ...), custom_call_target="tpu_custom_call" | custom-call | flops 1 | bytes 1 | tf_op jit(solution)/shard_map/hops_3/pallas_call | solution.py:191
  80.8 0.1 collective-permute-start.19
  80.9 11.4 %all_to_all.11 = f32[32,1,128]{2,1,0:T(1,128)S(1)} all-to-all(f32[32,1,128]{2,1,0:T(1,128)S(1)} %bitcast.23), channel_id=1, replica_groups=mesh['groups'=1,'sector'=32] {'sector'}, dimensions={0} | all-to-all | bytes 32768 | tf_op jit(solution)/shard_map/all_to_all | solution.py:339
  92.3 0.0 collective-permute-done.19.theirs
  92.3 1.3 %finish.1 = (bf16[16,128,128]{2,1,0:T(8,128)(2,1)}, bf16[16,128,128]{2,1,0:T(8,128)(2,1)}, f32[1]{0:T(128)}) custom-call(f32[32,128]{1,0:T(8,128)S(1)} %bitcast.22, bf16[16,128,128]{2,1,0:T(8,128)(2,1)S(1)} %copy-done.1, f32[16,128,128]{2,1,0:T(8,128)S(1)} %get-tuple-element.69.mine, f32[16,128,128]{2,1,0:T(8,128)S(1)} %collective-permute-done.19.theirs), custom_call_target="tpu_custom_call" | custom-call | tf_op jit(solution)/shard_map/finish/pallas_call | solution.py:237
  (9 shorter events, 0.0 us)
Async XLA Ops:
  0.6 19.4 %collective-permute-start.4 = (bf16[16,128,128]{2,1,0:T(8,128)(2,1)}, bf16[16,128,128]{2,1,0:T(8,128)(2,1)S(1)}, u32[]{:S(2)}, u32[]{:S(2)}) collective-permute-start(bf16[16,128,128]{2,1,0:T(8,128)(2,1)} %psi.1), channel_id=1, source_target_pairs={{0,1},{1,0},{2,3},{3,2},{4,5},{5,4},{6,7},{7,6},{8,16},{9,17},{10,... | collective-permute-start | bytes 1572872 | tf_op jit(solution)/shard_map/ppermute | solution.py:276
  1.1 18.9 %collective-permute-start.3 = (bf16[16,128,128]{2,1,0:T(8,128)(2,1)}, bf16[16,128,128]{2,1,0:T(8,128)(2,1)}, u32[]{:S(2)}, u32[]{:S(2)}) collective-permute-start(bf16[16,128,128]{2,1,0:T(8,128)(2,1)} %psi.1), channel_id=1, source_target_pairs={{0,8},{1,9},{2,10},{3,11},{4,12},{5,13},{6,14},{7,15},{8,0},{9,1},... | collective-permute-start | bytes 1572872 | tf_op jit(solution)/shard_map/ppermute | solution.py:269
  5.3 14.7 %collective-permute-start.2 = (bf16[16,128,128]{2,1,0:T(8,128)(2,1)}, bf16[16,128,128]{2,1,0:T(8,128)(2,1)}, u32[]{:S(2)}, u32[]{:S(2)}) collective-permute-start(bf16[16,128,128]{2,1,0:T(8,128)(2,1)} %psi.1), channel_id=1, source_target_pairs={{0,4},{1,5},{2,6},{3,7},{4,0},{5,1},{6,2},{7,3},{8,12},{9,13},{10,... | collective-permute-start | bytes 1572872 | tf_op jit(solution)/shard_map/ppermute | solution.py:269
  6.8 13.2 %collective-permute-start.1 = (bf16[16,128,128]{2,1,0:T(8,128)(2,1)}, bf16[16,128,128]{2,1,0:T(8,128)(2,1)S(1)}, u32[]{:S(2)}, u32[]{:S(2)}) collective-permute-start(bf16[16,128,128]{2,1,0:T(8,128)(2,1)} %psi.1), channel_id=1, source_target_pairs={{0,2},{1,3},{2,0},{3,1},{4,6},{5,7},{6,4},{7,5},{8,10},{9,11},{10,... | collective-permute-start | bytes 1572872 | tf_op jit(solution)/shard_map/ppermute | solution.py:269
  10.2 9.8 %collective-permute-start = (s32[256]{0:T(256)S(1)}, s32[256]{0:T(256)S(1)}, u32[]{:S(2)}, u32[]{:S(2)}) collective-permute-start(s32[256]{0:T(256)S(1)} %select_reduce_fusion.refs_1_), channel_id=1, source_target_pairs={{0,1},{1,0},{2,3},{3,2},{4,5},{5,4},{6,7},{7,6},{8,9},{9,8},{10,11... | collective-permute-start | bytes 3080 | tf_op jit(solution)/shard_map/ppermute | solution.py:269
  10.3 1.0 %copy-start = (bf16[16,128,128]{2,1,0:T(8,128)(2,1)S(1)}, bf16[16,128,128]{2,1,0:T(8,128)(2,1)}, u32[]{:S(2)}) copy-start(bf16[16,128,128]{2,1,0:T(8,128)(2,1)} %psi.1) | copy-start | bytes 1572868
  11.3 0.7 copy-start.6
  20.0 1.7 %copy-start.4 = (f32[16,128,128]{2,1,0:T(8,128)}, f32[16,128,128]{2,1,0:T(8,128)S(1)}, u32[]{:S(2)}) copy-start(f32[16,128,128]{2,1,0:T(8,128)S(1)} %get-tuple-element.43.refs_5_) | copy-start | bytes 3145732
  20.1 19.9 %copy-start.1 = (bf16[16,128,128]{2,1,0:T(8,128)(2,1)S(1)}, bf16[16,128,128]{2,1,0:T(8,128)(2,1)}, u32[]{:S(2)}) copy-start(bf16[16,128,128]{2,1,0:T(8,128)(2,1)} %psi.1) | copy-start | bytes 1572868
  20.1 16.1 %collective-permute-start.9 = (bf16[144,128,128]{2,1,0:T(8,128)(2,1)}, bf16[144,128,128]{2,1,0:T(8,128)(2,1)}, u32[]{:S(2)}, u32[]{:S(2)}) collective-permute-start(bf16[144,128,128]{2,1,0:T(8,128)(2,1)} %get-tuple-element.38.refs_3_), channel_id=1, source_target_pairs={{0,1},{1,0},{2,3},{3,2},{4,5},{5,4},{6,7},{7,6},{8,9},{9,8},{10,11... | collective-permute-start | bytes 14155784 | tf_op jit(solution)/shard_map/ppermute | solution.py:269
  20.6 14.1 %collective-permute-start.5 = (bf16[16,128,128]{2,1,0:T(8,128)(2,1)}, bf16[16,128,128]{2,1,0:T(8,128)(2,1)S(1)}, u32[]{:S(2)}, u32[]{:S(2)}) collective-permute-start(bf16[16,128,128]{2,1,0:T(8,128)(2,1)} %get-tuple-element.39.refs_8_), channel_id=1, source_target_pairs={{0,2},{1,3},{2,0},{3,1},{4,6},{5,7},{6,4},{7,5},{8,10},{9,11},{10,... | collective-permute-start | bytes 1572872 | tf_op jit(solution)/shard_map/ppermute | solution.py:269
  21.3 14.1 %collective-permute-start.7 = (bf16[16,128,128]{2,1,0:T(8,128)(2,1)S(1)}, bf16[16,128,128]{2,1,0:T(8,128)(2,1)S(1)}, u32[]{:S(2)}, u32[]{:S(2)}) collective-permute-start(bf16[16,128,128]{2,1,0:T(8,128)(2,1)S(1)} %get-tuple-element.41), channel_id=1, source_target_pairs={{0,8},{1,9},{2,10},{3,11},{4,12},{5,13},{6,14},{7,15},{8,0},{9,1},... | collective-permute-start | bytes 1572872 | tf_op jit(solution)/shard_map/ppermute | solution.py:269
  21.6 13.8 %collective-permute-start.8 = (bf16[16,128,128]{2,1,0:T(8,128)(2,1)}, bf16[16,128,128]{2,1,0:T(8,128)(2,1)}, u32[]{:S(2)}, u32[]{:S(2)}) collective-permute-start(bf16[16,128,128]{2,1,0:T(8,128)(2,1)} %get-tuple-element.40.refs_9_), channel_id=1, source_target_pairs={{0,1},{1,0},{2,3},{3,2},{4,5},{5,4},{6,7},{7,6},{8,16},{9,17},{10,... | collective-permute-start | bytes 1572872 | tf_op jit(solution)/shard_map/ppermute | solution.py:276
  21.6 14.5 %collective-permute-start.6 = (bf16[16,128,128]{2,1,0:T(8,128)(2,1)}, bf16[16,128,128]{2,1,0:T(8,128)(2,1)S(1)}, u32[]{:S(2)}, u32[]{:S(2)}) collective-permute-start(bf16[16,128,128]{2,1,0:T(8,128)(2,1)} %get-tuple-element.40.refs_9_), channel_id=1, source_target_pairs={{0,4},{1,5},{2,6},{3,7},{4,0},{5,1},{6,2},{7,3},{8,12},{9,13},{10,... | collective-permute-start | bytes 1572872 | tf_op jit(solution)/shard_map/ppermute | solution.py:269
  36.2 0.8 copy-start.2
  37.0 13.6 %collective-permute-start.11 = (bf16[16,128,128]{2,1,0:T(8,128)(2,1)S(1)}, bf16[16,128,128]{2,1,0:T(8,128)(2,1)S(1)}, u32[]{:S(2)}, u32[]{:S(2)}) collective-permute-start(bf16[16,128,128]{2,1,0:T(8,128)(2,1)S(1)} %broadcast_select_fusion.1.refs_8_), channel_id=1, source_target_pairs={{0,4},{1,5},{2,6},{3,7},{4,0},{5,1},{6,2},{7,3},{8,12},{9,13},{10,... | collective-permute-start | bytes 1572872 | tf_op jit(solution)/shard_map/ppermute | solution.py:269
  37.7 13.3 %collective-permute-start.10 = (bf16[16,128,128]{2,1,0:T(8,128)(2,1)S(1)}, bf16[16,128,128]{2,1,0:T(8,128)(2,1)S(1)}, u32[]{:S(2)}, u32[]{:S(2)}) collective-permute-start(bf16[16,128,128]{2,1,0:T(8,128)(2,1)S(1)} %broadcast_select_fusion.1.refs_8_), channel_id=1, source_target_pairs={{0,2},{1,3},{2,0},{3,1},{4,6},{5,7},{6,4},{7,5},{8,10},{9,11},{10,... | collective-permute-start | bytes 1572872 | tf_op jit(solution)/shard_map/ppermute | solution.py:269
  38.6 13.2 %collective-permute-start.12 = (bf16[16,128,128]{2,1,0:T(8,128)(2,1)}, bf16[16,128,128]{2,1,0:T(8,128)(2,1)}, u32[]{:S(2)}, u32[]{:S(2)}) collective-permute-start(bf16[16,128,128]{2,1,0:T(8,128)(2,1)} %get-tuple-element.51), channel_id=1, source_target_pairs={{0,8},{1,9},{2,10},{3,11},{4,12},{5,13},{6,14},{7,15},{8,0},{9,1},... | collective-permute-start | bytes 1572872 | tf_op jit(solution)/shard_map/ppermute | solution.py:269
  40.0 1.2 %copy-start.5 = (f32[16,128,128]{2,1,0:T(8,128)S(1)}, f32[16,128,128]{2,1,0:T(8,128)}, u32[]{:S(2)}) copy-start(f32[16,128,128]{2,1,0:T(8,128)} %copy-done.4) | copy-start | bytes 3145732
  41.2 15.3 %copy-start.3 = (bf16[16,128,128]{2,1,0:T(8,128)(2,1)S(1)}, bf16[16,128,128]{2,1,0:T(8,128)(2,1)}, u32[]{:S(2)}) copy-start(bf16[16,128,128]{2,1,0:T(8,128)(2,1)} %copy-done.2) | copy-start | bytes 1572868
  53.0 12.1 %collective-permute-start.14 = (bf16[16,128,128]{2,1,0:T(8,128)(2,1)S(1)}, bf16[16,128,128]{2,1,0:T(8,128)(2,1)S(1)}, u32[]{:S(2)}, u32[]{:S(2)}) collective-permute-start(bf16[16,128,128]{2,1,0:T(8,128)(2,1)S(1)} %broadcast_select_fusion.refs_11_), channel_id=1, source_target_pairs={{0,4},{1,5},{2,6},{3,7},{4,0},{5,1},{6,2},{7,3},{8,12},{9,13},{10,... | collective-permute-start | bytes 1572872 | tf_op jit(solution)/shard_map/ppermute | solution.py:269
  54.6 11.7 %collective-permute-start.13 = (bf16[16,128,128]{2,1,0:T(8,128)(2,1)S(1)}, bf16[16,128,128]{2,1,0:T(8,128)(2,1)S(1)}, u32[]{:S(2)}, u32[]{:S(2)}) collective-permute-start(bf16[16,128,128]{2,1,0:T(8,128)(2,1)S(1)} %broadcast_select_fusion.refs_11_), channel_id=1, source_target_pairs={{0,2},{1,3},{2,0},{3,1},{4,6},{5,7},{6,4},{7,5},{8,10},{9,11},{10,... | collective-permute-start | bytes 1572872 | tf_op jit(solution)/shard_map/ppermute | solution.py:269
  55.6 11.6 %collective-permute-start.15 = (bf16[16,128,128]{2,1,0:T(8,128)(2,1)S(1)}, bf16[16,128,128]{2,1,0:T(8,128)(2,1)S(1)}, u32[]{:S(2)}, u32[]{:S(2)}) collective-permute-start(bf16[16,128,128]{2,1,0:T(8,128)(2,1)S(1)} %get-tuple-element.58), channel_id=1, source_target_pairs={{0,8},{1,9},{2,10},{3,11},{4,12},{5,13},{6,14},{7,15},{8,0},{9,1},... | collective-permute-start | bytes 1572872 | tf_op jit(solution)/shard_map/ppermute | solution.py:269
  67.2 10.5 %collective-permute-start.16 = (bf16[16,128,128]{2,1,0:T(8,128)(2,1)S(1)}, bf16[16,128,128]{2,1,0:T(8,128)(2,1)S(1)}, u32[]{:S(2)}, u32[]{:S(2)}) collective-permute-start(bf16[16,128,128]{2,1,0:T(8,128)(2,1)S(1)} %get-tuple-element.65), channel_id=1, source_target_pairs={{0,2},{1,3},{2,0},{3,1},{4,6},{5,7},{6,4},{7,5},{8,10},{9,11},{10,... | collective-permute-start | bytes 1572872 | tf_op jit(solution)/shard_map/ppermute | solution.py:269
  68.0 10.4 %collective-permute-start.18 = (bf16[16,128,128]{2,1,0:T(8,128)(2,1)S(1)}, bf16[16,128,128]{2,1,0:T(8,128)(2,1)S(1)}, u32[]{:S(2)}, u32[]{:S(2)}) collective-permute-start(bf16[16,128,128]{2,1,0:T(8,128)(2,1)S(1)} %get-tuple-element.66), channel_id=1, source_target_pairs={{0,8},{1,9},{2,10},{3,11},{4,12},{5,13},{6,14},{7,15},{8,0},{9,1},... | collective-permute-start | bytes 1572872 | tf_op jit(solution)/shard_map/ppermute | solution.py:269
  68.3 10.1 %collective-permute-start.17 = (bf16[16,128,128]{2,1,0:T(8,128)(2,1)S(1)}, bf16[16,128,128]{2,1,0:T(8,128)(2,1)S(1)}, u32[]{:S(2)}, u32[]{:S(2)}) collective-permute-start(bf16[16,128,128]{2,1,0:T(8,128)(2,1)S(1)} %get-tuple-element.60.refs_6_), channel_id=1, source_target_pairs={{0,4},{1,5},{2,6},{3,7},{4,0},{5,1},{6,2},{7,3},{8,12},{9,13},{10,... | collective-permute-start | bytes 1572872 | tf_op jit(solution)/shard_map/ppermute | solution.py:269
  80.8 11.5 %collective-permute-start.19 = (f32[16,128,128]{2,1,0:T(8,128)S(1)}, f32[16,128,128]{2,1,0:T(8,128)S(1)}, u32[]{:S(2)}, u32[]{:S(2)}) collective-permute-start(f32[16,128,128]{2,1,0:T(8,128)S(1)} %get-tuple-element.70), channel_id=1, source_target_pairs={{0,1},{1,0},{2,3},{3,2},{4,5},{5,4},{6,7},{7,6},{8,9},{9,8},{10,11... | collective-permute-start | bytes 3145736 | tf_op jit(solution)/shard_map/ppermute | solution.py:269

commit v4 on v3

--- a/solution.py
+++ b/solution.py
@@ -10,7 +10,7 @@
 F32 = jnp.float32
 BF16 = jnp.bfloat16
 VMEM_BYTES = 16 * 1024 * 1024
-LOCAL_BYTES = 50 * 1024 * 1024
+LOCAL_BYTES = 51 * 1024 * 1024
 COST = pl.CostEstimate(flops=1, bytes_accessed=1, transcendentals=0)
 ANY = pl.BlockSpec(memory_space=pl.ANY)
 VMEM = pl.BlockSpec(memory_space=pltpu.VMEM)
@@ -59,20 +59,19 @@
     return hpsi.astype(BF16), residual, quotient.reshape(1)
 
 
-def local_kernel(onsite, psi, right, left, acc, square, moved, onsite_buf, psi_buf, r_buf, l_buf, middle, sems, moved_sems):
+def local_kernel(psi, right, left, acc, square, moved, psi_buf, r_buf, l_buf, middle, sems, moved_sems):
     rows, cols, size = psi.shape[0], psi.shape[1], psi.shape[2]
     chans = r_buf.shape[1]
     hops = right.shape[1] - chans
-    copies = [pltpu.make_async_copy(psi, psi_buf, sems.at[0, 0]), pltpu.make_async_copy(onsite, onsite_buf, sems.at[0, 1])]
+    psi_copy = pltpu.make_async_copy(psi, psi_buf, sems.at[0, 0])
     r_copy = [pltpu.make_async_copy(right.at[j, pl.ds(0, chans)], r_buf.at[j], sems.at[1, j]) for j in range(cols)]
     l_copy = [pltpu.make_async_copy(left.at[i, pl.ds(0, chans)], l_buf.at[i], sems.at[2, i]) for i in range(rows)]
     parts = [right.at[j, pl.ds(chans, hops)] for j in range(cols)] + [left.at[i, pl.ds(chans, hops)] for i in range(rows)]
     for n, part in enumerate(parts):
         parts[n] = pltpu.make_async_copy(part, moved.at[pl.ds(n * hops, hops)], moved_sems.at[n])
-    for copy in copies + r_copy + l_copy:
+    for copy in [psi_copy] + r_copy + l_copy:
         copy.start()
-    for copy in copies:
-        copy.wait()
+    psi_copy.wait()
     for j in range(cols):
         r_copy[j].wait()
         if j == 1:
@@ -95,14 +94,14 @@
         for j in range(cols):
             moved[first + i * cols + j] = psi_buf[i, j]
             block = psi_buf[i, j].astype(F32)
-            acc[i * cols + j] = summed[:, j * size : (j + 1) * size] + onsite_buf[i * cols + j] * block
+            acc[i * cols + j] = summed[:, j * size : (j + 1) * size]
             total += block * block
     square[...] = total
     for part in parts:
         part.wait()
 
 
-def local_call(onsite, psi, right, left, hops):
+def local_call(psi, right, left, hops):
     sec, size = psi.shape[:2]
     rows, cols, chans = left.shape[0], right.shape[0], left.shape[1] - hops
     return pl.pallas_call(
@@ -112,10 +111,9 @@
             jax.ShapeDtypeStruct((size, size), F32),
             jax.ShapeDtypeStruct(((rows + cols) * hops + sec, size, size), BF16),
         ),
-        in_specs=[HBM] * 4,
+        in_specs=[HBM] * 3,
         out_specs=[VMEM] * 3,
         scratch_shapes=[
-            pltpu.SMEM((sec,), F32),
             pltpu.VMEM((rows, cols, size, size), BF16),
             pltpu.VMEM((cols, chans, size, size), BF16),
             pltpu.VMEM((rows, chans, size, size), BF16),
@@ -126,52 +124,48 @@
         compiler_params=pltpu.CompilerParams(vmem_limit_bytes=LOCAL_BYTES),
         cost_estimate=COST,
         name="local_channels",
-    )(onsite, psi.reshape(rows, cols, size, size), right, left)
-
-
-def hop_kernel(base, count, first, last, capacity, *refs):
+    )(psi.reshape(rows, cols, size, size), right, left)
+
+
+def hop_kernel(base, count, first, diagonal, last, capacity, *refs):
     refs = list(refs)
     take = lambda n: [refs.pop(0) for _ in range(n)]
     order, *terms = take(3)
     envs = take(2 if first else 1)
     acc_in = take(1 if first else 2)
     bufs = take(count)
+    onsite = take(1)[0] if diagonal else None
     square = take(1)[0] if last else None
     acc = take(2)
     sums = take(1)[0]
     env = take(1)[0] if first else envs[0]
-    psi, sems, env_sems = refs
-    copies = [pltpu.make_async_copy(buf, psi.at[s], sems.at[s]) for s, buf in enumerate(bufs)]
-    fills = [pltpu.make_async_copy(envs[e], env.at[e], env_sems.at[e]) for e in range(2)] if first else []
-    for copy in copies + fills:
-        copy.start()
+    (sems,) = refs
+    fills = [pltpu.make_async_copy(envs[e], env.at[e], sems.at[e]) for e in range(2)] if first else []
     if first:
-        copies.append(pltpu.make_async_copy(acc_in[0], acc[0], env_sems.at[2]))
-        copies[-1].start()
+        fills.append(pltpu.make_async_copy(acc_in[0], acc[0], sems.at[2]))
+        for fill in fills:
+            fill.start()
         acc[1][...] = jnp.zeros(acc[1].shape, F32)
     else:
         for e in range(2):
             acc[e][...] = acc_in[e][...]
-    for copy in copies:
-        copy.wait()
     for fill in fills:
         fill.wait()
-
-    def owner_step(s, carry):
+    sec = acc[0].shape[0]
+    first_psi = env.shape[1] - sec
+    if diagonal:
+        for t in range(sec):
+            acc[0][t] = acc[0][t] + onsite[t] * env[0, first_psi + t].astype(F32)
+    for s, psi in enumerate(bufs):
         slot = order[base + s] * capacity
         words = [(e, terms[e][slot + r]) for e in range(2) for r in range(capacity)]
-        mids = [dot(psi[s, w & 255], env[e, (w >> 16) & 255]).astype(BF16) for e, w in words]
+        mids = [dot(psi[w & 255], env[e, (w >> 16) & 255]).astype(BF16) for e, w in words]
         parts = [dot(env[e, w >> 24], mid) for (e, w), mid in zip(words, mids)]
         for (e, w), part in zip(words, parts):
             t = (w >> 8) & 255
             acc[e][t] = acc[e][t] + part
-        return carry
-
-    lax.fori_loop(0, count, owner_step, 0, unroll=2)
     if last:
         total = jnp.zeros(acc[0].shape[1:], F32)
-        sec = acc[0].shape[0]
-        first_psi = env.shape[1] - sec
         for e in range(2):
             total = lax.fori_loop(0, sec, lambda t, v, e=e: v + env[e, first_psi + t].astype(F32) * acc[e][t], total)
         lanes = lax.broadcasted_iota(jnp.int32, sums.shape, 1)
@@ -180,7 +174,7 @@
         sums[...] = jnp.zeros(sums.shape, F32)
 
 
-def hop_call(name, order, base, terms, envs, accs, bufs, last_args, owners, capacity):
+def hop_call(name, order, base, terms, envs, accs, bufs, onsite, last_args, owners, capacity):
     sec, size = accs[0].shape[:2]
     first, last = len(accs) == 1, bool(last_args)
     count = len(bufs)
@@ -189,36 +183,51 @@
     if first:
         out_shape.append(jax.ShapeDtypeStruct((2,) + envs[0].shape, BF16))
     return pl.pallas_call(
-        functools.partial(hop_kernel, base, count, first, last, capacity),
+        functools.partial(hop_kernel, base, count, first, bool(onsite), last, capacity),
         out_shape=out_shape,
         in_specs=[SMEM] * 3
         + [ANY if first else VMEM] * (len(envs) + len(accs))
-        + [ANY] * count
+        + [VMEM] * count
+        + [SMEM] * len(onsite)
         + [VMEM] * len(last_args),
         out_specs=[VMEM] * len(out_shape),
-        scratch_shapes=[
-            pltpu.VMEM((count, sec, size, size), BF16),
-            pltpu.SemaphoreType.DMA((count,)),
-            pltpu.SemaphoreType.DMA((3,)),
-        ],
+        scratch_shapes=[pltpu.SemaphoreType.DMA((3,))],
         compiler_params=pltpu.CompilerParams(vmem_limit_bytes=VMEM_BYTES),
         cost_estimate=COST,
         name=name,
-    )(order, *terms, *envs, *accs, *bufs, *last_args)
-
-
-def hold_until(values, tokens):
+    )(order, *terms, *envs, *accs, *bufs, *onsite, *last_args)
+
+
+def hold_kernel(count, move, *refs):
+    if move:
+        src, dst = move
+        flag, values, sem = refs[-count - 2], refs[: -count - 2], refs[-1]
+
+        @pl.when(flag[0] != 0)
+        def _():
+            step = values[src].shape[0] // 4
+            copies = []
+            for n in range(4):
+                part = pl.ds(n * step, step)
+                copies.append(pltpu.make_async_copy(values[src].at[part], refs[dst - count - 1].at[part], sem.at[n]))
+                copies[-1].start()
+            for copy in copies:
+                copy.wait()
+
+
+def hold_until(values, tokens, move=None, flag=None):
     count = len(values)
     return pl.pallas_call(
-        lambda *refs: None,
+        functools.partial(hold_kernel, count, move),
         out_shape=[jax.ShapeDtypeStruct(value.shape, value.dtype) for value in values],
-        in_specs=[ANY] * (count + len(tokens)),
+        in_specs=[ANY] * (count + len(tokens)) + ([SMEM] if move else []),
         out_specs=[ANY] * count,
+        scratch_shapes=[pltpu.SemaphoreType.DMA((4,))],
         input_output_aliases={n: n for n in range(count)},
         compiler_params=pltpu.CompilerParams(vmem_limit_bytes=VMEM_BYTES),
         cost_estimate=COST,
         name="hold",
-    )(*values, *tokens)
+    )(*values, *tokens, *([flag] if move else []))
 
 
 def finish_kernel(sums, psi, mine, theirs, applied, residual, quotient):
@@ -276,26 +285,26 @@
         return lax.ppermute(value, "sector", pairs)
 
     me = lax.axis_index("sector")
-    outer = (me < z) | (me >= owners - z)
-    layer_masks = [0, z, jnp.where(outer, 2 * z, 3 * z), jnp.where(outer, 3 * z, 2 * z)]
+    outer = ((me < z) | (me >= owners - z)).astype(jnp.int32).reshape(1)
+    layer_masks = [0, z, 3 * z - outer * z, 2 * z + outer * z]
     groups = [
-        [(0, 0), (0, x), (0, y), (1, 0)],
-        [(0, xy), (1, y), (2, 0), (2, x), (2, y), (3, 0)],
-        [(3, x), (3, y), (1, x)],
-        [(2, xy), (3, xy), (1, xy)],
+        [(0, 0), (0, x), (0, y), (1, 0), (0, xy), (1, y)],
+        [(2, 0), (2, x), (2, y), (3, 0)],
+        [(1, x), (3, y), (3, x)],
+        [(1, xy), (3, xy), (2, xy)],
     ]
-    order = jnp.stack([me ^ layer_masks[b] ^ bits for group in groups for b, bits in group])
+    order = jnp.concatenate([me ^ layer_masks[b] ^ jnp.full((1,), bits) for group in groups for b, bits in group])
 
     held = {(0, 0): wavefunction}
     state = {"base": 0}
 
-    def hold(keys, *tokens):
-        held.update(zip(keys, hold_until([held[key] for key in keys], tokens)))
-
-    def run(group, last_args=()):
+    def hold(keys, *tokens, **move):
+        held.update(zip(keys, hold_until([held[key] for key in keys], tokens, **move)))
+
+    def run(group, onsite=(), last_args=()):
         out = hop_call(
             f"hops_{group}", order, state["base"], terms, state["envs"], state["accs"],
-            tuple(held[key] for key in groups[group]), last_args, owners, capacity,
+            tuple(held[key] for key in groups[group]), onsite, last_args, owners, capacity,
         )
         state["accs"] = out[:2]
         if group == 0:
@@ -308,34 +317,34 @@
     held["middle"] = swap_middle(wavefunction)
     terms = term_words(source_device, source_block, right_env.shape[0], capacity)
     terms = (terms, swap(terms, core))
-    acc, square, held["env"] = local_call(onsite_energy, wavefunction, right_env, left_env, hops)
-    hold([(0, x), (0, y), (1, 0), "middle", "env"], terms[1])
+    acc, square, held["env"] = local_call(wavefunction, right_env, left_env, hops)
+    hold([(0, x), (0, y), "middle", (1, 0), "env"], terms[1])
 
     held[0, xy] = swap(held[0, y], x)
     held[1, y] = swap(held[1, 0], y)
     held["outer"] = swap(held["middle"], z)
     held["middle_2"] = swap_middle(held[1, 0])
     held["env_sib"] = swap(held["env"], core)
-    hold([(0, xy), (1, y), "outer", "middle_2", "env_sib"])
-
-    held[2, 0] = jnp.where(outer, held["outer"], held["middle"])
+    hold(["env_sib", "middle", "middle_2", (1, y), (0, xy)], held["outer"], move=(5, 1), flag=outer)
+
+    held[2, 0] = held["middle"]
     held[2, x], held[2, y] = swap(held[2, 0], x), swap(held[2, 0], y)
     held["outer_2"] = swap(held["middle_2"], z)
     state["accs"], state["envs"] = (acc,), (held["env"], held["env_sib"])
     done = run(0)
-    hold([(2, x), (2, y), "outer_2", (0, x)], done)
-
-    held[3, 0] = jnp.where(outer, held["outer_2"], held["middle_2"])
+    hold(["middle_2", (0, x), (2, y), (2, x)], held["outer_2"], done, move=(4, 0), flag=outer)
+
+    held[3, 0] = held["middle_2"]
     held[3, x], held[3, y] = swap(held[3, 0], x), swap(held[3, 0], y)
     held[1, x] = swap(held[0, x], z)
-    done = run(1)
-    hold([(3, x), (3, y), (1, x), (2, y), (0, xy)], done)
+    done = run(1, (onsite_energy,))
+    hold([(1, x), (2, y), (0, xy), (3, y), (3, x)], done)
 
     held[2, xy] = swap(held[2, y], x)
     held[3, xy] = swap(held[3, x], y)
     held[1, xy] = swap(held[0, xy], z)
     run(2)
-    sums = run(3, (square,))
+    sums = run(3, (), (square,))
     sums = lax.all_to_all(sums, "sector", 0, 0, tiled=True)
     mine, theirs = state["accs"]
     return finish_call(sums, wavefunction, mine, swap(theirs, core))

time: 94 us -> 91.5 us (0.973)
  blocking collectives: 11.4 us -> 8.88 us
  Pallas kernels: 23.6 us -> 25.9 us
  other arithmetic: 1.47 us -> 0.31 us
    all_to_all x1, blocking collectives: 11.4 us -> 8.88 us  [spread_everywhere(): sums = lax.all_to_all(sums, 'sector', 0, 0, tiled=True)]
    pallas_call x8, Pallas kernels: 14.3 us -> 16.6 us  [the longest x4 14.2 us: hop_call(): pl.pallas_call(functools.partial(hop_kernel, base, count, first, bool(ons...]
    select_n x2 -> x0, other arithmetic: 1.16 us -> none  [the longest x1 1.1 us: spread_everywhere(): held[3, 0] = jnp.where(outer, held['outer_2'], held['middle_2'])]
  transfers between devices with their start and end apart: 20 -> 20, of which waited for: 11 -> 14; matrix products, arithmetic and copies ran while one was open for 2% -> 2% of each run, Pallas kernels for 21% -> 22%
where the time goes in v4:
time: 91.5 us; the launch traced here: 91.1 us
  waiting for transfers between devices  33 us (36%)
  Pallas kernels  25.9 us (28%)
  starting transfers between devices  17.2 us (19%)
  blocking collectives  8.88 us (10%)
  local copies, waits for them, and re-layouts  4.96 us (5%)
    ppermute x18, waiting for transfers between devices, swap(): return lax.ppermute(value, 'sector', [(i, i ^ mask) for i in range(owners)])  33 us
    ppermute x18, starting transfers between devices, swap(): return lax.ppermute(value, 'sector', [(i, i ^ mask) for i in range(owners)])  17.2 us
    pallas_call x4, Pallas kernels, hop_call(): pl.pallas_call(functools.partial(hop_kernel, base, count, first, bool(ons...  14.2 us
    all_to_all x1, blocking collectives, spread_everywhere(): sums = lax.all_to_all(sums, 'sector', 0, 0, tiled=True)  8.88 us
    pallas_call x1, Pallas kernels, local_call(): pl.pallas_call(local_kernel, out_shape=(jax.ShapeDtypeStruct((sec, size,...  8.05 us
    unnamed x14, local copies, waits for them, and re-layouts  3.32 us
    pallas_call x4, Pallas kernels, hold_until(): pl.pallas_call(functools.partial(hold_kernel, count, move), out_shape=[ja...  2.33 us
  transfers between devices with their start and end apart: 20, of which 14 were waited for; matrix products, arithmetic and copies ran while one was open for 2% of the time, Pallas kernels for 22%

profile of v4, /device:TPU:0, one launch (start us, length us, event | category | flops | bytes accessed | tf_op | source)
XLA Modules:
  0.0 91.1 jit_solution(257825461094734142)
XLA Ops:
  0.6 3.1 %collective-permute-start.4 = (bf16[16,128,128]{2,1,0:T(8,128)(2,1)}, bf16[16,128,128]{2,1,0:T(8,128)(2,1)S(1)}, u32[]{:S(2)}, u32[]{:S(2)}) collective-permute-start(bf16[16,128,128]{2,1,0:T(8,128)(2,1)} %psi.1), channel_id=1, source_target_pairs={{0,8},{1,9},{2,10},{3,11},{4,12},{5,13},{6,14},{7,15},{8,0},{9,1},... | collective-permute-start | bytes 1572872 | tf_op jit(solution)/shard_map/ppermute | solution.py:278
  3.7 0.0 collective-permute-start.3
  3.7 1.5 %collective-permute-start.2 = (bf16[16,128,128]{2,1,0:T(8,128)(2,1)}, bf16[16,128,128]{2,1,0:T(8,128)(2,1)}, u32[]{:S(2)}, u32[]{:S(2)}) collective-permute-start(bf16[16,128,128]{2,1,0:T(8,128)(2,1)} %psi.1), channel_id=1, source_target_pairs={{0,4},{1,5},{2,6},{3,7},{4,0},{5,1},{6,2},{7,3},{8,12},{9,13},{10,... | collective-permute-start | bytes 1572872 | tf_op jit(solution)/shard_map/ppermute | solution.py:278
  5.2 1.5 %collective-permute-start.1 = (bf16[16,128,128]{2,1,0:T(8,128)(2,1)}, bf16[16,128,128]{2,1,0:T(8,128)(2,1)S(1)}, u32[]{:S(2)}, u32[]{:S(2)}) collective-permute-start(bf16[16,128,128]{2,1,0:T(8,128)(2,1)} %psi.1), channel_id=1, source_target_pairs={{0,2},{1,3},{2,0},{3,1},{4,6},{5,7},{6,4},{7,5},{8,10},{9,11},{10,... | collective-permute-start | bytes 1572872 | tf_op jit(solution)/shard_map/ppermute | solution.py:278
  6.7 0.8 reshape.95
  7.5 0.8 reshape.96
  8.3 0.2 convert_reduce_fusion
  8.5 0.1 select_reduce_fusion.refs_1_
  8.6 0.1 collective-permute-start
  8.7 0.0 copy-start
  8.7 1.0 %copy-done = bf16[16,128,128]{2,1,0:T(8,128)(2,1)S(1)} copy-done((bf16[16,128,128]{2,1,0:T(8,128)(2,1)S(1)}, bf16[16,128,128]{2,1,0:T(8,128)(2,1)}, u32[]{:S(2)}) %copy-start) | copy-done | bytes 524312
  9.7 8.0 %local_channels.1 = (f32[16,128,128]{2,1,0:T(8,128)S(1)}, f32[128,128]{1,0:T(8,128)S(1)}, bf16[144,128,128]{2,1,0:T(8,128)(2,1)}) custom-call(bf16[4,4,128,128]{3,2,1,0:T(8,128)(2,1)S(1)} %bitcast.10, bf16[4,32,128,128]{3,2,1,0:T(8,128)(2,1)} %right.1, bf16[4,32,128,128]{3,2,1,0:T(8,128)(2,1)} %left.1), custom_call_target="tpu_custom_call" | custom-call | flops 1 | bytes 1 | tf_op jit(solution)/shard_map/local_channels/pallas_call | solution.py:107
  17.8 0.0 copy-start.4
  17.8 0.0 collective-permute-done.refs_5_.refs_2_
  17.8 0.0 collective-permute-done.4.refs_3_
  17.8 0.0 collective-permute-done.3.refs_2_
  17.8 0.5 collective-permute-done.2.refs_1_
  18.4 1.1 %collective-permute-done.1.refs_0_ = bf16[16,128,128]{2,1,0:T(8,128)(2,1)S(1)} collective-permute-done((bf16[16,128,128]{2,1,0:T(8,128)(2,1)}, bf16[16,128,128]{2,1,0:T(8,128)(2,1)S(1)}, u32[]{:S(2)}, u32[]{:S(2)}) %collective-permute-start.1) | collective-permute-done | bytes 524320 | tf_op jit(solution)/shard_map/ppermute | solution.py:278
  19.6 0.0 copy-start.2
  19.6 0.0 copy-start.1
  19.6 0.1 collective-permute-start.5
  19.7 2.0 %collective-permute-start.9 = (bf16[16,128,128]{2,1,0:T(8,128)(2,1)S(1)}, bf16[16,128,128]{2,1,0:T(8,128)(2,1)}, u32[]{:S(2)}, u32[]{:S(2)}) collective-permute-start(bf16[16,128,128]{2,1,0:T(8,128)(2,1)S(1)} %get-tuple-element.39.refs_1_), channel_id=1, source_target_pairs={{0,8},{1,9},{2,10},{3,11},{4,12},{5,13},{6,14},{7,15},{8,0},{9,1},... | collective-permute-start | bytes 1572872 | tf_op jit(solution)/shard_map/ppermute | solution.py:278
  21.6 1.5 %collective-permute-start.8 = (bf16[16,128,128]{2,1,0:T(8,128)(2,1)}, bf16[16,128,128]{2,1,0:T(8,128)(2,1)S(1)}, u32[]{:S(2)}, u32[]{:S(2)}) collective-permute-start(bf16[16,128,128]{2,1,0:T(8,128)(2,1)} %get-tuple-element.41.refs_8_), channel_id=1, source_target_pairs={{0,2},{1,3},{2,0},{3,1},{4,6},{5,7},{6,4},{7,5},{8,10},{9,11},{10,... | collective-permute-start | bytes 1572872 | tf_op jit(solution)/shard_map/ppermute | solution.py:278
  23.1 0.0 copy-done.4
  23.1 0.5 collective-permute-start.7
  23.6 0.0 collective-permute-start.6
  23.6 10.6 %collective-permute-done.9.refs_5_ = bf16[16,128,128]{2,1,0:T(8,128)(2,1)} collective-permute-done((bf16[16,128,128]{2,1,0:T(8,128)(2,1)S(1)}, bf16[16,128,128]{2,1,0:T(8,128)(2,1)}, u32[]{:S(2)}, u32[]{:S(2)}) %collective-permute-start.9) | collective-permute-done | bytes 524320 | tf_op jit(solution)/shard_map/ppermute | solution.py:278
  34.3 1.6 %collective-permute-done.8.refs_4_ = bf16[16,128,128]{2,1,0:T(8,128)(2,1)S(1)} collective-permute-done((bf16[16,128,128]{2,1,0:T(8,128)(2,1)}, bf16[16,128,128]{2,1,0:T(8,128)(2,1)S(1)}, u32[]{:S(2)}, u32[]{:S(2)}) %collective-permute-start.8) | collective-permute-done | bytes 524320 | tf_op jit(solution)/shard_map/ppermute | solution.py:278
  35.8 1.1 %collective-permute-done.7.refs_3_ = bf16[16,128,128]{2,1,0:T(8,128)(2,1)} collective-permute-done((bf16[16,128,128]{2,1,0:T(8,128)(2,1)S(1)}, bf16[16,128,128]{2,1,0:T(8,128)(2,1)}, u32[]{:S(2)}, u32[]{:S(2)}) %collective-permute-start.7) | collective-permute-done | bytes 524320 | tf_op jit(solution)/shard_map/ppermute | solution.py:278
  37.0 0.0 collective-permute-done.6.refs_2_
  37.0 0.0 collective-permute-done.5.refs_0_
  37.0 1.1 %hold.5 = (bf16[144,128,128]{2,1,0:T(8,128)(2,1)}, bf16[16,128,128]{2,1,0:T(8,128)(2,1)S(1)}, bf16[16,128,128]{2,1,0:T(8,128)(2,1)S(1)}, bf16[16,128,128]{2,1,0:T(8,128)(2,1)}, bf16[16,128,128]{2,1,0:T(8,128)(2,1)S(1)}) custom-call(bf16[144,128,128]{2,1,0:T(8,128)(2,1)} %collective-permu, ...), custom_call_target="tpu_custom_call", output_to_operand_aliasing={{0}: (0, {}), {1}: (1, {}), {2}: (2, {}), {3}: (3, {}), {4}... | custom-call | flops 1 | bytes 1 | tf_op jit(solution)/shard_map/hold/pallas_call | solution.py:220
  38.1 0.1 collective-permute-start.12
  38.2 0.0 copy-done.2
  38.2 0.6 collective-permute-start.11
  38.8 0.7 collective-permute-start.10
  39.5 0.1 concatenate.3.refs_0_
  39.6 0.0 copy-start.3
  39.6 1.0 %copy-done.3 = bf16[16,128,128]{2,1,0:T(8,128)(2,1)S(1)} copy-done((bf16[16,128,128]{2,1,0:T(8,128)(2,1)S(1)}, bf16[16,128,128]{2,1,0:T(8,128)(2,1)}, u32[]{:S(2)}) %copy-start.3) | copy-done | bytes 524312
  40.7 1.2 %copy-done.5 = f32[16,128,128]{2,1,0:T(8,128)S(1)} copy-done((f32[16,128,128]{2,1,0:T(8,128)S(1)}, f32[16,128,128]{2,1,0:T(8,128)}, u32[]{:S(2)}) %copy-start.5) | copy-done | bytes 1048600
  41.9 7.0 %hops_0.1 = (f32[16,128,128]{2,1,0:T(8,128)S(1)}, f32[16,128,128]{2,1,0:T(8,128)S(1)}, f32[8,128]{1,0:T(8,128)S(1)}, bf16[2,144,128,128]{3,2,1,0:T(8,128)(2,1)S(1)}) custom-call(s32[16]{0:T(128)S(1)} %concatenate.3.refs_0_, s32[256]{0:T(256)S(1)} %select_reduce_fusion.refs_1_, s32[256]{0:T(256)S(1)} %collective-permute-done.refs_5_.refs_2_, ...), custom_call_target="tpu_custom_call" | custom-call | flops 1 | bytes 1 | tf_op jit(solution)/shard_map/hops_0/pallas_call | solution.py:185
  48.9 2.3 %collective-permute-done.12.refs_4_ = bf16[16,128,128]{2,1,0:T(8,128)(2,1)} collective-permute-done((bf16[16,128,128]{2,1,0:T(8,128)(2,1)S(1)}, bf16[16,128,128]{2,1,0:T(8,128)(2,1)}, u32[]{:S(2)}, u32[]{:S(2)}) %collective-permute-start.12) | collective-permute-done | bytes 524320 | tf_op jit(solution)/shard_map/ppermute | solution.py:278
  51.1 0.1 collective-permute-done.11.refs_3_
  51.2 0.4 collective-permute-done.10.refs_2_
  51.6 1.1 %hold.6 = (bf16[16,128,128]{2,1,0:T(8,128)(2,1)S(1)}, bf16[16,128,128]{2,1,0:T(8,128)(2,1)S(1)}, bf16[16,128,128]{2,1,0:T(8,128)(2,1)S(1)}, bf16[16,128,128]{2,1,0:T(8,128)(2,1)}) custom-call(bf16[16,128,128]{2,1,0:T(8,128)(2,1)S(1)} %get-tuple-element.51.refs_0_, ...), custom_call_target="tpu_custom_call", output_to_operand_aliasing={{0}: (0, {}), {1}: (1, {}), {2}: (2, {}), {3}: (3, {})} | custom-call | flops 1 | bytes 1 | tf_op jit(solution)/shard_map/hold/pallas_call | solution.py:220
  52.8 0.6 collective-permute-start.13
  53.4 1.2 %collective-permute-start.15 = (bf16[16,128,128]{2,1,0:T(8,128)(2,1)S(1)}, bf16[16,128,128]{2,1,0:T(8,128)(2,1)S(1)}, u32[]{:S(2)}, u32[]{:S(2)}) collective-permute-start(bf16[16,128,128]{2,1,0:T(8,128)(2,1)S(1)} %get-tuple-element.55.refs_9_), channel_id=1, source_target_pairs={{0,2},{1,3},{2,0},{3,1},{4,6},{5,7},{6,4},{7,5},{8,10},{9,11},{10,... | collective-permute-start | bytes 1572872 | tf_op jit(solution)/shard_map/ppermute | solution.py:278
  54.6 0.5 collective-permute-start.14
  55.1 2.7 %hops_1.1 = (f32[16,128,128]{2,1,0:T(8,128)S(1)}, f32[16,128,128]{2,1,0:T(8,128)S(1)}, f32[8,128]{1,0:T(8,128)S(1)}) custom-call(s32[16]{0:T(128)S(1)} %concatenate.3.refs_0_, s32[256]{0:T(256)S(1)} %select_reduce_fusion.refs_1_, s32[256]{0:T(256)S(1)} %collective-permute-done.refs_5_.refs_2_, bf16[2,144,128,128]{3,2,1,0:T(8,128)(2,1)S(1)} %get-tuple-element.47.refs_3_, ...), custom_call_target="tpu_custom_call" | custom-call | flops 1 | bytes 1 | tf_op jit(solution)/shard_map/hops_1/pallas_call | solution.py:185
  57.8 7.1 %collective-permute-done.13.refs_0_ = bf16[16,128,128]{2,1,0:T(8,128)(2,1)S(1)} collective-permute-done((bf16[16,128,128]{2,1,0:T(8,128)(2,1)S(1)}, bf16[16,128,128]{2,1,0:T(8,128)(2,1)S(1)}, u32[]{:S(2)}, u32[]{:S(2)}) %collective-permute-start.13) | collective-permute-done | bytes 524320 | tf_op jit(solution)/shard_map/ppermute | solution.py:278
  64.9 0.1 collective-permute-done.15.refs_4_
  64.9 0.6 collective-permute-done.14.refs_3_
  65.6 1.7 %collective-permute-start.16 = (bf16[16,128,128]{2,1,0:T(8,128)(2,1)S(1)}, bf16[16,128,128]{2,1,0:T(8,128)(2,1)S(1)}, u32[]{:S(2)}, u32[]{:S(2)}) collective-permute-start(bf16[16,128,128]{2,1,0:T(8,128)(2,1)S(1)} %get-tuple-element.65), channel_id=1, source_target_pairs={{0,8},{1,9},{2,10},{3,11},{4,12},{5,13},{6,14},{7,15},{8,0},{9,1},... | collective-permute-start | bytes 1572872 | tf_op jit(solution)/shard_map/ppermute | solution.py:278
  67.4 1.1 %collective-permute-start.18 = (bf16[16,128,128]{2,1,0:T(8,128)(2,1)S(1)}, bf16[16,128,128]{2,1,0:T(8,128)(2,1)S(1)}, u32[]{:S(2)}, u32[]{:S(2)}) collective-permute-start(bf16[16,128,128]{2,1,0:T(8,128)(2,1)S(1)} %get-tuple-element.66), channel_id=1, source_target_pairs={{0,2},{1,3},{2,0},{3,1},{4,6},{5,7},{6,4},{7,5},{8,10},{9,11},{10,... | collective-permute-start | bytes 1572872 | tf_op jit(solution)/shard_map/ppermute | solution.py:278
  68.5 0.3 collective-permute-start.17
  68.8 2.3 %hops_2.1 = (f32[16,128,128]{2,1,0:T(8,128)S(1)}, f32[16,128,128]{2,1,0:T(8,128)S(1)}, f32[8,128]{1,0:T(8,128)}) custom-call(s32[16]{0:T(128)S(1)} %concatenate.3.refs_0_, s32[256]{0:T(256)S(1)} %select_reduce_fusion.refs_1_, s32[256]{0:T(256)S(1)} %collective-permute-done.refs_5_.refs_2_, bf16[2,144,128,128]{3,2,1,0:T(8,128)(2,1)S(1)} %get-tuple-element.47.refs_3_, ...), custom_call_target="tpu_custom_call" | custom-call | flops 1 | bytes 1 | tf_op jit(solution)/shard_map/hops_2/pallas_call | solution.py:185
  71.1 5.0 %collective-permute-done.16.refs_6_ = bf16[16,128,128]{2,1,0:T(8,128)(2,1)S(1)} collective-permute-done((bf16[16,128,128]{2,1,0:T(8,128)(2,1)S(1)}, bf16[16,128,128]{2,1,0:T(8,128)(2,1)S(1)}, u32[]{:S(2)}, u32[]{:S(2)}) %collective-permute-start.16) | collective-permute-done | bytes 524320 | tf_op jit(solution)/shard_map/ppermute | solution.py:278
  76.1 1.3 %collective-permute-done.18.refs_8_ = bf16[16,128,128]{2,1,0:T(8,128)(2,1)S(1)} collective-permute-done((bf16[16,128,128]{2,1,0:T(8,128)(2,1)S(1)}, bf16[16,128,128]{2,1,0:T(8,128)(2,1)S(1)}, u32[]{:S(2)}, u32[]{:S(2)}) %collective-permute-start.18) | collective-permute-done | bytes 524320 | tf_op jit(solution)/shard_map/ppermute | solution.py:278
  77.4 1.1 %collective-permute-done.17.refs_7_ = bf16[16,128,128]{2,1,0:T(8,128)(2,1)S(1)} collective-permute-done((bf16[16,128,128]{2,1,0:T(8,128)(2,1)S(1)}, bf16[16,128,128]{2,1,0:T(8,128)(2,1)S(1)}, u32[]{:S(2)}, u32[]{:S(2)}) %collective-permute-start.17) | collective-permute-done | bytes 524320 | tf_op jit(solution)/shard_map/ppermute | solution.py:278
  78.5 2.3 %hops_3.1 = (f32[16,128,128]{2,1,0:T(8,128)S(1)}, f32[16,128,128]{2,1,0:T(8,128)S(1)}, f32[32,128]{1,0:T(8,128)S(1)}) custom-call(s32[16]{0:T(128)S(1)} %concatenate.3.refs_0_, s32[256]{0:T(256)S(1)} %select_reduce_fusion.refs_1_, s32[256]{0:T(256)S(1)} %collective-permute-done.refs_5_.refs_2_, bf16[2,144,128,128]{3,2,1,0:T(8,128)(2,1)S(1)} %get-tuple-element.47.refs_3_, ...), custom_call_target="tpu_custom_call" | custom-call | flops 1 | bytes 1 | tf_op jit(solution)/shard_map/hops_3/pallas_call | solution.py:185
  80.8 0.1 collective-permute-start.19
  80.9 8.9 %all_to_all.11 = f32[32,1,128]{2,1,0:T(1,128)S(1)} all-to-all(f32[32,1,128]{2,1,0:T(1,128)S(1)} %bitcast.12), channel_id=1, replica_groups=mesh['groups'=1,'sector'=32] {'sector'}, dimensions={0} | all-to-all | bytes 32768 | tf_op jit(solution)/shard_map/all_to_all | solution.py:348
  89.8 0.0 collective-permute-done.19.theirs
  89.8 1.3 %finish.1 = (bf16[16,128,128]{2,1,0:T(8,128)(2,1)}, bf16[16,128,128]{2,1,0:T(8,128)(2,1)}, f32[1]{0:T(128)}) custom-call(f32[32,128]{1,0:T(8,128)S(1)} %bitcast.11, bf16[16,128,128]{2,1,0:T(8,128)(2,1)S(1)} %copy-done.1, f32[16,128,128]{2,1,0:T(8,128)S(1)} %get-tuple-element.69.mine, f32[16,128,128]{2,1,0:T(8,128)S(1)} %collective-permute-done.19.theirs), custom_call_target="tpu_custom_call" | custom-call | tf_op jit(solution)/shard_map/finish/pallas_call | solution.py:246
  (7 shorter events, 0.1 us)
Async XLA Ops:
  0.6 17.2 %collective-permute-start.4 = (bf16[16,128,128]{2,1,0:T(8,128)(2,1)}, bf16[16,128,128]{2,1,0:T(8,128)(2,1)S(1)}, u32[]{:S(2)}, u32[]{:S(2)}) collective-permute-start(bf16[16,128,128]{2,1,0:T(8,128)(2,1)} %psi.1), channel_id=1, source_target_pairs={{0,8},{1,9},{2,10},{3,11},{4,12},{5,13},{6,14},{7,15},{8,0},{9,1},... | collective-permute-start | bytes 1572872 | tf_op jit(solution)/shard_map/ppermute | solution.py:278
  3.7 14.1 %collective-permute-start.3 = (bf16[16,128,128]{2,1,0:T(8,128)(2,1)}, bf16[16,128,128]{2,1,0:T(8,128)(2,1)S(1)}, u32[]{:S(2)}, u32[]{:S(2)}) collective-permute-start(bf16[16,128,128]{2,1,0:T(8,128)(2,1)} %psi.1), channel_id=1, source_target_pairs={{0,1},{1,0},{2,3},{3,2},{4,5},{5,4},{6,7},{7,6},{8,16},{9,17},{10,... | collective-permute-start | bytes 1572872 | tf_op jit(solution)/shard_map/ppermute | solution.py:285
  3.7 14.7 %collective-permute-start.2 = (bf16[16,128,128]{2,1,0:T(8,128)(2,1)}, bf16[16,128,128]{2,1,0:T(8,128)(2,1)}, u32[]{:S(2)}, u32[]{:S(2)}) collective-permute-start(bf16[16,128,128]{2,1,0:T(8,128)(2,1)} %psi.1), channel_id=1, source_target_pairs={{0,4},{1,5},{2,6},{3,7},{4,0},{5,1},{6,2},{7,3},{8,12},{9,13},{10,... | collective-permute-start | bytes 1572872 | tf_op jit(solution)/shard_map/ppermute | solution.py:278
  5.2 14.3 %collective-permute-start.1 = (bf16[16,128,128]{2,1,0:T(8,128)(2,1)}, bf16[16,128,128]{2,1,0:T(8,128)(2,1)S(1)}, u32[]{:S(2)}, u32[]{:S(2)}) collective-permute-start(bf16[16,128,128]{2,1,0:T(8,128)(2,1)} %psi.1), channel_id=1, source_target_pairs={{0,2},{1,3},{2,0},{3,1},{4,6},{5,7},{6,4},{7,5},{8,10},{9,11},{10,... | collective-permute-start | bytes 1572872 | tf_op jit(solution)/shard_map/ppermute | solution.py:278
  8.6 9.2 %collective-permute-start = (s32[256]{0:T(256)S(1)}, s32[256]{0:T(256)S(1)}, u32[]{:S(2)}, u32[]{:S(2)}) collective-permute-start(s32[256]{0:T(256)S(1)} %select_reduce_fusion.refs_1_), channel_id=1, source_target_pairs={{0,1},{1,0},{2,3},{3,2},{4,5},{5,4},{6,7},{7,6},{8,9},{9,8},{10,11... | collective-permute-start | bytes 3080 | tf_op jit(solution)/shard_map/ppermute | solution.py:278
  8.7 1.0 %copy-start = (bf16[16,128,128]{2,1,0:T(8,128)(2,1)S(1)}, bf16[16,128,128]{2,1,0:T(8,128)(2,1)}, u32[]{:S(2)}) copy-start(bf16[16,128,128]{2,1,0:T(8,128)(2,1)} %psi.1) | copy-start | bytes 1572868
  17.8 5.3 %copy-start.4 = (f32[16,128,128]{2,1,0:T(8,128)}, f32[16,128,128]{2,1,0:T(8,128)S(1)}, u32[]{:S(2)}) copy-start(f32[16,128,128]{2,1,0:T(8,128)S(1)} %get-tuple-element.43.refs_5_) | copy-start | bytes 3145732
  19.6 18.6 %copy-start.2 = (bf16[16,128,128]{2,1,0:T(8,128)(2,1)}, bf16[16,128,128]{2,1,0:T(8,128)(2,1)S(1)}, u32[]{:S(2)}) copy-start(bf16[16,128,128]{2,1,0:T(8,128)(2,1)S(1)} %get-tuple-element.40.refs_9_) | copy-start | bytes 1572868
  19.6 20.0 %copy-start.1 = (bf16[16,128,128]{2,1,0:T(8,128)(2,1)S(1)}, bf16[16,128,128]{2,1,0:T(8,128)(2,1)}, u32[]{:S(2)}) copy-start(bf16[16,128,128]{2,1,0:T(8,128)(2,1)} %psi.1) | copy-start | bytes 1572868
  19.6 17.4 %collective-permute-start.5 = (bf16[144,128,128]{2,1,0:T(8,128)(2,1)}, bf16[144,128,128]{2,1,0:T(8,128)(2,1)}, u32[]{:S(2)}, u32[]{:S(2)}) collective-permute-start(bf16[144,128,128]{2,1,0:T(8,128)(2,1)} %get-tuple-element.38.refs_3_), channel_id=1, source_target_pairs={{0,1},{1,0},{2,3},{3,2},{4,5},{5,4},{6,7},{7,6},{8,9},{9,8},{10,11... | collective-permute-start | bytes 14155784 | tf_op jit(solution)/shard_map/ppermute | solution.py:278
  19.7 14.6 %collective-permute-start.9 = (bf16[16,128,128]{2,1,0:T(8,128)(2,1)S(1)}, bf16[16,128,128]{2,1,0:T(8,128)(2,1)}, u32[]{:S(2)}, u32[]{:S(2)}) collective-permute-start(bf16[16,128,128]{2,1,0:T(8,128)(2,1)S(1)} %get-tuple-element.39.refs_1_), channel_id=1, source_target_pairs={{0,8},{1,9},{2,10},{3,11},{4,12},{5,13},{6,14},{7,15},{8,0},{9,1},... | collective-permute-start | bytes 1572872 | tf_op jit(solution)/shard_map/ppermute | solution.py:278
  21.6 14.2 %collective-permute-start.8 = (bf16[16,128,128]{2,1,0:T(8,128)(2,1)}, bf16[16,128,128]{2,1,0:T(8,128)(2,1)S(1)}, u32[]{:S(2)}, u32[]{:S(2)}) collective-permute-start(bf16[16,128,128]{2,1,0:T(8,128)(2,1)} %get-tuple-element.41.refs_8_), channel_id=1, source_target_pairs={{0,2},{1,3},{2,0},{3,1},{4,6},{5,7},{6,4},{7,5},{8,10},{9,11},{10,... | collective-permute-start | bytes 1572872 | tf_op jit(solution)/shard_map/ppermute | solution.py:278
  23.1 13.8 %collective-permute-start.7 = (bf16[16,128,128]{2,1,0:T(8,128)(2,1)S(1)}, bf16[16,128,128]{2,1,0:T(8,128)(2,1)}, u32[]{:S(2)}, u32[]{:S(2)}) collective-permute-start(bf16[16,128,128]{2,1,0:T(8,128)(2,1)S(1)} %get-tuple-element.40.refs_9_), channel_id=1, source_target_pairs={{0,4},{1,5},{2,6},{3,7},{4,0},{5,1},{6,2},{7,3},{8,12},{9,13},{10,... | collective-permute-start | bytes 1572872 | tf_op jit(solution)/shard_map/ppermute | solution.py:278
  23.6 13.3 %collective-permute-start.6 = (bf16[16,128,128]{2,1,0:T(8,128)(2,1)S(1)}, bf16[16,128,128]{2,1,0:T(8,128)(2,1)S(1)}, u32[]{:S(2)}, u32[]{:S(2)}) collective-permute-start(bf16[16,128,128]{2,1,0:T(8,128)(2,1)S(1)} %get-tuple-element.40.refs_9_), channel_id=1, source_target_pairs={{0,1},{1,0},{2,3},{3,2},{4,5},{5,4},{6,7},{7,6},{8,16},{9,17},{10,... | collective-permute-start | bytes 1572872 | tf_op jit(solution)/shard_map/ppermute | solution.py:285
  38.1 13.0 %collective-permute-start.12 = (bf16[16,128,128]{2,1,0:T(8,128)(2,1)S(1)}, bf16[16,128,128]{2,1,0:T(8,128)(2,1)}, u32[]{:S(2)}, u32[]{:S(2)}) collective-permute-start(bf16[16,128,128]{2,1,0:T(8,128)(2,1)S(1)} %get-tuple-element.51.refs_0_), channel_id=1, source_target_pairs={{0,8},{1,9},{2,10},{3,11},{4,12},{5,13},{6,14},{7,15},{8,0},{9,1},... | collective-permute-start | bytes 1572872 | tf_op jit(solution)/shard_map/ppermute | solution.py:278
  38.2 13.0 %collective-permute-start.11 = (bf16[16,128,128]{2,1,0:T(8,128)(2,1)S(1)}, bf16[16,128,128]{2,1,0:T(8,128)(2,1)}, u32[]{:S(2)}, u32[]{:S(2)}) collective-permute-start(bf16[16,128,128]{2,1,0:T(8,128)(2,1)S(1)} %get-tuple-element.50.refs_6_), channel_id=1, source_target_pairs={{0,2},{1,3},{2,0},{3,1},{4,6},{5,7},{6,4},{7,5},{8,10},{9,11},{10,... | collective-permute-start | bytes 1572872 | tf_op jit(solution)/shard_map/ppermute | solution.py:278
  38.8 12.8 %collective-permute-start.10 = (bf16[16,128,128]{2,1,0:T(8,128)(2,1)S(1)}, bf16[16,128,128]{2,1,0:T(8,128)(2,1)S(1)}, u32[]{:S(2)}, u32[]{:S(2)}) collective-permute-start(bf16[16,128,128]{2,1,0:T(8,128)(2,1)S(1)} %get-tuple-element.50.refs_6_), channel_id=1, source_target_pairs={{0,4},{1,5},{2,6},{3,7},{4,0},{5,1},{6,2},{7,3},{8,12},{9,13},{10,... | collective-permute-start | bytes 1572872 | tf_op jit(solution)/shard_map/ppermute | solution.py:278
  39.6 1.0 %copy-start.3 = (bf16[16,128,128]{2,1,0:T(8,128)(2,1)S(1)}, bf16[16,128,128]{2,1,0:T(8,128)(2,1)}, u32[]{:S(2)}) copy-start(bf16[16,128,128]{2,1,0:T(8,128)(2,1)} %copy-done.2) | copy-start | bytes 1572868
  40.7 1.2 %copy-start.5 = (f32[16,128,128]{2,1,0:T(8,128)S(1)}, f32[16,128,128]{2,1,0:T(8,128)}, u32[]{:S(2)}) copy-start(f32[16,128,128]{2,1,0:T(8,128)} %copy-done.4) | copy-start | bytes 3145732
  41.9 13.2 %copy-start.6 = (f32[16]{0:T(128)S(1)}, f32[16]{0:T(128)}, u32[]{:S(2)}) copy-start(f32[16]{0:T(128)} %refs_10_.1) | copy-start | bytes 196
  52.8 12.1 %collective-permute-start.13 = (bf16[16,128,128]{2,1,0:T(8,128)(2,1)S(1)}, bf16[16,128,128]{2,1,0:T(8,128)(2,1)S(1)}, u32[]{:S(2)}, u32[]{:S(2)}) collective-permute-start(bf16[16,128,128]{2,1,0:T(8,128)(2,1)S(1)} %get-tuple-element.58), channel_id=1, source_target_pairs={{0,8},{1,9},{2,10},{3,11},{4,12},{5,13},{6,14},{7,15},{8,0},{9,1},... | collective-permute-start | bytes 1572872 | tf_op jit(solution)/shard_map/ppermute | solution.py:278
  53.4 11.5 %collective-permute-start.15 = (bf16[16,128,128]{2,1,0:T(8,128)(2,1)S(1)}, bf16[16,128,128]{2,1,0:T(8,128)(2,1)S(1)}, u32[]{:S(2)}, u32[]{:S(2)}) collective-permute-start(bf16[16,128,128]{2,1,0:T(8,128)(2,1)S(1)} %get-tuple-element.55.refs_9_), channel_id=1, source_target_pairs={{0,2},{1,3},{2,0},{3,1},{4,6},{5,7},{6,4},{7,5},{8,10},{9,11},{10,... | collective-permute-start | bytes 1572872 | tf_op jit(solution)/shard_map/ppermute | solution.py:278
  54.6 11.0 %collective-permute-start.14 = (bf16[16,128,128]{2,1,0:T(8,128)(2,1)S(1)}, bf16[16,128,128]{2,1,0:T(8,128)(2,1)S(1)}, u32[]{:S(2)}, u32[]{:S(2)}) collective-permute-start(bf16[16,128,128]{2,1,0:T(8,128)(2,1)S(1)} %get-tuple-element.55.refs_9_), channel_id=1, source_target_pairs={{0,4},{1,5},{2,6},{3,7},{4,0},{5,1},{6,2},{7,3},{8,12},{9,13},{10,... | collective-permute-start | bytes 1572872 | tf_op jit(solution)/shard_map/ppermute | solution.py:278
  65.6 10.5 %collective-permute-start.16 = (bf16[16,128,128]{2,1,0:T(8,128)(2,1)S(1)}, bf16[16,128,128]{2,1,0:T(8,128)(2,1)S(1)}, u32[]{:S(2)}, u32[]{:S(2)}) collective-permute-start(bf16[16,128,128]{2,1,0:T(8,128)(2,1)S(1)} %get-tuple-element.65), channel_id=1, source_target_pairs={{0,8},{1,9},{2,10},{3,11},{4,12},{5,13},{6,14},{7,15},{8,0},{9,1},... | collective-permute-start | bytes 1572872 | tf_op jit(solution)/shard_map/ppermute | solution.py:278
  67.4 10.0 %collective-permute-start.18 = (bf16[16,128,128]{2,1,0:T(8,128)(2,1)S(1)}, bf16[16,128,128]{2,1,0:T(8,128)(2,1)S(1)}, u32[]{:S(2)}, u32[]{:S(2)}) collective-permute-start(bf16[16,128,128]{2,1,0:T(8,128)(2,1)S(1)} %get-tuple-element.66), channel_id=1, source_target_pairs={{0,2},{1,3},{2,0},{3,1},{4,6},{5,7},{6,4},{7,5},{8,10},{9,11},{10,... | collective-permute-start | bytes 1572872 | tf_op jit(solution)/shard_map/ppermute | solution.py:278
  68.5 10.0 %collective-permute-start.17 = (bf16[16,128,128]{2,1,0:T(8,128)(2,1)S(1)}, bf16[16,128,128]{2,1,0:T(8,128)(2,1)S(1)}, u32[]{:S(2)}, u32[]{:S(2)}) collective-permute-start(bf16[16,128,128]{2,1,0:T(8,128)(2,1)S(1)} %get-tuple-element.62.refs_8_), channel_id=1, source_target_pairs={{0,4},{1,5},{2,6},{3,7},{4,0},{5,1},{6,2},{7,3},{8,12},{9,13},{10,... | collective-permute-start | bytes 1572872 | tf_op jit(solution)/shard_map/ppermute | solution.py:278
  80.8 9.0 %collective-permute-start.19 = (f32[16,128,128]{2,1,0:T(8,128)S(1)}, f32[16,128,128]{2,1,0:T(8,128)S(1)}, u32[]{:S(2)}, u32[]{:S(2)}) collective-permute-start(f32[16,128,128]{2,1,0:T(8,128)S(1)} %get-tuple-element.70), channel_id=1, source_target_pairs={{0,1},{1,0},{2,3},{3,2},{4,5},{5,4},{6,7},{7,6},{8,9},{9,8},{10,11... | collective-permute-start | bytes 3145736 | tf_op jit(solution)/shard_map/ppermute | solution.py:278

commit v5 on v4

--- a/solution.py
+++ b/solution.py
@@ -127,7 +127,7 @@
     )(psi.reshape(rows, cols, size, size), right, left)
 
 
-def hop_kernel(base, count, first, diagonal, last, capacity, *refs):
+def hop_kernel(base, count, first, diagonal, tally, last, capacity, *refs):
     refs = list(refs)
     take = lambda n: [refs.pop(0) for _ in range(n)]
     order, *terms = take(3)
@@ -135,6 +135,7 @@
     acc_in = take(1 if first else 2)
     bufs = take(count)
     onsite = take(1)[0] if diagonal else None
+    tally_in = take(1)[0] if tally == "add" else None
     square = take(1)[0] if last else None
     acc = take(2)
     sums = take(1)[0]
@@ -156,6 +157,7 @@
     if diagonal:
         for t in range(sec):
             acc[0][t] = acc[0][t] + onsite[t] * env[0, first_psi + t].astype(F32)
+    total = tally_in[...] if tally == "add" else jnp.zeros(acc[0].shape[1:], F32)
     for s, psi in enumerate(bufs):
         slot = order[base + s] * capacity
         words = [(e, terms[e][slot + r]) for e in range(2) for r in range(capacity)]
@@ -164,38 +166,43 @@
         for (e, w), part in zip(words, parts):
             t = (w >> 8) & 255
             acc[e][t] = acc[e][t] + part
-    if last:
-        total = jnp.zeros(acc[0].shape[1:], F32)
+            if tally == "add":
+                total += env[e, first_psi + t].astype(F32) * part
+    if tally == "all":
         for e in range(2):
             total = lax.fori_loop(0, sec, lambda t, v, e=e: v + env[e, first_psi + t].astype(F32) * acc[e][t], total)
+    if last:
         lanes = lax.broadcasted_iota(jnp.int32, sums.shape, 1)
         sums[...] = jnp.where(lanes < sums.shape[1] // 2, jnp.sum(total), jnp.sum(square[...]))
+    elif tally:
+        sums[...] = total
     else:
         sums[...] = jnp.zeros(sums.shape, F32)
 
 
-def hop_call(name, order, base, terms, envs, accs, bufs, onsite, last_args, owners, capacity):
+def hop_call(name, order, base, terms, envs, accs, bufs, onsite, tally, tallies, square, owners, capacity):
     sec, size = accs[0].shape[:2]
-    first, last = len(accs) == 1, bool(last_args)
+    first, last = len(accs) == 1, bool(square)
     count = len(bufs)
     acc_shape = jax.ShapeDtypeStruct((sec, size, size), F32)
-    out_shape = [acc_shape, acc_shape, jax.ShapeDtypeStruct((owners, size), F32) if last else TOKEN]
+    side = (owners, size) if last else (size, size) if tally else (8, 128)
+    out_shape = [acc_shape, acc_shape, jax.ShapeDtypeStruct(side, F32)]
     if first:
         out_shape.append(jax.ShapeDtypeStruct((2,) + envs[0].shape, BF16))
     return pl.pallas_call(
-        functools.partial(hop_kernel, base, count, first, bool(onsite), last, capacity),
+        functools.partial(hop_kernel, base, count, first, bool(onsite), tally, last, capacity),
         out_shape=out_shape,
         in_specs=[SMEM] * 3
         + [ANY if first else VMEM] * (len(envs) + len(accs))
         + [VMEM] * count
         + [SMEM] * len(onsite)
-        + [VMEM] * len(last_args),
+        + [VMEM] * len(tallies + square),
         out_specs=[VMEM] * len(out_shape),
         scratch_shapes=[pltpu.SemaphoreType.DMA((3,))],
         compiler_params=pltpu.CompilerParams(vmem_limit_bytes=VMEM_BYTES),
         cost_estimate=COST,
         name=name,
-    )(order, *terms, *envs, *accs, *bufs, *onsite, *last_args)
+    )(order, *terms, *envs, *accs, *bufs, *onsite, *tallies, *square)
 
 
 def hold_kernel(count, move, *refs):
@@ -290,8 +297,8 @@
     groups = [
         [(0, 0), (0, x), (0, y), (1, 0), (0, xy), (1, y)],
         [(2, 0), (2, x), (2, y), (3, 0)],
-        [(1, x), (3, y), (3, x)],
-        [(1, xy), (3, xy), (2, xy)],
+        [(3, y), (3, x), (1, x)],
+        [(1, xy), (2, xy), (3, xy)],
     ]
     order = jnp.concatenate([me ^ layer_masks[b] ^ jnp.full((1,), bits) for group in groups for b, bits in group])
 
@@ -301,10 +308,10 @@
     def hold(keys, *tokens, **move):
         held.update(zip(keys, hold_until([held[key] for key in keys], tokens, **move)))
 
-    def run(group, onsite=(), last_args=()):
+    def run(group, onsite=(), tally=None, tallies=(), square=()):
         out = hop_call(
             f"hops_{group}", order, state["base"], terms, state["envs"], state["accs"],
-            tuple(held[key] for key in groups[group]), onsite, last_args, owners, capacity,
+            tuple(held[key] for key in groups[group]), onsite, tally, tallies, square, owners, capacity,
         )
         state["accs"] = out[:2]
         if group == 0:
@@ -343,8 +350,8 @@
     held[2, xy] = swap(held[2, y], x)
     held[3, xy] = swap(held[3, x], y)
     held[1, xy] = swap(held[0, xy], z)
-    run(2)
-    sums = run(3, (), (square,))
+    tally = run(2, (), "all")
+    sums = run(3, (), "add", (tally,), (square,))
     sums = lax.all_to_all(sums, "sector", 0, 0, tiled=True)
     mine, theirs = state["accs"]
     return finish_call(sums, wavefunction, mine, swap(theirs, core))

time: 91.5 us -> 91.2 us (level)
  no operation moved by 1% of the time
where the time goes in v5:
time: 91.2 us; the launch traced here: 90.7 us
  waiting for transfers between devices  33.1 us (36%)
  Pallas kernels  25.5 us (28%)
  starting transfers between devices  17.2 us (19%)
  blocking collectives  8.89 us (10%)
  local copies, waits for them, and re-layouts  4.96 us (5%)
    ppermute x18, waiting for transfers between devices, swap(): return lax.ppermute(value, 'sector', [(i, i ^ mask) for i in range(owners)])  33.1 us
    ppermute x18, starting transfers between devices, swap(): return lax.ppermute(value, 'sector', [(i, i ^ mask) for i in range(owners)])  17.2 us
    pallas_call x4, Pallas kernels, hop_call(): pl.pallas_call(functools.partial(hop_kernel, base, count, first, bool(ons...  13.8 us
    all_to_all x1, blocking collectives, spread_everywhere(): sums = lax.all_to_all(sums, 'sector', 0, 0, tiled=True)  8.89 us
    pallas_call x1, Pallas kernels, local_call(): pl.pallas_call(local_kernel, out_shape=(jax.ShapeDtypeStruct((sec, size,...  8.05 us
    unnamed x14, local copies, waits for them, and re-layouts  3.32 us
    pallas_call x4, Pallas kernels, hold_until(): pl.pallas_call(functools.partial(hold_kernel, count, move), out_shape=[ja...  2.33 us
  transfers between devices with their start and end apart: 20, of which 14 were waited for; matrix products, arithmetic and copies ran while one was open for 2% of the time, Pallas kernels for 22%

profile of v5, /device:TPU:0, one launch (start us, length us, event | category | flops | bytes accessed | tf_op | source)
XLA Modules:
  0.0 90.7 jit_solution(6566112292386168596)
XLA Ops:
  0.6 3.1 %collective-permute-start.4 = (bf16[16,128,128]{2,1,0:T(8,128)(2,1)}, bf16[16,128,128]{2,1,0:T(8,128)(2,1)S(1)}, u32[]{:S(2)}, u32[]{:S(2)}) collective-permute-start(bf16[16,128,128]{2,1,0:T(8,128)(2,1)} %psi.1), channel_id=1, source_target_pairs={{0,8},{1,9},{2,10},{3,11},{4,12},{5,13},{6,14},{7,15},{8,0},{9,1},... | collective-permute-start | bytes 1572872 | tf_op jit(solution)/shard_map/ppermute | solution.py:285
  3.7 0.0 collective-permute-start.3
  3.7 1.5 %collective-permute-start.2 = (bf16[16,128,128]{2,1,0:T(8,128)(2,1)}, bf16[16,128,128]{2,1,0:T(8,128)(2,1)}, u32[]{:S(2)}, u32[]{:S(2)}) collective-permute-start(bf16[16,128,128]{2,1,0:T(8,128)(2,1)} %psi.1), channel_id=1, source_target_pairs={{0,4},{1,5},{2,6},{3,7},{4,0},{5,1},{6,2},{7,3},{8,12},{9,13},{10,... | collective-permute-start | bytes 1572872 | tf_op jit(solution)/shard_map/ppermute | solution.py:285
  5.2 1.5 %collective-permute-start.1 = (bf16[16,128,128]{2,1,0:T(8,128)(2,1)}, bf16[16,128,128]{2,1,0:T(8,128)(2,1)S(1)}, u32[]{:S(2)}, u32[]{:S(2)}) collective-permute-start(bf16[16,128,128]{2,1,0:T(8,128)(2,1)} %psi.1), channel_id=1, source_target_pairs={{0,2},{1,3},{2,0},{3,1},{4,6},{5,7},{6,4},{7,5},{8,10},{9,11},{10,... | collective-permute-start | bytes 1572872 | tf_op jit(solution)/shard_map/ppermute | solution.py:285
  6.7 0.8 reshape.95
  7.5 0.8 reshape.96
  8.3 0.2 convert_reduce_fusion
  8.5 0.1 select_reduce_fusion.refs_1_
  8.6 0.1 collective-permute-start
  8.7 0.0 copy-start
  8.7 1.0 %copy-done = bf16[16,128,128]{2,1,0:T(8,128)(2,1)S(1)} copy-done((bf16[16,128,128]{2,1,0:T(8,128)(2,1)S(1)}, bf16[16,128,128]{2,1,0:T(8,128)(2,1)}, u32[]{:S(2)}) %copy-start) | copy-done | bytes 524312
  9.7 8.0 %local_channels.1 = (f32[16,128,128]{2,1,0:T(8,128)S(1)}, f32[128,128]{1,0:T(8,128)S(1)}, bf16[144,128,128]{2,1,0:T(8,128)(2,1)}) custom-call(bf16[4,4,128,128]{3,2,1,0:T(8,128)(2,1)S(1)} %bitcast.10, bf16[4,32,128,128]{3,2,1,0:T(8,128)(2,1)} %right.1, bf16[4,32,128,128]{3,2,1,0:T(8,128)(2,1)} %left.1), custom_call_target="tpu_custom_call" | custom-call | flops 1 | bytes 1 | tf_op jit(solution)/shard_map/local_channels/pallas_call | solution.py:107
  17.8 0.0 copy-start.4
  17.8 0.0 collective-permute-done.refs_5_.refs_2_
  17.8 0.0 collective-permute-done.4.refs_3_
  17.8 0.0 collective-permute-done.3.refs_2_
  17.8 0.5 collective-permute-done.2.refs_1_
  18.4 1.1 %collective-permute-done.1.refs_0_ = bf16[16,128,128]{2,1,0:T(8,128)(2,1)S(1)} collective-permute-done((bf16[16,128,128]{2,1,0:T(8,128)(2,1)}, bf16[16,128,128]{2,1,0:T(8,128)(2,1)S(1)}, u32[]{:S(2)}, u32[]{:S(2)}) %collective-permute-start.1) | collective-permute-done | bytes 524320 | tf_op jit(solution)/shard_map/ppermute | solution.py:285
  19.6 0.0 copy-start.2
  19.6 0.0 copy-start.1
  19.6 0.1 collective-permute-start.5
  19.7 2.0 %collective-permute-start.9 = (bf16[16,128,128]{2,1,0:T(8,128)(2,1)S(1)}, bf16[16,128,128]{2,1,0:T(8,128)(2,1)}, u32[]{:S(2)}, u32[]{:S(2)}) collective-permute-start(bf16[16,128,128]{2,1,0:T(8,128)(2,1)S(1)} %get-tuple-element.40.refs_1_), channel_id=1, source_target_pairs={{0,8},{1,9},{2,10},{3,11},{4,12},{5,13},{6,14},{7,15},{8,0},{9,1},... | collective-permute-start | bytes 1572872 | tf_op jit(solution)/shard_map/ppermute | solution.py:285
  21.6 1.5 %collective-permute-start.8 = (bf16[16,128,128]{2,1,0:T(8,128)(2,1)}, bf16[16,128,128]{2,1,0:T(8,128)(2,1)S(1)}, u32[]{:S(2)}, u32[]{:S(2)}) collective-permute-start(bf16[16,128,128]{2,1,0:T(8,128)(2,1)} %get-tuple-element.42.refs_8_), channel_id=1, source_target_pairs={{0,2},{1,3},{2,0},{3,1},{4,6},{5,7},{6,4},{7,5},{8,10},{9,11},{10,... | collective-permute-start | bytes 1572872 | tf_op jit(solution)/shard_map/ppermute | solution.py:285
  23.1 0.0 copy-done.4
  23.1 0.5 collective-permute-start.7
  23.6 0.0 collective-permute-start.6
  23.6 10.6 %collective-permute-done.9.refs_5_ = bf16[16,128,128]{2,1,0:T(8,128)(2,1)} collective-permute-done((bf16[16,128,128]{2,1,0:T(8,128)(2,1)S(1)}, bf16[16,128,128]{2,1,0:T(8,128)(2,1)}, u32[]{:S(2)}, u32[]{:S(2)}) %collective-permute-start.9) | collective-permute-done | bytes 524320 | tf_op jit(solution)/shard_map/ppermute | solution.py:285
  34.3 1.6 %collective-permute-done.8.refs_4_ = bf16[16,128,128]{2,1,0:T(8,128)(2,1)S(1)} collective-permute-done((bf16[16,128,128]{2,1,0:T(8,128)(2,1)}, bf16[16,128,128]{2,1,0:T(8,128)(2,1)S(1)}, u32[]{:S(2)}, u32[]{:S(2)}) %collective-permute-start.8) | collective-permute-done | bytes 524320 | tf_op jit(solution)/shard_map/ppermute | solution.py:285
  35.8 1.1 %collective-permute-done.7.refs_3_ = bf16[16,128,128]{2,1,0:T(8,128)(2,1)} collective-permute-done((bf16[16,128,128]{2,1,0:T(8,128)(2,1)S(1)}, bf16[16,128,128]{2,1,0:T(8,128)(2,1)}, u32[]{:S(2)}, u32[]{:S(2)}) %collective-permute-start.7) | collective-permute-done | bytes 524320 | tf_op jit(solution)/shard_map/ppermute | solution.py:285
  37.0 0.0 collective-permute-done.6.refs_2_
  37.0 0.0 collective-permute-done.5.refs_0_
  37.0 1.1 %hold.5 = (bf16[144,128,128]{2,1,0:T(8,128)(2,1)}, bf16[16,128,128]{2,1,0:T(8,128)(2,1)S(1)}, bf16[16,128,128]{2,1,0:T(8,128)(2,1)S(1)}, bf16[16,128,128]{2,1,0:T(8,128)(2,1)}, bf16[16,128,128]{2,1,0:T(8,128)(2,1)S(1)}) custom-call(bf16[144,128,128]{2,1,0:T(8,128)(2,1)} %collective-permu, ...), custom_call_target="tpu_custom_call", output_to_operand_aliasing={{0}: (0, {}), {1}: (1, {}), {2}: (2, {}), {3}: (3, {}), {4}... | custom-call | flops 1 | bytes 1 | tf_op jit(solution)/shard_map/hold/pallas_call | solution.py:227
  38.1 0.1 collective-permute-start.12
  38.2 0.0 copy-done.2
  38.2 0.6 collective-permute-start.11
  38.8 0.7 collective-permute-start.10
  39.5 0.1 concatenate.3.refs_0_
  39.6 0.0 copy-start.3
  39.6 1.0 %copy-done.3 = bf16[16,128,128]{2,1,0:T(8,128)(2,1)S(1)} copy-done((bf16[16,128,128]{2,1,0:T(8,128)(2,1)S(1)}, bf16[16,128,128]{2,1,0:T(8,128)(2,1)}, u32[]{:S(2)}) %copy-start.3) | copy-done | bytes 524312
  40.7 1.2 %copy-done.5 = f32[16,128,128]{2,1,0:T(8,128)S(1)} copy-done((f32[16,128,128]{2,1,0:T(8,128)S(1)}, f32[16,128,128]{2,1,0:T(8,128)}, u32[]{:S(2)}) %copy-start.5) | copy-done | bytes 1048600
  41.9 7.0 %hops_0.1 = (f32[16,128,128]{2,1,0:T(8,128)S(1)}, f32[16,128,128]{2,1,0:T(8,128)S(1)}, f32[8,128]{1,0:T(8,128)S(1)}, bf16[2,144,128,128]{3,2,1,0:T(8,128)(2,1)S(1)}) custom-call(s32[16]{0:T(128)S(1)} %concatenate.3.refs_0_, s32[256]{0:T(256)S(1)} %select_reduce_fusion.refs_1_, s32[256]{0:T(256)S(1)} %collective-permute-done.refs_5_.refs_2_, ...), custom_call_target="tpu_custom_call" | custom-call | flops 1 | bytes 1 | tf_op jit(solution)/shard_map/hops_0/pallas_call | solution.py:192
  48.9 2.3 %collective-permute-done.12.refs_4_ = bf16[16,128,128]{2,1,0:T(8,128)(2,1)} collective-permute-done((bf16[16,128,128]{2,1,0:T(8,128)(2,1)S(1)}, bf16[16,128,128]{2,1,0:T(8,128)(2,1)}, u32[]{:S(2)}, u32[]{:S(2)}) %collective-permute-start.12) | collective-permute-done | bytes 524320 | tf_op jit(solution)/shard_map/ppermute | solution.py:285
  51.1 0.1 collective-permute-done.11.refs_3_
  51.2 0.4 collective-permute-done.10.refs_2_
  51.6 1.1 %hold.6 = (bf16[16,128,128]{2,1,0:T(8,128)(2,1)S(1)}, bf16[16,128,128]{2,1,0:T(8,128)(2,1)S(1)}, bf16[16,128,128]{2,1,0:T(8,128)(2,1)S(1)}, bf16[16,128,128]{2,1,0:T(8,128)(2,1)}) custom-call(bf16[16,128,128]{2,1,0:T(8,128)(2,1)S(1)} %get-tuple-element.52.refs_0_, ...), custom_call_target="tpu_custom_call", output_to_operand_aliasing={{0}: (0, {}), {1}: (1, {}), {2}: (2, {}), {3}: (3, {})} | custom-call | flops 1 | bytes 1 | tf_op jit(solution)/shard_map/hold/pallas_call | solution.py:227
  52.8 0.6 collective-permute-start.13
  53.4 1.2 %collective-permute-start.15 = (bf16[16,128,128]{2,1,0:T(8,128)(2,1)S(1)}, bf16[16,128,128]{2,1,0:T(8,128)(2,1)S(1)}, u32[]{:S(2)}, u32[]{:S(2)}) collective-permute-start(bf16[16,128,128]{2,1,0:T(8,128)(2,1)S(1)} %get-tuple-element.56.refs_9_), channel_id=1, source_target_pairs={{0,2},{1,3},{2,0},{3,1},{4,6},{5,7},{6,4},{7,5},{8,10},{9,11},{10,... | collective-permute-start | bytes 1572872 | tf_op jit(solution)/shard_map/ppermute | solution.py:285
  54.6 0.5 collective-permute-start.14
  55.1 2.7 %hops_1.1 = (f32[16,128,128]{2,1,0:T(8,128)S(1)}, f32[16,128,128]{2,1,0:T(8,128)S(1)}, f32[8,128]{1,0:T(8,128)S(1)}) custom-call(s32[16]{0:T(128)S(1)} %concatenate.3.refs_0_, s32[256]{0:T(256)S(1)} %select_reduce_fusion.refs_1_, s32[256]{0:T(256)S(1)} %collective-permute-done.refs_5_.refs_2_, bf16[2,144,128,128]{3,2,1,0:T(8,128)(2,1)S(1)} %get-tuple-element.48.refs_3_, ...), custom_call_target="tpu_custom_call" | custom-call | flops 1 | bytes 1 | tf_op jit(solution)/shard_map/hops_1/pallas_call | solution.py:192
  57.8 7.1 %collective-permute-done.13.refs_0_ = bf16[16,128,128]{2,1,0:T(8,128)(2,1)S(1)} collective-permute-done((bf16[16,128,128]{2,1,0:T(8,128)(2,1)S(1)}, bf16[16,128,128]{2,1,0:T(8,128)(2,1)S(1)}, u32[]{:S(2)}, u32[]{:S(2)}) %collective-permute-start.13) | collective-permute-done | bytes 524320 | tf_op jit(solution)/shard_map/ppermute | solution.py:285
  64.9 0.1 collective-permute-done.15.refs_4_
  64.9 0.6 collective-permute-done.14.refs_3_
  65.6 1.7 %collective-permute-start.16 = (bf16[16,128,128]{2,1,0:T(8,128)(2,1)S(1)}, bf16[16,128,128]{2,1,0:T(8,128)(2,1)S(1)}, u32[]{:S(2)}, u32[]{:S(2)}) collective-permute-start(bf16[16,128,128]{2,1,0:T(8,128)(2,1)S(1)} %get-tuple-element.66), channel_id=1, source_target_pairs={{0,8},{1,9},{2,10},{3,11},{4,12},{5,13},{6,14},{7,15},{8,0},{9,1},... | collective-permute-start | bytes 1572872 | tf_op jit(solution)/shard_map/ppermute | solution.py:285
  67.4 1.1 %collective-permute-start.17 = (bf16[16,128,128]{2,1,0:T(8,128)(2,1)S(1)}, bf16[16,128,128]{2,1,0:T(8,128)(2,1)S(1)}, u32[]{:S(2)}, u32[]{:S(2)}) collective-permute-start(bf16[16,128,128]{2,1,0:T(8,128)(2,1)S(1)} %get-tuple-element.67), channel_id=1, source_target_pairs={{0,2},{1,3},{2,0},{3,1},{4,6},{5,7},{6,4},{7,5},{8,10},{9,11},{10,... | collective-permute-start | bytes 1572872 | tf_op jit(solution)/shard_map/ppermute | solution.py:285
  68.5 0.3 collective-permute-start.18
  68.8 2.2 %hops_2.1 = (f32[16,128,128]{2,1,0:T(8,128)S(1)}, f32[16,128,128]{2,1,0:T(8,128)S(1)}, f32[128,128]{1,0:T(8,128)S(1)}) custom-call(s32[16]{0:T(128)S(1)} %concatenate.3.refs_0_, s32[256]{0:T(256)S(1)} %select_reduce_fusion.refs_1_, s32[256]{0:T(256)S(1)} %collective-permute-done.refs_5_.refs_2_, bf16[2,144,128,128]{3,2,1,0:T(8,128)(2,1)S(1)} %get-tuple-element.48.refs_3_, ...), custom_call_target="tpu_custom_call" | custom-call | flops 1 | bytes 1 | tf_op jit(solution)/shard_map/hops_2/pallas_call | solution.py:192
  71.0 5.1 %collective-permute-done.16.refs_6_ = bf16[16,128,128]{2,1,0:T(8,128)(2,1)S(1)} collective-permute-done((bf16[16,128,128]{2,1,0:T(8,128)(2,1)S(1)}, bf16[16,128,128]{2,1,0:T(8,128)(2,1)S(1)}, u32[]{:S(2)}, u32[]{:S(2)}) %collective-permute-start.16) | collective-permute-done | bytes 524320 | tf_op jit(solution)/shard_map/ppermute | solution.py:285
  76.1 1.3 %collective-permute-done.17.refs_7_ = bf16[16,128,128]{2,1,0:T(8,128)(2,1)S(1)} collective-permute-done((bf16[16,128,128]{2,1,0:T(8,128)(2,1)S(1)}, bf16[16,128,128]{2,1,0:T(8,128)(2,1)S(1)}, u32[]{:S(2)}, u32[]{:S(2)}) %collective-permute-start.17) | collective-permute-done | bytes 524320 | tf_op jit(solution)/shard_map/ppermute | solution.py:285
  77.4 1.1 %collective-permute-done.18.refs_8_ = bf16[16,128,128]{2,1,0:T(8,128)(2,1)S(1)} collective-permute-done((bf16[16,128,128]{2,1,0:T(8,128)(2,1)S(1)}, bf16[16,128,128]{2,1,0:T(8,128)(2,1)S(1)}, u32[]{:S(2)}, u32[]{:S(2)}) %collective-permute-start.18) | collective-permute-done | bytes 524320 | tf_op jit(solution)/shard_map/ppermute | solution.py:285
  78.5 2.0 %hops_3.1 = (f32[16,128,128]{2,1,0:T(8,128)S(1)}, f32[16,128,128]{2,1,0:T(8,128)S(1)}, f32[32,128]{1,0:T(8,128)S(1)}) custom-call(s32[16]{0:T(128)S(1)} %concatenate.3.refs_0_, s32[256]{0:T(256)S(1)} %select_reduce_fusion.refs_1_, s32[256]{0:T(256)S(1)} %collective-permute-done.refs_5_.refs_2_, bf16[2,144,128,128]{3,2,1,0:T(8,128)(2,1)S(1)} %get-tuple-element.48.refs_3_, ...), custom_call_target="tpu_custom_call" | custom-call | flops 1 | bytes 1 | tf_op jit(solution)/shard_map/hops_3/pallas_call | solution.py:192
  80.5 0.1 collective-permute-start.19
  80.5 8.9 %all_to_all.11 = f32[32,1,128]{2,1,0:T(1,128)S(1)} all-to-all(f32[32,1,128]{2,1,0:T(1,128)S(1)} %bitcast.12), channel_id=1, replica_groups=mesh['groups'=1,'sector'=32] {'sector'}, dimensions={0} | all-to-all | bytes 32768 | tf_op jit(solution)/shard_map/all_to_all | solution.py:355
  89.4 0.0 collective-permute-done.19.theirs
  89.4 1.3 %finish.1 = (bf16[16,128,128]{2,1,0:T(8,128)(2,1)}, bf16[16,128,128]{2,1,0:T(8,128)(2,1)}, f32[1]{0:T(128)}) custom-call(f32[32,128]{1,0:T(8,128)S(1)} %bitcast.11, bf16[16,128,128]{2,1,0:T(8,128)(2,1)S(1)} %copy-done.1, f32[16,128,128]{2,1,0:T(8,128)S(1)} %get-tuple-element.71.mine, f32[16,128,128]{2,1,0:T(8,128)S(1)} %collective-permute-done.19.theirs), custom_call_target="tpu_custom_call" | custom-call | tf_op jit(solution)/shard_map/finish/pallas_call | solution.py:253
  (7 shorter events, 0.1 us)
Async XLA Ops:
  0.6 17.2 %collective-permute-start.4 = (bf16[16,128,128]{2,1,0:T(8,128)(2,1)}, bf16[16,128,128]{2,1,0:T(8,128)(2,1)S(1)}, u32[]{:S(2)}, u32[]{:S(2)}) collective-permute-start(bf16[16,128,128]{2,1,0:T(8,128)(2,1)} %psi.1), channel_id=1, source_target_pairs={{0,8},{1,9},{2,10},{3,11},{4,12},{5,13},{6,14},{7,15},{8,0},{9,1},... | collective-permute-start | bytes 1572872 | tf_op jit(solution)/shard_map/ppermute | solution.py:285
  3.7 14.1 %collective-permute-start.3 = (bf16[16,128,128]{2,1,0:T(8,128)(2,1)}, bf16[16,128,128]{2,1,0:T(8,128)(2,1)S(1)}, u32[]{:S(2)}, u32[]{:S(2)}) collective-permute-start(bf16[16,128,128]{2,1,0:T(8,128)(2,1)} %psi.1), channel_id=1, source_target_pairs={{0,1},{1,0},{2,3},{3,2},{4,5},{5,4},{6,7},{7,6},{8,16},{9,17},{10,... | collective-permute-start | bytes 1572872 | tf_op jit(solution)/shard_map/ppermute | solution.py:292
  3.7 14.7 %collective-permute-start.2 = (bf16[16,128,128]{2,1,0:T(8,128)(2,1)}, bf16[16,128,128]{2,1,0:T(8,128)(2,1)}, u32[]{:S(2)}, u32[]{:S(2)}) collective-permute-start(bf16[16,128,128]{2,1,0:T(8,128)(2,1)} %psi.1), channel_id=1, source_target_pairs={{0,4},{1,5},{2,6},{3,7},{4,0},{5,1},{6,2},{7,3},{8,12},{9,13},{10,... | collective-permute-start | bytes 1572872 | tf_op jit(solution)/shard_map/ppermute | solution.py:285
  5.2 14.3 %collective-permute-start.1 = (bf16[16,128,128]{2,1,0:T(8,128)(2,1)}, bf16[16,128,128]{2,1,0:T(8,128)(2,1)S(1)}, u32[]{:S(2)}, u32[]{:S(2)}) collective-permute-start(bf16[16,128,128]{2,1,0:T(8,128)(2,1)} %psi.1), channel_id=1, source_target_pairs={{0,2},{1,3},{2,0},{3,1},{4,6},{5,7},{6,4},{7,5},{8,10},{9,11},{10,... | collective-permute-start | bytes 1572872 | tf_op jit(solution)/shard_map/ppermute | solution.py:285
  8.6 9.2 %collective-permute-start = (s32[256]{0:T(256)S(1)}, s32[256]{0:T(256)S(1)}, u32[]{:S(2)}, u32[]{:S(2)}) collective-permute-start(s32[256]{0:T(256)S(1)} %select_reduce_fusion.refs_1_), channel_id=1, source_target_pairs={{0,1},{1,0},{2,3},{3,2},{4,5},{5,4},{6,7},{7,6},{8,9},{9,8},{10,11... | collective-permute-start | bytes 3080 | tf_op jit(solution)/shard_map/ppermute | solution.py:285
  8.7 1.0 %copy-start = (bf16[16,128,128]{2,1,0:T(8,128)(2,1)S(1)}, bf16[16,128,128]{2,1,0:T(8,128)(2,1)}, u32[]{:S(2)}) copy-start(bf16[16,128,128]{2,1,0:T(8,128)(2,1)} %psi.1) | copy-start | bytes 1572868
  17.8 5.3 %copy-start.4 = (f32[16,128,128]{2,1,0:T(8,128)}, f32[16,128,128]{2,1,0:T(8,128)S(1)}, u32[]{:S(2)}) copy-start(f32[16,128,128]{2,1,0:T(8,128)S(1)} %get-tuple-element.44.refs_5_) | copy-start | bytes 3145732
  19.6 18.6 %copy-start.2 = (bf16[16,128,128]{2,1,0:T(8,128)(2,1)}, bf16[16,128,128]{2,1,0:T(8,128)(2,1)S(1)}, u32[]{:S(2)}) copy-start(bf16[16,128,128]{2,1,0:T(8,128)(2,1)S(1)} %get-tuple-element.41.refs_9_) | copy-start | bytes 1572868
  19.6 20.0 %copy-start.1 = (bf16[16,128,128]{2,1,0:T(8,128)(2,1)S(1)}, bf16[16,128,128]{2,1,0:T(8,128)(2,1)}, u32[]{:S(2)}) copy-start(bf16[16,128,128]{2,1,0:T(8,128)(2,1)} %psi.1) | copy-start | bytes 1572868
  19.6 17.4 %collective-permute-start.5 = (bf16[144,128,128]{2,1,0:T(8,128)(2,1)}, bf16[144,128,128]{2,1,0:T(8,128)(2,1)}, u32[]{:S(2)}, u32[]{:S(2)}) collective-permute-start(bf16[144,128,128]{2,1,0:T(8,128)(2,1)} %get-tuple-element.39.refs_3_), channel_id=1, source_target_pairs={{0,1},{1,0},{2,3},{3,2},{4,5},{5,4},{6,7},{7,6},{8,9},{9,8},{10,11... | collective-permute-start | bytes 14155784 | tf_op jit(solution)/shard_map/ppermute | solution.py:285
  19.7 14.6 %collective-permute-start.9 = (bf16[16,128,128]{2,1,0:T(8,128)(2,1)S(1)}, bf16[16,128,128]{2,1,0:T(8,128)(2,1)}, u32[]{:S(2)}, u32[]{:S(2)}) collective-permute-start(bf16[16,128,128]{2,1,0:T(8,128)(2,1)S(1)} %get-tuple-element.40.refs_1_), channel_id=1, source_target_pairs={{0,8},{1,9},{2,10},{3,11},{4,12},{5,13},{6,14},{7,15},{8,0},{9,1},... | collective-permute-start | bytes 1572872 | tf_op jit(solution)/shard_map/ppermute | solution.py:285
  21.6 14.2 %collective-permute-start.8 = (bf16[16,128,128]{2,1,0:T(8,128)(2,1)}, bf16[16,128,128]{2,1,0:T(8,128)(2,1)S(1)}, u32[]{:S(2)}, u32[]{:S(2)}) collective-permute-start(bf16[16,128,128]{2,1,0:T(8,128)(2,1)} %get-tuple-element.42.refs_8_), channel_id=1, source_target_pairs={{0,2},{1,3},{2,0},{3,1},{4,6},{5,7},{6,4},{7,5},{8,10},{9,11},{10,... | collective-permute-start | bytes 1572872 | tf_op jit(solution)/shard_map/ppermute | solution.py:285
  23.1 13.8 %collective-permute-start.7 = (bf16[16,128,128]{2,1,0:T(8,128)(2,1)S(1)}, bf16[16,128,128]{2,1,0:T(8,128)(2,1)}, u32[]{:S(2)}, u32[]{:S(2)}) collective-permute-start(bf16[16,128,128]{2,1,0:T(8,128)(2,1)S(1)} %get-tuple-element.41.refs_9_), channel_id=1, source_target_pairs={{0,4},{1,5},{2,6},{3,7},{4,0},{5,1},{6,2},{7,3},{8,12},{9,13},{10,... | collective-permute-start | bytes 1572872 | tf_op jit(solution)/shard_map/ppermute | solution.py:285
  23.6 13.3 %collective-permute-start.6 = (bf16[16,128,128]{2,1,0:T(8,128)(2,1)S(1)}, bf16[16,128,128]{2,1,0:T(8,128)(2,1)S(1)}, u32[]{:S(2)}, u32[]{:S(2)}) collective-permute-start(bf16[16,128,128]{2,1,0:T(8,128)(2,1)S(1)} %get-tuple-element.41.refs_9_), channel_id=1, source_target_pairs={{0,1},{1,0},{2,3},{3,2},{4,5},{5,4},{6,7},{7,6},{8,16},{9,17},{10,... | collective-permute-start | bytes 1572872 | tf_op jit(solution)/shard_map/ppermute | solution.py:292
  38.1 13.0 %collective-permute-start.12 = (bf16[16,128,128]{2,1,0:T(8,128)(2,1)S(1)}, bf16[16,128,128]{2,1,0:T(8,128)(2,1)}, u32[]{:S(2)}, u32[]{:S(2)}) collective-permute-start(bf16[16,128,128]{2,1,0:T(8,128)(2,1)S(1)} %get-tuple-element.52.refs_0_), channel_id=1, source_target_pairs={{0,8},{1,9},{2,10},{3,11},{4,12},{5,13},{6,14},{7,15},{8,0},{9,1},... | collective-permute-start | bytes 1572872 | tf_op jit(solution)/shard_map/ppermute | solution.py:285
  38.2 13.0 %collective-permute-start.11 = (bf16[16,128,128]{2,1,0:T(8,128)(2,1)S(1)}, bf16[16,128,128]{2,1,0:T(8,128)(2,1)}, u32[]{:S(2)}, u32[]{:S(2)}) collective-permute-start(bf16[16,128,128]{2,1,0:T(8,128)(2,1)S(1)} %get-tuple-element.51.refs_6_), channel_id=1, source_target_pairs={{0,2},{1,3},{2,0},{3,1},{4,6},{5,7},{6,4},{7,5},{8,10},{9,11},{10,... | collective-permute-start | bytes 1572872 | tf_op jit(solution)/shard_map/ppermute | solution.py:285
  38.8 12.8 %collective-permute-start.10 = (bf16[16,128,128]{2,1,0:T(8,128)(2,1)S(1)}, bf16[16,128,128]{2,1,0:T(8,128)(2,1)S(1)}, u32[]{:S(2)}, u32[]{:S(2)}) collective-permute-start(bf16[16,128,128]{2,1,0:T(8,128)(2,1)S(1)} %get-tuple-element.51.refs_6_), channel_id=1, source_target_pairs={{0,4},{1,5},{2,6},{3,7},{4,0},{5,1},{6,2},{7,3},{8,12},{9,13},{10,... | collective-permute-start | bytes 1572872 | tf_op jit(solution)/shard_map/ppermute | solution.py:285
  39.6 1.0 %copy-start.3 = (bf16[16,128,128]{2,1,0:T(8,128)(2,1)S(1)}, bf16[16,128,128]{2,1,0:T(8,128)(2,1)}, u32[]{:S(2)}) copy-start(bf16[16,128,128]{2,1,0:T(8,128)(2,1)} %copy-done.2) | copy-start | bytes 1572868
  40.7 1.2 %copy-start.5 = (f32[16,128,128]{2,1,0:T(8,128)S(1)}, f32[16,128,128]{2,1,0:T(8,128)}, u32[]{:S(2)}) copy-start(f32[16,128,128]{2,1,0:T(8,128)} %copy-done.4) | copy-start | bytes 3145732
  41.9 13.2 %copy-start.6 = (f32[16]{0:T(128)S(1)}, f32[16]{0:T(128)}, u32[]{:S(2)}) copy-start(f32[16]{0:T(128)} %refs_10_.1) | copy-start | bytes 196
  52.8 12.1 %collective-permute-start.13 = (bf16[16,128,128]{2,1,0:T(8,128)(2,1)S(1)}, bf16[16,128,128]{2,1,0:T(8,128)(2,1)S(1)}, u32[]{:S(2)}, u32[]{:S(2)}) collective-permute-start(bf16[16,128,128]{2,1,0:T(8,128)(2,1)S(1)} %get-tuple-element.59), channel_id=1, source_target_pairs={{0,8},{1,9},{2,10},{3,11},{4,12},{5,13},{6,14},{7,15},{8,0},{9,1},... | collective-permute-start | bytes 1572872 | tf_op jit(solution)/shard_map/ppermute | solution.py:285
  53.4 11.5 %collective-permute-start.15 = (bf16[16,128,128]{2,1,0:T(8,128)(2,1)S(1)}, bf16[16,128,128]{2,1,0:T(8,128)(2,1)S(1)}, u32[]{:S(2)}, u32[]{:S(2)}) collective-permute-start(bf16[16,128,128]{2,1,0:T(8,128)(2,1)S(1)} %get-tuple-element.56.refs_9_), channel_id=1, source_target_pairs={{0,2},{1,3},{2,0},{3,1},{4,6},{5,7},{6,4},{7,5},{8,10},{9,11},{10,... | collective-permute-start | bytes 1572872 | tf_op jit(solution)/shard_map/ppermute | solution.py:285
  54.6 11.0 %collective-permute-start.14 = (bf16[16,128,128]{2,1,0:T(8,128)(2,1)S(1)}, bf16[16,128,128]{2,1,0:T(8,128)(2,1)S(1)}, u32[]{:S(2)}, u32[]{:S(2)}) collective-permute-start(bf16[16,128,128]{2,1,0:T(8,128)(2,1)S(1)} %get-tuple-element.56.refs_9_), channel_id=1, source_target_pairs={{0,4},{1,5},{2,6},{3,7},{4,0},{5,1},{6,2},{7,3},{8,12},{9,13},{10,... | collective-permute-start | bytes 1572872 | tf_op jit(solution)/shard_map/ppermute | solution.py:285
  65.6 10.5 %collective-permute-start.16 = (bf16[16,128,128]{2,1,0:T(8,128)(2,1)S(1)}, bf16[16,128,128]{2,1,0:T(8,128)(2,1)S(1)}, u32[]{:S(2)}, u32[]{:S(2)}) collective-permute-start(bf16[16,128,128]{2,1,0:T(8,128)(2,1)S(1)} %get-tuple-element.66), channel_id=1, source_target_pairs={{0,8},{1,9},{2,10},{3,11},{4,12},{5,13},{6,14},{7,15},{8,0},{9,1},... | collective-permute-start | bytes 1572872 | tf_op jit(solution)/shard_map/ppermute | solution.py:285
  67.4 10.0 %collective-permute-start.17 = (bf16[16,128,128]{2,1,0:T(8,128)(2,1)S(1)}, bf16[16,128,128]{2,1,0:T(8,128)(2,1)S(1)}, u32[]{:S(2)}, u32[]{:S(2)}) collective-permute-start(bf16[16,128,128]{2,1,0:T(8,128)(2,1)S(1)} %get-tuple-element.67), channel_id=1, source_target_pairs={{0,2},{1,3},{2,0},{3,1},{4,6},{5,7},{6,4},{7,5},{8,10},{9,11},{10,... | collective-permute-start | bytes 1572872 | tf_op jit(solution)/shard_map/ppermute | solution.py:285
  68.5 10.0 %collective-permute-start.18 = (bf16[16,128,128]{2,1,0:T(8,128)(2,1)S(1)}, bf16[16,128,128]{2,1,0:T(8,128)(2,1)S(1)}, u32[]{:S(2)}, u32[]{:S(2)}) collective-permute-start(bf16[16,128,128]{2,1,0:T(8,128)(2,1)S(1)} %get-tuple-element.62.refs_7_), channel_id=1, source_target_pairs={{0,4},{1,5},{2,6},{3,7},{4,0},{5,1},{6,2},{7,3},{8,12},{9,13},{10,... | collective-permute-start | bytes 1572872 | tf_op jit(solution)/shard_map/ppermute | solution.py:285
  80.5 9.0 %collective-permute-start.19 = (f32[16,128,128]{2,1,0:T(8,128)S(1)}, f32[16,128,128]{2,1,0:T(8,128)S(1)}, u32[]{:S(2)}, u32[]{:S(2)}) collective-permute-start(f32[16,128,128]{2,1,0:T(8,128)S(1)} %get-tuple-element.72), channel_id=1, source_target_pairs={{0,1},{1,0},{2,3},{3,2},{4,5},{5,4},{6,7},{7,6},{8,9},{9,8},{10,11... | collective-permute-start | bytes 3145736 | tf_op jit(solution)/shard_map/ppermute | solution.py:285

commit v6 on v5

--- a/solution.py
+++ b/solution.py
@@ -332,7 +332,8 @@
     held["outer"] = swap(held["middle"], z)
     held["middle_2"] = swap_middle(held[1, 0])
     held["env_sib"] = swap(held["env"], core)
-    hold(["env_sib", "middle", "middle_2", (1, y), (0, xy)], held["outer"], move=(5, 1), flag=outer)
+    hold(["middle"], held["outer"], move=(1, 0), flag=outer)
+    hold(["env_sib", "middle", "middle_2", (1, y), (0, xy)])
 
     held[2, 0] = held["middle"]
     held[2, x], held[2, y] = swap(held[2, 0], x), swap(held[2, 0], y)

time: 91.2 us -> 90.8 us (level)
  waiting for transfers between devices: 33.1 us -> 29.5 us
  starting transfers between devices: 17.2 us -> 19.3 us
  blocking collectives: 8.89 us -> 9.9 us
    ppermute x18, waiting for transfers between devices: 33.1 us -> 29.5 us  [swap(): return lax.ppermute(value, 'sector', [(i, i ^ mask) for i in range(owners)])]
    ppermute x18, starting transfers between devices: 17.2 us -> 19.3 us  [swap(): return lax.ppermute(value, 'sector', [(i, i ^ mask) for i in range(owners)])]
    all_to_all x1, blocking collectives: 8.89 us -> 9.9 us  [spread_everywhere(): sums = lax.all_to_all(sums, 'sector', 0, 0, tiled=True)]
    pallas_call x4 -> x5, Pallas kernels: 2.33 us -> 2.36 us  [hold_until(): pl.pallas_call(functools.partial(hold_kernel, count, move), out_shape=[ja...]
  transfers between devices with their start and end apart: 20 -> 20, of which waited for: 14 -> 13; matrix products, arithmetic and copies ran while one was open for 2% -> 2% of each run, Pallas kernels for 22% -> 23%
where the time goes in v6:
time: 90.8 us; the launch traced here: 90.3 us
  waiting for transfers between devices  29.5 us (32%)
  Pallas kernels  25.5 us (28%)
  starting transfers between devices  19.3 us (21%)
  blocking collectives  9.9 us (11%)
  local copies, waits for them, and re-layouts  4.96 us (5%)
    ppermute x18, waiting for transfers between devices, swap(): return lax.ppermute(value, 'sector', [(i, i ^ mask) for i in range(owners)])  29.5 us
    ppermute x18, starting transfers between devices, swap(): return lax.ppermute(value, 'sector', [(i, i ^ mask) for i in range(owners)])  19.3 us
    pallas_call x4, Pallas kernels, hop_call(): pl.pallas_call(functools.partial(hop_kernel, base, count, first, bool(ons...  13.8 us
    all_to_all x1, blocking collectives, spread_everywhere(): sums = lax.all_to_all(sums, 'sector', 0, 0, tiled=True)  9.9 us
    pallas_call x1, Pallas kernels, local_call(): pl.pallas_call(local_kernel, out_shape=(jax.ShapeDtypeStruct((sec, size,...  8.05 us
    unnamed x14, local copies, waits for them, and re-layouts  3.32 us
    pallas_call x5, Pallas kernels, hold_until(): pl.pallas_call(functools.partial(hold_kernel, count, move), out_shape=[ja...  2.36 us
  transfers between devices with their start and end apart: 20, of which 13 were waited for; matrix products, arithmetic and copies ran while one was open for 2% of the time, Pallas kernels for 23%

profile of v6, /device:TPU:0, one launch (start us, length us, event | category | flops | bytes accessed | tf_op | source)
XLA Modules:
  0.0 90.3 jit_solution(7456017707339867313)
XLA Ops:
  0.6 3.1 %collective-permute-start.4 = (bf16[16,128,128]{2,1,0:T(8,128)(2,1)}, bf16[16,128,128]{2,1,0:T(8,128)(2,1)S(1)}, u32[]{:S(2)}, u32[]{:S(2)}) collective-permute-start(bf16[16,128,128]{2,1,0:T(8,128)(2,1)} %psi.1), channel_id=1, source_target_pairs={{0,8},{1,9},{2,10},{3,11},{4,12},{5,13},{6,14},{7,15},{8,0},{9,1},... | collective-permute-start | bytes 1572872 | tf_op jit(solution)/shard_map/ppermute | solution.py:285
  3.7 0.0 collective-permute-start.3
  3.7 1.5 %collective-permute-start.2 = (bf16[16,128,128]{2,1,0:T(8,128)(2,1)}, bf16[16,128,128]{2,1,0:T(8,128)(2,1)}, u32[]{:S(2)}, u32[]{:S(2)}) collective-permute-start(bf16[16,128,128]{2,1,0:T(8,128)(2,1)} %psi.1), channel_id=1, source_target_pairs={{0,4},{1,5},{2,6},{3,7},{4,0},{5,1},{6,2},{7,3},{8,12},{9,13},{10,... | collective-permute-start | bytes 1572872 | tf_op jit(solution)/shard_map/ppermute | solution.py:285
  5.2 1.5 %collective-permute-start.1 = (bf16[16,128,128]{2,1,0:T(8,128)(2,1)}, bf16[16,128,128]{2,1,0:T(8,128)(2,1)S(1)}, u32[]{:S(2)}, u32[]{:S(2)}) collective-permute-start(bf16[16,128,128]{2,1,0:T(8,128)(2,1)} %psi.1), channel_id=1, source_target_pairs={{0,2},{1,3},{2,0},{3,1},{4,6},{5,7},{6,4},{7,5},{8,10},{9,11},{10,... | collective-permute-start | bytes 1572872 | tf_op jit(solution)/shard_map/ppermute | solution.py:285
  6.7 0.8 reshape.95
  7.5 0.8 reshape.96
  8.3 0.2 convert_reduce_fusion
  8.5 0.1 select_reduce_fusion.refs_1_
  8.6 0.1 collective-permute-start
  8.7 0.0 copy-start
  8.7 1.0 %copy-done = bf16[16,128,128]{2,1,0:T(8,128)(2,1)S(1)} copy-done((bf16[16,128,128]{2,1,0:T(8,128)(2,1)S(1)}, bf16[16,128,128]{2,1,0:T(8,128)(2,1)}, u32[]{:S(2)}) %copy-start) | copy-done | bytes 524312
  9.7 8.0 %local_channels.1 = (f32[16,128,128]{2,1,0:T(8,128)S(1)}, f32[128,128]{1,0:T(8,128)S(1)}, bf16[144,128,128]{2,1,0:T(8,128)(2,1)}) custom-call(bf16[4,4,128,128]{3,2,1,0:T(8,128)(2,1)S(1)} %bitcast.10, bf16[4,32,128,128]{3,2,1,0:T(8,128)(2,1)} %right.1, bf16[4,32,128,128]{3,2,1,0:T(8,128)(2,1)} %left.1), custom_call_target="tpu_custom_call" | custom-call | flops 1 | bytes 1 | tf_op jit(solution)/shard_map/local_channels/pallas_call | solution.py:107
  17.8 0.0 copy-start.4
  17.8 0.0 collective-permute-done.refs_5_.refs_2_
  17.8 0.0 collective-permute-done.4.refs_3_
  17.8 0.0 collective-permute-done.3.refs_2_
  17.8 0.5 collective-permute-done.2.refs_1_
  18.4 1.1 %collective-permute-done.1.refs_0_ = bf16[16,128,128]{2,1,0:T(8,128)(2,1)S(1)} collective-permute-done((bf16[16,128,128]{2,1,0:T(8,128)(2,1)}, bf16[16,128,128]{2,1,0:T(8,128)(2,1)S(1)}, u32[]{:S(2)}, u32[]{:S(2)}) %collective-permute-start.1) | collective-permute-done | bytes 524320 | tf_op jit(solution)/shard_map/ppermute | solution.py:285
  19.6 0.0 copy-start.2
  19.6 0.0 copy-start.1
  19.6 0.1 collective-permute-start.5
  19.7 2.0 %collective-permute-start.6 = (bf16[16,128,128]{2,1,0:T(8,128)(2,1)S(1)}, bf16[16,128,128]{2,1,0:T(8,128)(2,1)}, u32[]{:S(2)}, u32[]{:S(2)}) collective-permute-start(bf16[16,128,128]{2,1,0:T(8,128)(2,1)S(1)} %get-tuple-element.40.refs_0_), channel_id=1, source_target_pairs={{0,8},{1,9},{2,10},{3,11},{4,12},{5,13},{6,14},{7,15},{8,0},{9,1},... | collective-permute-start | bytes 1572872 | tf_op jit(solution)/shard_map/ppermute | solution.py:285
  21.6 1.5 %collective-permute-start.9 = (bf16[16,128,128]{2,1,0:T(8,128)(2,1)}, bf16[16,128,128]{2,1,0:T(8,128)(2,1)S(1)}, u32[]{:S(2)}, u32[]{:S(2)}) collective-permute-start(bf16[16,128,128]{2,1,0:T(8,128)(2,1)} %get-tuple-element.42.refs_8_), channel_id=1, source_target_pairs={{0,2},{1,3},{2,0},{3,1},{4,6},{5,7},{6,4},{7,5},{8,10},{9,11},{10,... | collective-permute-start | bytes 1572872 | tf_op jit(solution)/shard_map/ppermute | solution.py:285
  23.1 0.0 copy-done.4
  23.1 0.5 collective-permute-start.8
  23.6 0.0 collective-permute-start.7
  23.6 10.6 %collective-permute-done.6.refs_1_ = bf16[16,128,128]{2,1,0:T(8,128)(2,1)} collective-permute-done((bf16[16,128,128]{2,1,0:T(8,128)(2,1)S(1)}, bf16[16,128,128]{2,1,0:T(8,128)(2,1)}, u32[]{:S(2)}, u32[]{:S(2)}) %collective-permute-start.6) | collective-permute-done | bytes 524320 | tf_op jit(solution)/shard_map/ppermute | solution.py:285
  34.3 1.1 %hold.6.refs_1_ = bf16[16,128,128]{2,1,0:T(8,128)(2,1)S(1)} custom-call(bf16[16,128,128]{2,1,0:T(8,128)(2,1)S(1)} %get-tuple-element.40.refs_0_, bf16[16,128,128]{2,1,0:T(8,128)(2,1)} %collective-permute-done.6.refs_1_, s32[1]{0:T(128)} %bitcast.5.refs_2_.refs_6_), custom_call_target="tpu_custom_call", output_to_operand_aliasing={{}: (0, {})} | custom-call | flops 1 | bytes 1 | tf_op jit(solution)/shard_map/hold/pallas_call | solution.py:227
  35.4 0.4 collective-permute-done.9.refs_4_
  35.8 1.1 %collective-permute-done.8.refs_3_ = bf16[16,128,128]{2,1,0:T(8,128)(2,1)} collective-permute-done((bf16[16,128,128]{2,1,0:T(8,128)(2,1)S(1)}, bf16[16,128,128]{2,1,0:T(8,128)(2,1)}, u32[]{:S(2)}, u32[]{:S(2)}) %collective-permute-start.8) | collective-permute-done | bytes 524320 | tf_op jit(solution)/shard_map/ppermute | solution.py:285
  37.0 0.0 collective-permute-done.7.refs_2_
  37.0 0.0 collective-permute-done.5.refs_0_
  37.0 0.5 collective-permute-start.12
  37.5 0.0 copy-done.2
  37.5 0.5 collective-permute-start.11
  38.0 1.5 %collective-permute-start.10 = (bf16[16,128,128]{2,1,0:T(8,128)(2,1)S(1)}, bf16[16,128,128]{2,1,0:T(8,128)(2,1)S(1)}, u32[]{:S(2)}, u32[]{:S(2)}) collective-permute-start(bf16[16,128,128]{2,1,0:T(8,128)(2,1)S(1)} %get-tuple-element.51.refs_6_), channel_id=1, source_target_pairs={{0,4},{1,5},{2,6},{3,7},{4,0},{5,1},{6,2},{7,3},{8,12},{9,13},{10,... | collective-permute-start | bytes 1572872 | tf_op jit(solution)/shard_map/ppermute | solution.py:285
  39.5 0.1 concatenate.3.refs_0_
  39.6 0.0 copy-start.3
  39.6 1.0 %copy-done.3 = bf16[16,128,128]{2,1,0:T(8,128)(2,1)S(1)} copy-done((bf16[16,128,128]{2,1,0:T(8,128)(2,1)S(1)}, bf16[16,128,128]{2,1,0:T(8,128)(2,1)}, u32[]{:S(2)}) %copy-start.3) | copy-done | bytes 524312
  40.7 1.2 %copy-done.5 = f32[16,128,128]{2,1,0:T(8,128)S(1)} copy-done((f32[16,128,128]{2,1,0:T(8,128)S(1)}, f32[16,128,128]{2,1,0:T(8,128)}, u32[]{:S(2)}) %copy-start.5) | copy-done | bytes 1048600
  41.9 7.0 %hops_0.1 = (f32[16,128,128]{2,1,0:T(8,128)S(1)}, f32[16,128,128]{2,1,0:T(8,128)S(1)}, f32[8,128]{1,0:T(8,128)S(1)}, bf16[2,144,128,128]{3,2,1,0:T(8,128)(2,1)S(1)}) custom-call(s32[16]{0:T(128)S(1)} %concatenate.3.refs_0_, s32[256]{0:T(256)S(1)} %select_reduce_fusion.refs_1_, s32[256]{0:T(256)S(1)} %collective-permute-done.refs_5_.refs_2_, ...), custom_call_target="tpu_custom_call" | custom-call | flops 1 | bytes 1 | tf_op jit(solution)/shard_map/hops_0/pallas_call | solution.py:192
  48.9 1.2 %collective-permute-done.12.refs_4_ = bf16[16,128,128]{2,1,0:T(8,128)(2,1)} collective-permute-done((bf16[16,128,128]{2,1,0:T(8,128)(2,1)S(1)}, bf16[16,128,128]{2,1,0:T(8,128)(2,1)}, u32[]{:S(2)}, u32[]{:S(2)}) %collective-permute-start.12) | collective-permute-done | bytes 524320 | tf_op jit(solution)/shard_map/ppermute | solution.py:285
  50.0 0.2 collective-permute-done.11.refs_3_
  50.2 0.4 collective-permute-done.10.refs_2_
  50.6 1.1 %hold.8 = (bf16[16,128,128]{2,1,0:T(8,128)(2,1)S(1)}, bf16[16,128,128]{2,1,0:T(8,128)(2,1)S(1)}, bf16[16,128,128]{2,1,0:T(8,128)(2,1)S(1)}, bf16[16,128,128]{2,1,0:T(8,128)(2,1)}) custom-call(bf16[16,128,128]{2,1,0:T(8,128)(2,1)S(1)} %get-tuple-element.52.refs_0_, ...), custom_call_target="tpu_custom_call", output_to_operand_aliasing={{0}: (0, {}), {1}: (1, {}), {2}: (2, {}), {3}: (3, {})} | custom-call | flops 1 | bytes 1 | tf_op jit(solution)/shard_map/hold/pallas_call | solution.py:227
  51.8 0.5 collective-permute-start.13
  52.3 1.2 %collective-permute-start.15 = (bf16[16,128,128]{2,1,0:T(8,128)(2,1)S(1)}, bf16[16,128,128]{2,1,0:T(8,128)(2,1)S(1)}, u32[]{:S(2)}, u32[]{:S(2)}) collective-permute-start(bf16[16,128,128]{2,1,0:T(8,128)(2,1)S(1)} %get-tuple-element.56.refs_9_), channel_id=1, source_target_pairs={{0,2},{1,3},{2,0},{3,1},{4,6},{5,7},{6,4},{7,5},{8,10},{9,11},{10,... | collective-permute-start | bytes 1572872 | tf_op jit(solution)/shard_map/ppermute | solution.py:285
  53.5 1.0 %collective-permute-start.14 = (bf16[16,128,128]{2,1,0:T(8,128)(2,1)S(1)}, bf16[16,128,128]{2,1,0:T(8,128)(2,1)S(1)}, u32[]{:S(2)}, u32[]{:S(2)}) collective-permute-start(bf16[16,128,128]{2,1,0:T(8,128)(2,1)S(1)} %get-tuple-element.56.refs_9_), channel_id=1, source_target_pairs={{0,4},{1,5},{2,6},{3,7},{4,0},{5,1},{6,2},{7,3},{8,12},{9,13},{10,... | collective-permute-start | bytes 1572872 | tf_op jit(solution)/shard_map/ppermute | solution.py:285
  54.5 2.7 %hops_1.1 = (f32[16,128,128]{2,1,0:T(8,128)S(1)}, f32[16,128,128]{2,1,0:T(8,128)S(1)}, f32[8,128]{1,0:T(8,128)S(1)}) custom-call(s32[16]{0:T(128)S(1)} %concatenate.3.refs_0_, s32[256]{0:T(256)S(1)} %select_reduce_fusion.refs_1_, s32[256]{0:T(256)S(1)} %collective-permute-done.refs_5_.refs_2_, bf16[2,144,128,128]{3,2,1,0:T(8,128)(2,1)S(1)} %get-tuple-element.48.refs_3_, ...), custom_call_target="tpu_custom_call" | custom-call | flops 1 | bytes 1 | tf_op jit(solution)/shard_map/hops_1/pallas_call | solution.py:192
  57.2 6.6 %collective-permute-done.13.refs_0_ = bf16[16,128,128]{2,1,0:T(8,128)(2,1)S(1)} collective-permute-done((bf16[16,128,128]{2,1,0:T(8,128)(2,1)S(1)}, bf16[16,128,128]{2,1,0:T(8,128)(2,1)S(1)}, u32[]{:S(2)}, u32[]{:S(2)}) %collective-permute-start.13) | collective-permute-done | bytes 524320 | tf_op jit(solution)/shard_map/ppermute | solution.py:285
  63.8 0.0 collective-permute-done.15.refs_4_
  63.8 0.6 collective-permute-done.14.refs_3_
  64.5 1.7 %collective-permute-start.16 = (bf16[16,128,128]{2,1,0:T(8,128)(2,1)S(1)}, bf16[16,128,128]{2,1,0:T(8,128)(2,1)S(1)}, u32[]{:S(2)}, u32[]{:S(2)}) collective-permute-start(bf16[16,128,128]{2,1,0:T(8,128)(2,1)S(1)} %get-tuple-element.66), channel_id=1, source_target_pairs={{0,8},{1,9},{2,10},{3,11},{4,12},{5,13},{6,14},{7,15},{8,0},{9,1},... | collective-permute-start | bytes 1572872 | tf_op jit(solution)/shard_map/ppermute | solution.py:285
  66.1 1.3 %collective-permute-start.17 = (bf16[16,128,128]{2,1,0:T(8,128)(2,1)S(1)}, bf16[16,128,128]{2,1,0:T(8,128)(2,1)S(1)}, u32[]{:S(2)}, u32[]{:S(2)}) collective-permute-start(bf16[16,128,128]{2,1,0:T(8,128)(2,1)S(1)} %get-tuple-element.67), channel_id=1, source_target_pairs={{0,2},{1,3},{2,0},{3,1},{4,6},{5,7},{6,4},{7,5},{8,10},{9,11},{10,... | collective-permute-start | bytes 1572872 | tf_op jit(solution)/shard_map/ppermute | solution.py:285
  67.4 0.8 collective-permute-start.18
  68.2 2.2 %hops_2.1 = (f32[16,128,128]{2,1,0:T(8,128)S(1)}, f32[16,128,128]{2,1,0:T(8,128)S(1)}, f32[128,128]{1,0:T(8,128)S(1)}) custom-call(s32[16]{0:T(128)S(1)} %concatenate.3.refs_0_, s32[256]{0:T(256)S(1)} %select_reduce_fusion.refs_1_, s32[256]{0:T(256)S(1)} %collective-permute-done.refs_5_.refs_2_, bf16[2,144,128,128]{3,2,1,0:T(8,128)(2,1)S(1)} %get-tuple-element.48.refs_3_, ...), custom_call_target="tpu_custom_call" | custom-call | flops 1 | bytes 1 | tf_op jit(solution)/shard_map/hops_2/pallas_call | solution.py:192
  70.4 4.5 %collective-permute-done.16.refs_6_ = bf16[16,128,128]{2,1,0:T(8,128)(2,1)S(1)} collective-permute-done((bf16[16,128,128]{2,1,0:T(8,128)(2,1)S(1)}, bf16[16,128,128]{2,1,0:T(8,128)(2,1)S(1)}, u32[]{:S(2)}, u32[]{:S(2)}) %collective-permute-start.16) | collective-permute-done | bytes 524320 | tf_op jit(solution)/shard_map/ppermute | solution.py:285
  74.9 1.0 %collective-permute-done.17.refs_7_ = bf16[16,128,128]{2,1,0:T(8,128)(2,1)S(1)} collective-permute-done((bf16[16,128,128]{2,1,0:T(8,128)(2,1)S(1)}, bf16[16,128,128]{2,1,0:T(8,128)(2,1)S(1)}, u32[]{:S(2)}, u32[]{:S(2)}) %collective-permute-start.17) | collective-permute-done | bytes 524320 | tf_op jit(solution)/shard_map/ppermute | solution.py:285
  75.9 1.1 %collective-permute-done.18.refs_8_ = bf16[16,128,128]{2,1,0:T(8,128)(2,1)S(1)} collective-permute-done((bf16[16,128,128]{2,1,0:T(8,128)(2,1)S(1)}, bf16[16,128,128]{2,1,0:T(8,128)(2,1)S(1)}, u32[]{:S(2)}, u32[]{:S(2)}) %collective-permute-start.18) | collective-permute-done | bytes 524320 | tf_op jit(solution)/shard_map/ppermute | solution.py:285
  77.1 2.0 %hops_3.1 = (f32[16,128,128]{2,1,0:T(8,128)S(1)}, f32[16,128,128]{2,1,0:T(8,128)S(1)}, f32[32,128]{1,0:T(8,128)S(1)}) custom-call(s32[16]{0:T(128)S(1)} %concatenate.3.refs_0_, s32[256]{0:T(256)S(1)} %select_reduce_fusion.refs_1_, s32[256]{0:T(256)S(1)} %collective-permute-done.refs_5_.refs_2_, bf16[2,144,128,128]{3,2,1,0:T(8,128)(2,1)S(1)} %get-tuple-element.48.refs_3_, ...), custom_call_target="tpu_custom_call" | custom-call | flops 1 | bytes 1 | tf_op jit(solution)/shard_map/hops_3/pallas_call | solution.py:192
  79.0 0.1 collective-permute-start.19
  79.1 9.9 %all_to_all.11 = f32[32,1,128]{2,1,0:T(1,128)S(1)} all-to-all(f32[32,1,128]{2,1,0:T(1,128)S(1)} %bitcast.12), channel_id=1, replica_groups=mesh['groups'=1,'sector'=32] {'sector'}, dimensions={0} | all-to-all | bytes 32768 | tf_op jit(solution)/shard_map/all_to_all | solution.py:356
  89.0 0.0 collective-permute-done.19.theirs
  89.0 1.3 %finish.1 = (bf16[16,128,128]{2,1,0:T(8,128)(2,1)}, bf16[16,128,128]{2,1,0:T(8,128)(2,1)}, f32[1]{0:T(128)}) custom-call(f32[32,128]{1,0:T(8,128)S(1)} %bitcast.11, bf16[16,128,128]{2,1,0:T(8,128)(2,1)S(1)} %copy-done.1, f32[16,128,128]{2,1,0:T(8,128)S(1)} %get-tuple-element.71.mine, f32[16,128,128]{2,1,0:T(8,128)S(1)} %collective-permute-done.19.theirs), custom_call_target="tpu_custom_call" | custom-call | tf_op jit(solution)/shard_map/finish/pallas_call | solution.py:253
  (8 shorter events, 0.1 us)
Async XLA Ops:
  0.6 17.2 %collective-permute-start.4 = (bf16[16,128,128]{2,1,0:T(8,128)(2,1)}, bf16[16,128,128]{2,1,0:T(8,128)(2,1)S(1)}, u32[]{:S(2)}, u32[]{:S(2)}) collective-permute-start(bf16[16,128,128]{2,1,0:T(8,128)(2,1)} %psi.1), channel_id=1, source_target_pairs={{0,8},{1,9},{2,10},{3,11},{4,12},{5,13},{6,14},{7,15},{8,0},{9,1},... | collective-permute-start | bytes 1572872 | tf_op jit(solution)/shard_map/ppermute | solution.py:285
  3.7 14.1 %collective-permute-start.3 = (bf16[16,128,128]{2,1,0:T(8,128)(2,1)}, bf16[16,128,128]{2,1,0:T(8,128)(2,1)S(1)}, u32[]{:S(2)}, u32[]{:S(2)}) collective-permute-start(bf16[16,128,128]{2,1,0:T(8,128)(2,1)} %psi.1), channel_id=1, source_target_pairs={{0,1},{1,0},{2,3},{3,2},{4,5},{5,4},{6,7},{7,6},{8,16},{9,17},{10,... | collective-permute-start | bytes 1572872 | tf_op jit(solution)/shard_map/ppermute | solution.py:292
  3.7 14.7 %collective-permute-start.2 = (bf16[16,128,128]{2,1,0:T(8,128)(2,1)}, bf16[16,128,128]{2,1,0:T(8,128)(2,1)}, u32[]{:S(2)}, u32[]{:S(2)}) collective-permute-start(bf16[16,128,128]{2,1,0:T(8,128)(2,1)} %psi.1), channel_id=1, source_target_pairs={{0,4},{1,5},{2,6},{3,7},{4,0},{5,1},{6,2},{7,3},{8,12},{9,13},{10,... | collective-permute-start | bytes 1572872 | tf_op jit(solution)/shard_map/ppermute | solution.py:285
  5.2 14.3 %collective-permute-start.1 = (bf16[16,128,128]{2,1,0:T(8,128)(2,1)}, bf16[16,128,128]{2,1,0:T(8,128)(2,1)S(1)}, u32[]{:S(2)}, u32[]{:S(2)}) collective-permute-start(bf16[16,128,128]{2,1,0:T(8,128)(2,1)} %psi.1), channel_id=1, source_target_pairs={{0,2},{1,3},{2,0},{3,1},{4,6},{5,7},{6,4},{7,5},{8,10},{9,11},{10,... | collective-permute-start | bytes 1572872 | tf_op jit(solution)/shard_map/ppermute | solution.py:285
  8.6 9.2 %collective-permute-start = (s32[256]{0:T(256)S(1)}, s32[256]{0:T(256)S(1)}, u32[]{:S(2)}, u32[]{:S(2)}) collective-permute-start(s32[256]{0:T(256)S(1)} %select_reduce_fusion.refs_1_), channel_id=1, source_target_pairs={{0,1},{1,0},{2,3},{3,2},{4,5},{5,4},{6,7},{7,6},{8,9},{9,8},{10,11... | collective-permute-start | bytes 3080 | tf_op jit(solution)/shard_map/ppermute | solution.py:285
  8.7 1.0 %copy-start = (bf16[16,128,128]{2,1,0:T(8,128)(2,1)S(1)}, bf16[16,128,128]{2,1,0:T(8,128)(2,1)}, u32[]{:S(2)}) copy-start(bf16[16,128,128]{2,1,0:T(8,128)(2,1)} %psi.1) | copy-start | bytes 1572868
  17.8 5.3 %copy-start.4 = (f32[16,128,128]{2,1,0:T(8,128)}, f32[16,128,128]{2,1,0:T(8,128)S(1)}, u32[]{:S(2)}) copy-start(f32[16,128,128]{2,1,0:T(8,128)S(1)} %get-tuple-element.44.refs_5_) | copy-start | bytes 3145732
  19.6 17.9 %copy-start.2 = (bf16[16,128,128]{2,1,0:T(8,128)(2,1)}, bf16[16,128,128]{2,1,0:T(8,128)(2,1)S(1)}, u32[]{:S(2)}) copy-start(bf16[16,128,128]{2,1,0:T(8,128)(2,1)S(1)} %get-tuple-element.41.refs_9_) | copy-start | bytes 1572868
  19.6 20.0 %copy-start.1 = (bf16[16,128,128]{2,1,0:T(8,128)(2,1)S(1)}, bf16[16,128,128]{2,1,0:T(8,128)(2,1)}, u32[]{:S(2)}) copy-start(bf16[16,128,128]{2,1,0:T(8,128)(2,1)} %psi.1) | copy-start | bytes 1572868
  19.6 17.4 %collective-permute-start.5 = (bf16[144,128,128]{2,1,0:T(8,128)(2,1)}, bf16[144,128,128]{2,1,0:T(8,128)(2,1)}, u32[]{:S(2)}, u32[]{:S(2)}) collective-permute-start(bf16[144,128,128]{2,1,0:T(8,128)(2,1)} %get-tuple-element.39.refs_3_), channel_id=1, source_target_pairs={{0,1},{1,0},{2,3},{3,2},{4,5},{5,4},{6,7},{7,6},{8,9},{9,8},{10,11... | collective-permute-start | bytes 14155784 | tf_op jit(solution)/shard_map/ppermute | solution.py:285
  19.7 14.6 %collective-permute-start.6 = (bf16[16,128,128]{2,1,0:T(8,128)(2,1)S(1)}, bf16[16,128,128]{2,1,0:T(8,128)(2,1)}, u32[]{:S(2)}, u32[]{:S(2)}) collective-permute-start(bf16[16,128,128]{2,1,0:T(8,128)(2,1)S(1)} %get-tuple-element.40.refs_0_), channel_id=1, source_target_pairs={{0,8},{1,9},{2,10},{3,11},{4,12},{5,13},{6,14},{7,15},{8,0},{9,1},... | collective-permute-start | bytes 1572872 | tf_op jit(solution)/shard_map/ppermute | solution.py:285
  21.6 14.2 %collective-permute-start.9 = (bf16[16,128,128]{2,1,0:T(8,128)(2,1)}, bf16[16,128,128]{2,1,0:T(8,128)(2,1)S(1)}, u32[]{:S(2)}, u32[]{:S(2)}) collective-permute-start(bf16[16,128,128]{2,1,0:T(8,128)(2,1)} %get-tuple-element.42.refs_8_), channel_id=1, source_target_pairs={{0,2},{1,3},{2,0},{3,1},{4,6},{5,7},{6,4},{7,5},{8,10},{9,11},{10,... | collective-permute-start | bytes 1572872 | tf_op jit(solution)/shard_map/ppermute | solution.py:285
  23.1 13.8 %collective-permute-start.8 = (bf16[16,128,128]{2,1,0:T(8,128)(2,1)S(1)}, bf16[16,128,128]{2,1,0:T(8,128)(2,1)}, u32[]{:S(2)}, u32[]{:S(2)}) collective-permute-start(bf16[16,128,128]{2,1,0:T(8,128)(2,1)S(1)} %get-tuple-element.41.refs_9_), channel_id=1, source_target_pairs={{0,4},{1,5},{2,6},{3,7},{4,0},{5,1},{6,2},{7,3},{8,12},{9,13},{10,... | collective-permute-start | bytes 1572872 | tf_op jit(solution)/shard_map/ppermute | solution.py:285
  23.6 13.3 %collective-permute-start.7 = (bf16[16,128,128]{2,1,0:T(8,128)(2,1)S(1)}, bf16[16,128,128]{2,1,0:T(8,128)(2,1)S(1)}, u32[]{:S(2)}, u32[]{:S(2)}) collective-permute-start(bf16[16,128,128]{2,1,0:T(8,128)(2,1)S(1)} %get-tuple-element.41.refs_9_), channel_id=1, source_target_pairs={{0,1},{1,0},{2,3},{3,2},{4,5},{5,4},{6,7},{7,6},{8,16},{9,17},{10,... | collective-permute-start | bytes 1572872 | tf_op jit(solution)/shard_map/ppermute | solution.py:292
  37.0 13.0 %collective-permute-start.12 = (bf16[16,128,128]{2,1,0:T(8,128)(2,1)S(1)}, bf16[16,128,128]{2,1,0:T(8,128)(2,1)}, u32[]{:S(2)}, u32[]{:S(2)}) collective-permute-start(bf16[16,128,128]{2,1,0:T(8,128)(2,1)S(1)} %get-tuple-element.52.refs_0_), channel_id=1, source_target_pairs={{0,8},{1,9},{2,10},{3,11},{4,12},{5,13},{6,14},{7,15},{8,0},{9,1},... | collective-permute-start | bytes 1572872 | tf_op jit(solution)/shard_map/ppermute | solution.py:285
  37.5 12.7 %collective-permute-start.11 = (bf16[16,128,128]{2,1,0:T(8,128)(2,1)S(1)}, bf16[16,128,128]{2,1,0:T(8,128)(2,1)}, u32[]{:S(2)}, u32[]{:S(2)}) collective-permute-start(bf16[16,128,128]{2,1,0:T(8,128)(2,1)S(1)} %get-tuple-element.51.refs_6_), channel_id=1, source_target_pairs={{0,2},{1,3},{2,0},{3,1},{4,6},{5,7},{6,4},{7,5},{8,10},{9,11},{10,... | collective-permute-start | bytes 1572872 | tf_op jit(solution)/shard_map/ppermute | solution.py:285
  38.0 12.6 %collective-permute-start.10 = (bf16[16,128,128]{2,1,0:T(8,128)(2,1)S(1)}, bf16[16,128,128]{2,1,0:T(8,128)(2,1)S(1)}, u32[]{:S(2)}, u32[]{:S(2)}) collective-permute-start(bf16[16,128,128]{2,1,0:T(8,128)(2,1)S(1)} %get-tuple-element.51.refs_6_), channel_id=1, source_target_pairs={{0,4},{1,5},{2,6},{3,7},{4,0},{5,1},{6,2},{7,3},{8,12},{9,13},{10,... | collective-permute-start | bytes 1572872 | tf_op jit(solution)/shard_map/ppermute | solution.py:285
  39.6 1.0 %copy-start.3 = (bf16[16,128,128]{2,1,0:T(8,128)(2,1)S(1)}, bf16[16,128,128]{2,1,0:T(8,128)(2,1)}, u32[]{:S(2)}) copy-start(bf16[16,128,128]{2,1,0:T(8,128)(2,1)} %copy-done.2) | copy-start | bytes 1572868
  40.7 1.2 %copy-start.5 = (f32[16,128,128]{2,1,0:T(8,128)S(1)}, f32[16,128,128]{2,1,0:T(8,128)}, u32[]{:S(2)}) copy-start(f32[16,128,128]{2,1,0:T(8,128)} %copy-done.4) | copy-start | bytes 3145732
  41.9 12.6 %copy-start.6 = (f32[16]{0:T(128)S(1)}, f32[16]{0:T(128)}, u32[]{:S(2)}) copy-start(f32[16]{0:T(128)} %refs_10_.1) | copy-start | bytes 196
  51.8 12.0 %collective-permute-start.13 = (bf16[16,128,128]{2,1,0:T(8,128)(2,1)S(1)}, bf16[16,128,128]{2,1,0:T(8,128)(2,1)S(1)}, u32[]{:S(2)}, u32[]{:S(2)}) collective-permute-start(bf16[16,128,128]{2,1,0:T(8,128)(2,1)S(1)} %get-tuple-element.59), channel_id=1, source_target_pairs={{0,8},{1,9},{2,10},{3,11},{4,12},{5,13},{6,14},{7,15},{8,0},{9,1},... | collective-permute-start | bytes 1572872 | tf_op jit(solution)/shard_map/ppermute | solution.py:285
  52.3 11.5 %collective-permute-start.15 = (bf16[16,128,128]{2,1,0:T(8,128)(2,1)S(1)}, bf16[16,128,128]{2,1,0:T(8,128)(2,1)S(1)}, u32[]{:S(2)}, u32[]{:S(2)}) collective-permute-start(bf16[16,128,128]{2,1,0:T(8,128)(2,1)S(1)} %get-tuple-element.56.refs_9_), channel_id=1, source_target_pairs={{0,2},{1,3},{2,0},{3,1},{4,6},{5,7},{6,4},{7,5},{8,10},{9,11},{10,... | collective-permute-start | bytes 1572872 | tf_op jit(solution)/shard_map/ppermute | solution.py:285
  53.5 10.9 %collective-permute-start.14 = (bf16[16,128,128]{2,1,0:T(8,128)(2,1)S(1)}, bf16[16,128,128]{2,1,0:T(8,128)(2,1)S(1)}, u32[]{:S(2)}, u32[]{:S(2)}) collective-permute-start(bf16[16,128,128]{2,1,0:T(8,128)(2,1)S(1)} %get-tuple-element.56.refs_9_), channel_id=1, source_target_pairs={{0,4},{1,5},{2,6},{3,7},{4,0},{5,1},{6,2},{7,3},{8,12},{9,13},{10,... | collective-permute-start | bytes 1572872 | tf_op jit(solution)/shard_map/ppermute | solution.py:285
  64.5 10.4 %collective-permute-start.16 = (bf16[16,128,128]{2,1,0:T(8,128)(2,1)S(1)}, bf16[16,128,128]{2,1,0:T(8,128)(2,1)S(1)}, u32[]{:S(2)}, u32[]{:S(2)}) collective-permute-start(bf16[16,128,128]{2,1,0:T(8,128)(2,1)S(1)} %get-tuple-element.66), channel_id=1, source_target_pairs={{0,8},{1,9},{2,10},{3,11},{4,12},{5,13},{6,14},{7,15},{8,0},{9,1},... | collective-permute-start | bytes 1572872 | tf_op jit(solution)/shard_map/ppermute | solution.py:285
  66.1 9.8 %collective-permute-start.17 = (bf16[16,128,128]{2,1,0:T(8,128)(2,1)S(1)}, bf16[16,128,128]{2,1,0:T(8,128)(2,1)S(1)}, u32[]{:S(2)}, u32[]{:S(2)}) collective-permute-start(bf16[16,128,128]{2,1,0:T(8,128)(2,1)S(1)} %get-tuple-element.67), channel_id=1, source_target_pairs={{0,2},{1,3},{2,0},{3,1},{4,6},{5,7},{6,4},{7,5},{8,10},{9,11},{10,... | collective-permute-start | bytes 1572872 | tf_op jit(solution)/shard_map/ppermute | solution.py:285
  67.4 9.6 %collective-permute-start.18 = (bf16[16,128,128]{2,1,0:T(8,128)(2,1)S(1)}, bf16[16,128,128]{2,1,0:T(8,128)(2,1)S(1)}, u32[]{:S(2)}, u32[]{:S(2)}) collective-permute-start(bf16[16,128,128]{2,1,0:T(8,128)(2,1)S(1)} %get-tuple-element.62.refs_7_), channel_id=1, source_target_pairs={{0,4},{1,5},{2,6},{3,7},{4,0},{5,1},{6,2},{7,3},{8,12},{9,13},{10,... | collective-permute-start | bytes 1572872 | tf_op jit(solution)/shard_map/ppermute | solution.py:285
  79.0 10.0 %collective-permute-start.19 = (f32[16,128,128]{2,1,0:T(8,128)S(1)}, f32[16,128,128]{2,1,0:T(8,128)S(1)}, u32[]{:S(2)}, u32[]{:S(2)}) collective-permute-start(f32[16,128,128]{2,1,0:T(8,128)S(1)} %get-tuple-element.72), channel_id=1, source_target_pairs={{0,1},{1,0},{2,3},{3,2},{4,5},{5,4},{6,7},{7,6},{8,9},{9,8},{10,11... | collective-permute-start | bytes 3145736 | tf_op jit(solution)/shard_map/ppermute | solution.py:285

commit v7 on v6

--- a/solution.py
+++ b/solution.py
@@ -298,7 +298,7 @@
         [(0, 0), (0, x), (0, y), (1, 0), (0, xy), (1, y)],
         [(2, 0), (2, x), (2, y), (3, 0)],
         [(3, y), (3, x), (1, x)],
-        [(1, xy), (2, xy), (3, xy)],
+        [(3, xy), (2, xy), (1, xy)],
     ]
     order = jnp.concatenate([me ^ layer_masks[b] ^ jnp.full((1,), bits) for group in groups for b, bits in group])
 
@@ -333,7 +333,7 @@
     held["middle_2"] = swap_middle(held[1, 0])
     held["env_sib"] = swap(held["env"], core)
     hold(["middle"], held["outer"], move=(1, 0), flag=outer)
-    hold(["env_sib", "middle", "middle_2", (1, y), (0, xy)])
+    hold(["env_sib", "middle_2", (1, y), (0, xy), "middle"])
 
     held[2, 0] = held["middle"]
     held[2, x], held[2, y] = swap(held[2, 0], x), swap(held[2, 0], y)

time: 90.8 us -> 90.8 us (level)
  transfers between devices with their start and end apart: 20 -> 20, of which waited for: 13 -> 14; matrix products, arithmetic and copies ran while one was open for 2% -> 2% of each run, Pallas kernels for 23% -> 23%
where the time goes in v7:
time: 90.8 us; the launch traced here: 90.3 us
  waiting for transfers between devices  29.2 us (32%)
  Pallas kernels  25.5 us (28%)
  starting transfers between devices  19.6 us (22%)
  blocking collectives  9.9 us (11%)
  local copies, waits for them, and re-layouts  4.96 us (5%)
    ppermute x18, waiting for transfers between devices, swap(): return lax.ppermute(value, 'sector', [(i, i ^ mask) for i in range(owners)])  29.2 us
    ppermute x18, starting transfers between devices, swap(): return lax.ppermute(value, 'sector', [(i, i ^ mask) for i in range(owners)])  19.6 us
    pallas_call x4, Pallas kernels, hop_call(): pl.pallas_call(functools.partial(hop_kernel, base, count, first, bool(ons...  13.8 us
    all_to_all x1, blocking collectives, spread_everywhere(): sums = lax.all_to_all(sums, 'sector', 0, 0, tiled=True)  9.9 us
    pallas_call x1, Pallas kernels, local_call(): pl.pallas_call(local_kernel, out_shape=(jax.ShapeDtypeStruct((sec, size,...  8.05 us
    unnamed x14, local copies, waits for them, and re-layouts  3.32 us
    pallas_call x5, Pallas kernels, hold_until(): pl.pallas_call(functools.partial(hold_kernel, count, move), out_shape=[ja...  2.36 us
  transfers between devices with their start and end apart: 20, of which 14 were waited for; matrix products, arithmetic and copies ran while one was open for 2% of the time, Pallas kernels for 23%

profile of v7, /device:TPU:0, one launch (start us, length us, event | category | flops | bytes accessed | tf_op | source)
XLA Modules:
  0.0 90.3 jit_solution(1893726529430348633)
XLA Ops:
  0.6 3.1 %collective-permute-start.4 = (bf16[16,128,128]{2,1,0:T(8,128)(2,1)}, bf16[16,128,128]{2,1,0:T(8,128)(2,1)S(1)}, u32[]{:S(2)}, u32[]{:S(2)}) collective-permute-start(bf16[16,128,128]{2,1,0:T(8,128)(2,1)} %psi.1), channel_id=1, source_target_pairs={{0,8},{1,9},{2,10},{3,11},{4,12},{5,13},{6,14},{7,15},{8,0},{9,1},... | collective-permute-start | bytes 1572872 | tf_op jit(solution)/shard_map/ppermute | solution.py:285
  3.7 0.0 collective-permute-start.3
  3.7 1.5 %collective-permute-start.2 = (bf16[16,128,128]{2,1,0:T(8,128)(2,1)}, bf16[16,128,128]{2,1,0:T(8,128)(2,1)}, u32[]{:S(2)}, u32[]{:S(2)}) collective-permute-start(bf16[16,128,128]{2,1,0:T(8,128)(2,1)} %psi.1), channel_id=1, source_target_pairs={{0,4},{1,5},{2,6},{3,7},{4,0},{5,1},{6,2},{7,3},{8,12},{9,13},{10,... | collective-permute-start | bytes 1572872 | tf_op jit(solution)/shard_map/ppermute | solution.py:285
  5.2 1.5 %collective-permute-start.1 = (bf16[16,128,128]{2,1,0:T(8,128)(2,1)}, bf16[16,128,128]{2,1,0:T(8,128)(2,1)S(1)}, u32[]{:S(2)}, u32[]{:S(2)}) collective-permute-start(bf16[16,128,128]{2,1,0:T(8,128)(2,1)} %psi.1), channel_id=1, source_target_pairs={{0,2},{1,3},{2,0},{3,1},{4,6},{5,7},{6,4},{7,5},{8,10},{9,11},{10,... | collective-permute-start | bytes 1572872 | tf_op jit(solution)/shard_map/ppermute | solution.py:285
  6.7 0.8 reshape.95
  7.5 0.8 reshape.96
  8.3 0.2 convert_reduce_fusion
  8.5 0.1 select_reduce_fusion.refs_1_
  8.6 0.1 collective-permute-start
  8.7 0.0 copy-start
  8.7 1.0 %copy-done = bf16[16,128,128]{2,1,0:T(8,128)(2,1)S(1)} copy-done((bf16[16,128,128]{2,1,0:T(8,128)(2,1)S(1)}, bf16[16,128,128]{2,1,0:T(8,128)(2,1)}, u32[]{:S(2)}) %copy-start) | copy-done | bytes 524312
  9.7 8.0 %local_channels.1 = (f32[16,128,128]{2,1,0:T(8,128)S(1)}, f32[128,128]{1,0:T(8,128)S(1)}, bf16[144,128,128]{2,1,0:T(8,128)(2,1)}) custom-call(bf16[4,4,128,128]{3,2,1,0:T(8,128)(2,1)S(1)} %bitcast.10, bf16[4,32,128,128]{3,2,1,0:T(8,128)(2,1)} %right.1, bf16[4,32,128,128]{3,2,1,0:T(8,128)(2,1)} %left.1), custom_call_target="tpu_custom_call" | custom-call | flops 1 | bytes 1 | tf_op jit(solution)/shard_map/local_channels/pallas_call | solution.py:107
  17.8 0.0 copy-start.4
  17.8 0.0 collective-permute-done.refs_5_.refs_2_
  17.8 0.0 collective-permute-done.4.refs_3_
  17.8 0.0 collective-permute-done.3.refs_2_
  17.8 0.5 collective-permute-done.2.refs_1_
  18.4 1.1 %collective-permute-done.1.refs_0_ = bf16[16,128,128]{2,1,0:T(8,128)(2,1)S(1)} collective-permute-done((bf16[16,128,128]{2,1,0:T(8,128)(2,1)}, bf16[16,128,128]{2,1,0:T(8,128)(2,1)S(1)}, u32[]{:S(2)}, u32[]{:S(2)}) %collective-permute-start.1) | collective-permute-done | bytes 524320 | tf_op jit(solution)/shard_map/ppermute | solution.py:285
  19.6 0.0 copy-start.2
  19.6 0.0 copy-start.1
  19.6 0.1 collective-permute-start.5
  19.7 2.0 %collective-permute-start.9 = (bf16[16,128,128]{2,1,0:T(8,128)(2,1)S(1)}, bf16[16,128,128]{2,1,0:T(8,128)(2,1)}, u32[]{:S(2)}, u32[]{:S(2)}) collective-permute-start(bf16[16,128,128]{2,1,0:T(8,128)(2,1)S(1)} %get-tuple-element.42.refs_0_), channel_id=1, source_target_pairs={{0,8},{1,9},{2,10},{3,11},{4,12},{5,13},{6,14},{7,15},{8,0},{9,1},... | collective-permute-start | bytes 1572872 | tf_op jit(solution)/shard_map/ppermute | solution.py:285
  21.6 1.5 %collective-permute-start.8 = (bf16[16,128,128]{2,1,0:T(8,128)(2,1)}, bf16[16,128,128]{2,1,0:T(8,128)(2,1)S(1)}, u32[]{:S(2)}, u32[]{:S(2)}) collective-permute-start(bf16[16,128,128]{2,1,0:T(8,128)(2,1)} %get-tuple-element.41.refs_8_), channel_id=1, source_target_pairs={{0,2},{1,3},{2,0},{3,1},{4,6},{5,7},{6,4},{7,5},{8,10},{9,11},{10,... | collective-permute-start | bytes 1572872 | tf_op jit(solution)/shard_map/ppermute | solution.py:285
  23.1 0.0 copy-done.4
  23.1 0.5 collective-permute-start.7
  23.6 0.0 collective-permute-start.6
  23.6 10.6 %collective-permute-done.9.refs_1_ = bf16[16,128,128]{2,1,0:T(8,128)(2,1)} collective-permute-done((bf16[16,128,128]{2,1,0:T(8,128)(2,1)S(1)}, bf16[16,128,128]{2,1,0:T(8,128)(2,1)}, u32[]{:S(2)}, u32[]{:S(2)}) %collective-permute-start.9) | collective-permute-done | bytes 524320 | tf_op jit(solution)/shard_map/ppermute | solution.py:285
  34.3 1.1 %hold.6.refs_4_ = bf16[16,128,128]{2,1,0:T(8,128)(2,1)S(1)} custom-call(bf16[16,128,128]{2,1,0:T(8,128)(2,1)S(1)} %get-tuple-element.42.refs_0_, bf16[16,128,128]{2,1,0:T(8,128)(2,1)} %collective-permute-done.9.refs_1_, s32[1]{0:T(128)} %bitcast.5.refs_2_.refs_6_), custom_call_target="tpu_custom_call", output_to_operand_aliasing={{}: (0, {})} | custom-call | flops 1 | bytes 1 | tf_op jit(solution)/shard_map/hold/pallas_call | solution.py:227
  35.4 0.4 collective-permute-done.8.refs_3_
  35.8 1.1 %collective-permute-done.7.refs_2_ = bf16[16,128,128]{2,1,0:T(8,128)(2,1)} collective-permute-done((bf16[16,128,128]{2,1,0:T(8,128)(2,1)S(1)}, bf16[16,128,128]{2,1,0:T(8,128)(2,1)}, u32[]{:S(2)}, u32[]{:S(2)}) %collective-permute-start.7) | collective-permute-done | bytes 524320 | tf_op jit(solution)/shard_map/ppermute | solution.py:285
  37.0 0.0 collective-permute-done.6.refs_1_
  37.0 0.0 collective-permute-done.5.refs_0_
  37.0 0.5 collective-permute-start.12
  37.5 0.0 copy-done.2
  37.5 0.5 collective-permute-start.11
  38.0 1.5 %collective-permute-start.10 = (bf16[16,128,128]{2,1,0:T(8,128)(2,1)S(1)}, bf16[16,128,128]{2,1,0:T(8,128)(2,1)S(1)}, u32[]{:S(2)}, u32[]{:S(2)}) collective-permute-start(bf16[16,128,128]{2,1,0:T(8,128)(2,1)S(1)} %get-tuple-element.51.refs_6_), channel_id=1, source_target_pairs={{0,4},{1,5},{2,6},{3,7},{4,0},{5,1},{6,2},{7,3},{8,12},{9,13},{10,... | collective-permute-start | bytes 1572872 | tf_op jit(solution)/shard_map/ppermute | solution.py:285
  39.5 0.1 concatenate.3.refs_0_
  39.6 0.0 copy-start.3
  39.6 1.0 %copy-done.3 = bf16[16,128,128]{2,1,0:T(8,128)(2,1)S(1)} copy-done((bf16[16,128,128]{2,1,0:T(8,128)(2,1)S(1)}, bf16[16,128,128]{2,1,0:T(8,128)(2,1)}, u32[]{:S(2)}) %copy-start.3) | copy-done | bytes 524312
  40.7 1.2 %copy-done.5 = f32[16,128,128]{2,1,0:T(8,128)S(1)} copy-done((f32[16,128,128]{2,1,0:T(8,128)S(1)}, f32[16,128,128]{2,1,0:T(8,128)}, u32[]{:S(2)}) %copy-start.5) | copy-done | bytes 1048600
  41.9 7.0 %hops_0.1 = (f32[16,128,128]{2,1,0:T(8,128)S(1)}, f32[16,128,128]{2,1,0:T(8,128)S(1)}, f32[8,128]{1,0:T(8,128)S(1)}, bf16[2,144,128,128]{3,2,1,0:T(8,128)(2,1)S(1)}) custom-call(s32[16]{0:T(128)S(1)} %concatenate.3.refs_0_, s32[256]{0:T(256)S(1)} %select_reduce_fusion.refs_1_, s32[256]{0:T(256)S(1)} %collective-permute-done.refs_5_.refs_2_, ...), custom_call_target="tpu_custom_call" | custom-call | flops 1 | bytes 1 | tf_op jit(solution)/shard_map/hops_0/pallas_call | solution.py:192
  48.9 1.2 %collective-permute-done.12.refs_4_ = bf16[16,128,128]{2,1,0:T(8,128)(2,1)} collective-permute-done((bf16[16,128,128]{2,1,0:T(8,128)(2,1)S(1)}, bf16[16,128,128]{2,1,0:T(8,128)(2,1)}, u32[]{:S(2)}, u32[]{:S(2)}) %collective-permute-start.12) | collective-permute-done | bytes 524320 | tf_op jit(solution)/shard_map/ppermute | solution.py:285
  50.0 0.2 collective-permute-done.11.refs_3_
  50.2 0.4 collective-permute-done.10.refs_2_
  50.6 1.1 %hold.8 = (bf16[16,128,128]{2,1,0:T(8,128)(2,1)S(1)}, bf16[16,128,128]{2,1,0:T(8,128)(2,1)S(1)}, bf16[16,128,128]{2,1,0:T(8,128)(2,1)S(1)}, bf16[16,128,128]{2,1,0:T(8,128)(2,1)}) custom-call(bf16[16,128,128]{2,1,0:T(8,128)(2,1)S(1)} %get-tuple-element.52.refs_0_, ...), custom_call_target="tpu_custom_call", output_to_operand_aliasing={{0}: (0, {}), {1}: (1, {}), {2}: (2, {}), {3}: (3, {})} | custom-call | flops 1 | bytes 1 | tf_op jit(solution)/shard_map/hold/pallas_call | solution.py:227
  51.8 0.5 collective-permute-start.13
  52.3 1.2 %collective-permute-start.15 = (bf16[16,128,128]{2,1,0:T(8,128)(2,1)S(1)}, bf16[16,128,128]{2,1,0:T(8,128)(2,1)S(1)}, u32[]{:S(2)}, u32[]{:S(2)}) collective-permute-start(bf16[16,128,128]{2,1,0:T(8,128)(2,1)S(1)} %get-tuple-element.56.refs_9_), channel_id=1, source_target_pairs={{0,2},{1,3},{2,0},{3,1},{4,6},{5,7},{6,4},{7,5},{8,10},{9,11},{10,... | collective-permute-start | bytes 1572872 | tf_op jit(solution)/shard_map/ppermute | solution.py:285
  53.5 1.0 %collective-permute-start.14 = (bf16[16,128,128]{2,1,0:T(8,128)(2,1)S(1)}, bf16[16,128,128]{2,1,0:T(8,128)(2,1)S(1)}, u32[]{:S(2)}, u32[]{:S(2)}) collective-permute-start(bf16[16,128,128]{2,1,0:T(8,128)(2,1)S(1)} %get-tuple-element.56.refs_9_), channel_id=1, source_target_pairs={{0,4},{1,5},{2,6},{3,7},{4,0},{5,1},{6,2},{7,3},{8,12},{9,13},{10,... | collective-permute-start | bytes 1572872 | tf_op jit(solution)/shard_map/ppermute | solution.py:285
  54.5 2.7 %hops_1.1 = (f32[16,128,128]{2,1,0:T(8,128)S(1)}, f32[16,128,128]{2,1,0:T(8,128)S(1)}, f32[8,128]{1,0:T(8,128)S(1)}) custom-call(s32[16]{0:T(128)S(1)} %concatenate.3.refs_0_, s32[256]{0:T(256)S(1)} %select_reduce_fusion.refs_1_, s32[256]{0:T(256)S(1)} %collective-permute-done.refs_5_.refs_2_, bf16[2,144,128,128]{3,2,1,0:T(8,128)(2,1)S(1)} %get-tuple-element.48.refs_3_, ...), custom_call_target="tpu_custom_call" | custom-call | flops 1 | bytes 1 | tf_op jit(solution)/shard_map/hops_1/pallas_call | solution.py:192
  57.2 6.5 %collective-permute-done.13.refs_0_ = bf16[16,128,128]{2,1,0:T(8,128)(2,1)S(1)} collective-permute-done((bf16[16,128,128]{2,1,0:T(8,128)(2,1)S(1)}, bf16[16,128,128]{2,1,0:T(8,128)(2,1)S(1)}, u32[]{:S(2)}, u32[]{:S(2)}) %collective-permute-start.13) | collective-permute-done | bytes 524320 | tf_op jit(solution)/shard_map/ppermute | solution.py:285
  63.7 0.4 collective-permute-done.15.refs_4_
  64.0 0.4 collective-permute-done.14.refs_3_
  64.5 1.2 %collective-permute-start.17 = (bf16[16,128,128]{2,1,0:T(8,128)(2,1)S(1)}, bf16[16,128,128]{2,1,0:T(8,128)(2,1)S(1)}, u32[]{:S(2)}, u32[]{:S(2)}) collective-permute-start(bf16[16,128,128]{2,1,0:T(8,128)(2,1)S(1)} %get-tuple-element.66), channel_id=1, source_target_pairs={{0,2},{1,3},{2,0},{3,1},{4,6},{5,7},{6,4},{7,5},{8,10},{9,11},{10,... | collective-permute-start | bytes 1572872 | tf_op jit(solution)/shard_map/ppermute | solution.py:285
  65.6 1.8 %collective-permute-start.18 = (bf16[16,128,128]{2,1,0:T(8,128)(2,1)S(1)}, bf16[16,128,128]{2,1,0:T(8,128)(2,1)S(1)}, u32[]{:S(2)}, u32[]{:S(2)}) collective-permute-start(bf16[16,128,128]{2,1,0:T(8,128)(2,1)S(1)} %get-tuple-element.67), channel_id=1, source_target_pairs={{0,8},{1,9},{2,10},{3,11},{4,12},{5,13},{6,14},{7,15},{8,0},{9,1},... | collective-permute-start | bytes 1572872 | tf_op jit(solution)/shard_map/ppermute | solution.py:285
  67.4 1.1 %collective-permute-start.16 = (bf16[16,128,128]{2,1,0:T(8,128)(2,1)S(1)}, bf16[16,128,128]{2,1,0:T(8,128)(2,1)S(1)}, u32[]{:S(2)}, u32[]{:S(2)}) collective-permute-start(bf16[16,128,128]{2,1,0:T(8,128)(2,1)S(1)} %get-tuple-element.62.refs_7_), channel_id=1, source_target_pairs={{0,4},{1,5},{2,6},{3,7},{4,0},{5,1},{6,2},{7,3},{8,12},{9,13},{10,... | collective-permute-start | bytes 1572872 | tf_op jit(solution)/shard_map/ppermute | solution.py:285
  68.5 2.2 %hops_2.1 = (f32[16,128,128]{2,1,0:T(8,128)S(1)}, f32[16,128,128]{2,1,0:T(8,128)S(1)}, f32[128,128]{1,0:T(8,128)S(1)}) custom-call(s32[16]{0:T(128)S(1)} %concatenate.3.refs_0_, s32[256]{0:T(256)S(1)} %select_reduce_fusion.refs_1_, s32[256]{0:T(256)S(1)} %collective-permute-done.refs_5_.refs_2_, bf16[2,144,128,128]{3,2,1,0:T(8,128)(2,1)S(1)} %get-tuple-element.48.refs_3_, ...), custom_call_target="tpu_custom_call" | custom-call | flops 1 | bytes 1 | tf_op jit(solution)/shard_map/hops_2/pallas_call | solution.py:192
  70.8 4.3 %collective-permute-done.17.refs_7_ = bf16[16,128,128]{2,1,0:T(8,128)(2,1)S(1)} collective-permute-done((bf16[16,128,128]{2,1,0:T(8,128)(2,1)S(1)}, bf16[16,128,128]{2,1,0:T(8,128)(2,1)S(1)}, u32[]{:S(2)}, u32[]{:S(2)}) %collective-permute-start.17) | collective-permute-done | bytes 524320 | tf_op jit(solution)/shard_map/ppermute | solution.py:285
  75.0 0.6 collective-permute-done.18.refs_8_
  75.6 1.4 %collective-permute-done.16.refs_6_ = bf16[16,128,128]{2,1,0:T(8,128)(2,1)S(1)} collective-permute-done((bf16[16,128,128]{2,1,0:T(8,128)(2,1)S(1)}, bf16[16,128,128]{2,1,0:T(8,128)(2,1)S(1)}, u32[]{:S(2)}, u32[]{:S(2)}) %collective-permute-start.16) | collective-permute-done | bytes 524320 | tf_op jit(solution)/shard_map/ppermute | solution.py:285
  77.1 2.0 %hops_3.1 = (f32[16,128,128]{2,1,0:T(8,128)S(1)}, f32[16,128,128]{2,1,0:T(8,128)S(1)}, f32[32,128]{1,0:T(8,128)S(1)}) custom-call(s32[16]{0:T(128)S(1)} %concatenate.3.refs_0_, s32[256]{0:T(256)S(1)} %select_reduce_fusion.refs_1_, s32[256]{0:T(256)S(1)} %collective-permute-done.refs_5_.refs_2_, bf16[2,144,128,128]{3,2,1,0:T(8,128)(2,1)S(1)} %get-tuple-element.48.refs_3_, ...), custom_call_target="tpu_custom_call" | custom-call | flops 1 | bytes 1 | tf_op jit(solution)/shard_map/hops_3/pallas_call | solution.py:192
  79.1 0.1 collective-permute-start.19
  79.1 9.9 %all_to_all.11 = f32[32,1,128]{2,1,0:T(1,128)S(1)} all-to-all(f32[32,1,128]{2,1,0:T(1,128)S(1)} %bitcast.12), channel_id=1, replica_groups=mesh['groups'=1,'sector'=32] {'sector'}, dimensions={0} | all-to-all | bytes 32768 | tf_op jit(solution)/shard_map/all_to_all | solution.py:356
  89.0 0.0 collective-permute-done.19.theirs
  89.1 1.3 %finish.1 = (bf16[16,128,128]{2,1,0:T(8,128)(2,1)}, bf16[16,128,128]{2,1,0:T(8,128)(2,1)}, f32[1]{0:T(128)}) custom-call(f32[32,128]{1,0:T(8,128)S(1)} %bitcast.11, bf16[16,128,128]{2,1,0:T(8,128)(2,1)S(1)} %copy-done.1, f32[16,128,128]{2,1,0:T(8,128)S(1)} %get-tuple-element.71.mine, f32[16,128,128]{2,1,0:T(8,128)S(1)} %collective-permute-done.19.theirs), custom_call_target="tpu_custom_call" | custom-call | tf_op jit(solution)/shard_map/finish/pallas_call | solution.py:253
  (8 shorter events, 0.1 us)
Async XLA Ops:
  0.6 17.2 %collective-permute-start.4 = (bf16[16,128,128]{2,1,0:T(8,128)(2,1)}, bf16[16,128,128]{2,1,0:T(8,128)(2,1)S(1)}, u32[]{:S(2)}, u32[]{:S(2)}) collective-permute-start(bf16[16,128,128]{2,1,0:T(8,128)(2,1)} %psi.1), channel_id=1, source_target_pairs={{0,8},{1,9},{2,10},{3,11},{4,12},{5,13},{6,14},{7,15},{8,0},{9,1},... | collective-permute-start | bytes 1572872 | tf_op jit(solution)/shard_map/ppermute | solution.py:285
  3.7 14.1 %collective-permute-start.3 = (bf16[16,128,128]{2,1,0:T(8,128)(2,1)}, bf16[16,128,128]{2,1,0:T(8,128)(2,1)S(1)}, u32[]{:S(2)}, u32[]{:S(2)}) collective-permute-start(bf16[16,128,128]{2,1,0:T(8,128)(2,1)} %psi.1), channel_id=1, source_target_pairs={{0,1},{1,0},{2,3},{3,2},{4,5},{5,4},{6,7},{7,6},{8,16},{9,17},{10,... | collective-permute-start | bytes 1572872 | tf_op jit(solution)/shard_map/ppermute | solution.py:292
  3.7 14.7 %collective-permute-start.2 = (bf16[16,128,128]{2,1,0:T(8,128)(2,1)}, bf16[16,128,128]{2,1,0:T(8,128)(2,1)}, u32[]{:S(2)}, u32[]{:S(2)}) collective-permute-start(bf16[16,128,128]{2,1,0:T(8,128)(2,1)} %psi.1), channel_id=1, source_target_pairs={{0,4},{1,5},{2,6},{3,7},{4,0},{5,1},{6,2},{7,3},{8,12},{9,13},{10,... | collective-permute-start | bytes 1572872 | tf_op jit(solution)/shard_map/ppermute | solution.py:285
  5.2 14.3 %collective-permute-start.1 = (bf16[16,128,128]{2,1,0:T(8,128)(2,1)}, bf16[16,128,128]{2,1,0:T(8,128)(2,1)S(1)}, u32[]{:S(2)}, u32[]{:S(2)}) collective-permute-start(bf16[16,128,128]{2,1,0:T(8,128)(2,1)} %psi.1), channel_id=1, source_target_pairs={{0,2},{1,3},{2,0},{3,1},{4,6},{5,7},{6,4},{7,5},{8,10},{9,11},{10,... | collective-permute-start | bytes 1572872 | tf_op jit(solution)/shard_map/ppermute | solution.py:285
  8.6 9.2 %collective-permute-start = (s32[256]{0:T(256)S(1)}, s32[256]{0:T(256)S(1)}, u32[]{:S(2)}, u32[]{:S(2)}) collective-permute-start(s32[256]{0:T(256)S(1)} %select_reduce_fusion.refs_1_), channel_id=1, source_target_pairs={{0,1},{1,0},{2,3},{3,2},{4,5},{5,4},{6,7},{7,6},{8,9},{9,8},{10,11... | collective-permute-start | bytes 3080 | tf_op jit(solution)/shard_map/ppermute | solution.py:285
  8.7 1.0 %copy-start = (bf16[16,128,128]{2,1,0:T(8,128)(2,1)S(1)}, bf16[16,128,128]{2,1,0:T(8,128)(2,1)}, u32[]{:S(2)}) copy-start(bf16[16,128,128]{2,1,0:T(8,128)(2,1)} %psi.1) | copy-start | bytes 1572868
  17.8 5.3 %copy-start.4 = (f32[16,128,128]{2,1,0:T(8,128)}, f32[16,128,128]{2,1,0:T(8,128)S(1)}, u32[]{:S(2)}) copy-start(f32[16,128,128]{2,1,0:T(8,128)S(1)} %get-tuple-element.44.refs_5_) | copy-start | bytes 3145732
  19.6 17.9 %copy-start.2 = (bf16[16,128,128]{2,1,0:T(8,128)(2,1)}, bf16[16,128,128]{2,1,0:T(8,128)(2,1)S(1)}, u32[]{:S(2)}) copy-start(bf16[16,128,128]{2,1,0:T(8,128)(2,1)S(1)} %get-tuple-element.40.refs_9_) | copy-start | bytes 1572868
  19.6 20.0 %copy-start.1 = (bf16[16,128,128]{2,1,0:T(8,128)(2,1)S(1)}, bf16[16,128,128]{2,1,0:T(8,128)(2,1)}, u32[]{:S(2)}) copy-start(bf16[16,128,128]{2,1,0:T(8,128)(2,1)} %psi.1) | copy-start | bytes 1572868
  19.6 17.4 %collective-permute-start.5 = (bf16[144,128,128]{2,1,0:T(8,128)(2,1)}, bf16[144,128,128]{2,1,0:T(8,128)(2,1)}, u32[]{:S(2)}, u32[]{:S(2)}) collective-permute-start(bf16[144,128,128]{2,1,0:T(8,128)(2,1)} %get-tuple-element.39.refs_3_), channel_id=1, source_target_pairs={{0,1},{1,0},{2,3},{3,2},{4,5},{5,4},{6,7},{7,6},{8,9},{9,8},{10,11... | collective-permute-start | bytes 14155784 | tf_op jit(solution)/shard_map/ppermute | solution.py:285
  19.7 14.6 %collective-permute-start.9 = (bf16[16,128,128]{2,1,0:T(8,128)(2,1)S(1)}, bf16[16,128,128]{2,1,0:T(8,128)(2,1)}, u32[]{:S(2)}, u32[]{:S(2)}) collective-permute-start(bf16[16,128,128]{2,1,0:T(8,128)(2,1)S(1)} %get-tuple-element.42.refs_0_), channel_id=1, source_target_pairs={{0,8},{1,9},{2,10},{3,11},{4,12},{5,13},{6,14},{7,15},{8,0},{9,1},... | collective-permute-start | bytes 1572872 | tf_op jit(solution)/shard_map/ppermute | solution.py:285
  21.6 14.2 %collective-permute-start.8 = (bf16[16,128,128]{2,1,0:T(8,128)(2,1)}, bf16[16,128,128]{2,1,0:T(8,128)(2,1)S(1)}, u32[]{:S(2)}, u32[]{:S(2)}) collective-permute-start(bf16[16,128,128]{2,1,0:T(8,128)(2,1)} %get-tuple-element.41.refs_8_), channel_id=1, source_target_pairs={{0,2},{1,3},{2,0},{3,1},{4,6},{5,7},{6,4},{7,5},{8,10},{9,11},{10,... | collective-permute-start | bytes 1572872 | tf_op jit(solution)/shard_map/ppermute | solution.py:285
  23.1 13.8 %collective-permute-start.7 = (bf16[16,128,128]{2,1,0:T(8,128)(2,1)S(1)}, bf16[16,128,128]{2,1,0:T(8,128)(2,1)}, u32[]{:S(2)}, u32[]{:S(2)}) collective-permute-start(bf16[16,128,128]{2,1,0:T(8,128)(2,1)S(1)} %get-tuple-element.40.refs_9_), channel_id=1, source_target_pairs={{0,4},{1,5},{2,6},{3,7},{4,0},{5,1},{6,2},{7,3},{8,12},{9,13},{10,... | collective-permute-start | bytes 1572872 | tf_op jit(solution)/shard_map/ppermute | solution.py:285
  23.6 13.3 %collective-permute-start.6 = (bf16[16,128,128]{2,1,0:T(8,128)(2,1)S(1)}, bf16[16,128,128]{2,1,0:T(8,128)(2,1)S(1)}, u32[]{:S(2)}, u32[]{:S(2)}) collective-permute-start(bf16[16,128,128]{2,1,0:T(8,128)(2,1)S(1)} %get-tuple-element.40.refs_9_), channel_id=1, source_target_pairs={{0,1},{1,0},{2,3},{3,2},{4,5},{5,4},{6,7},{7,6},{8,16},{9,17},{10,... | collective-permute-start | bytes 1572872 | tf_op jit(solution)/shard_map/ppermute | solution.py:292
  37.0 13.0 %collective-permute-start.12 = (bf16[16,128,128]{2,1,0:T(8,128)(2,1)S(1)}, bf16[16,128,128]{2,1,0:T(8,128)(2,1)}, u32[]{:S(2)}, u32[]{:S(2)}) collective-permute-start(bf16[16,128,128]{2,1,0:T(8,128)(2,1)S(1)} %get-tuple-element.52.refs_0_), channel_id=1, source_target_pairs={{0,8},{1,9},{2,10},{3,11},{4,12},{5,13},{6,14},{7,15},{8,0},{9,1},... | collective-permute-start | bytes 1572872 | tf_op jit(solution)/shard_map/ppermute | solution.py:285
  37.5 12.7 %collective-permute-start.11 = (bf16[16,128,128]{2,1,0:T(8,128)(2,1)S(1)}, bf16[16,128,128]{2,1,0:T(8,128)(2,1)}, u32[]{:S(2)}, u32[]{:S(2)}) collective-permute-start(bf16[16,128,128]{2,1,0:T(8,128)(2,1)S(1)} %get-tuple-element.51.refs_6_), channel_id=1, source_target_pairs={{0,2},{1,3},{2,0},{3,1},{4,6},{5,7},{6,4},{7,5},{8,10},{9,11},{10,... | collective-permute-start | bytes 1572872 | tf_op jit(solution)/shard_map/ppermute | solution.py:285
  38.0 12.6 %collective-permute-start.10 = (bf16[16,128,128]{2,1,0:T(8,128)(2,1)S(1)}, bf16[16,128,128]{2,1,0:T(8,128)(2,1)S(1)}, u32[]{:S(2)}, u32[]{:S(2)}) collective-permute-start(bf16[16,128,128]{2,1,0:T(8,128)(2,1)S(1)} %get-tuple-element.51.refs_6_), channel_id=1, source_target_pairs={{0,4},{1,5},{2,6},{3,7},{4,0},{5,1},{6,2},{7,3},{8,12},{9,13},{10,... | collective-permute-start | bytes 1572872 | tf_op jit(solution)/shard_map/ppermute | solution.py:285
  39.6 1.0 %copy-start.3 = (bf16[16,128,128]{2,1,0:T(8,128)(2,1)S(1)}, bf16[16,128,128]{2,1,0:T(8,128)(2,1)}, u32[]{:S(2)}) copy-start(bf16[16,128,128]{2,1,0:T(8,128)(2,1)} %copy-done.2) | copy-start | bytes 1572868
  40.7 1.2 %copy-start.5 = (f32[16,128,128]{2,1,0:T(8,128)S(1)}, f32[16,128,128]{2,1,0:T(8,128)}, u32[]{:S(2)}) copy-start(f32[16,128,128]{2,1,0:T(8,128)} %copy-done.4) | copy-start | bytes 3145732
  41.9 12.6 %copy-start.6 = (f32[16]{0:T(128)S(1)}, f32[16]{0:T(128)}, u32[]{:S(2)}) copy-start(f32[16]{0:T(128)} %refs_10_.1) | copy-start | bytes 196
  51.8 11.9 %collective-permute-start.13 = (bf16[16,128,128]{2,1,0:T(8,128)(2,1)S(1)}, bf16[16,128,128]{2,1,0:T(8,128)(2,1)S(1)}, u32[]{:S(2)}, u32[]{:S(2)}) collective-permute-start(bf16[16,128,128]{2,1,0:T(8,128)(2,1)S(1)} %get-tuple-element.59), channel_id=1, source_target_pairs={{0,8},{1,9},{2,10},{3,11},{4,12},{5,13},{6,14},{7,15},{8,0},{9,1},... | collective-permute-start | bytes 1572872 | tf_op jit(solution)/shard_map/ppermute | solution.py:285
  52.3 11.7 %collective-permute-start.15 = (bf16[16,128,128]{2,1,0:T(8,128)(2,1)S(1)}, bf16[16,128,128]{2,1,0:T(8,128)(2,1)S(1)}, u32[]{:S(2)}, u32[]{:S(2)}) collective-permute-start(bf16[16,128,128]{2,1,0:T(8,128)(2,1)S(1)} %get-tuple-element.56.refs_9_), channel_id=1, source_target_pairs={{0,2},{1,3},{2,0},{3,1},{4,6},{5,7},{6,4},{7,5},{8,10},{9,11},{10,... | collective-permute-start | bytes 1572872 | tf_op jit(solution)/shard_map/ppermute | solution.py:285
  53.5 10.9 %collective-permute-start.14 = (bf16[16,128,128]{2,1,0:T(8,128)(2,1)S(1)}, bf16[16,128,128]{2,1,0:T(8,128)(2,1)S(1)}, u32[]{:S(2)}, u32[]{:S(2)}) collective-permute-start(bf16[16,128,128]{2,1,0:T(8,128)(2,1)S(1)} %get-tuple-element.56.refs_9_), channel_id=1, source_target_pairs={{0,4},{1,5},{2,6},{3,7},{4,0},{5,1},{6,2},{7,3},{8,12},{9,13},{10,... | collective-permute-start | bytes 1572872 | tf_op jit(solution)/shard_map/ppermute | solution.py:285
  64.5 10.5 %collective-permute-start.17 = (bf16[16,128,128]{2,1,0:T(8,128)(2,1)S(1)}, bf16[16,128,128]{2,1,0:T(8,128)(2,1)S(1)}, u32[]{:S(2)}, u32[]{:S(2)}) collective-permute-start(bf16[16,128,128]{2,1,0:T(8,128)(2,1)S(1)} %get-tuple-element.66), channel_id=1, source_target_pairs={{0,2},{1,3},{2,0},{3,1},{4,6},{5,7},{6,4},{7,5},{8,10},{9,11},{10,... | collective-permute-start | bytes 1572872 | tf_op jit(solution)/shard_map/ppermute | solution.py:285
  65.6 10.0 %collective-permute-start.18 = (bf16[16,128,128]{2,1,0:T(8,128)(2,1)S(1)}, bf16[16,128,128]{2,1,0:T(8,128)(2,1)S(1)}, u32[]{:S(2)}, u32[]{:S(2)}) collective-permute-start(bf16[16,128,128]{2,1,0:T(8,128)(2,1)S(1)} %get-tuple-element.67), channel_id=1, source_target_pairs={{0,8},{1,9},{2,10},{3,11},{4,12},{5,13},{6,14},{7,15},{8,0},{9,1},... | collective-permute-start | bytes 1572872 | tf_op jit(solution)/shard_map/ppermute | solution.py:285
  67.4 9.6 %collective-permute-start.16 = (bf16[16,128,128]{2,1,0:T(8,128)(2,1)S(1)}, bf16[16,128,128]{2,1,0:T(8,128)(2,1)S(1)}, u32[]{:S(2)}, u32[]{:S(2)}) collective-permute-start(bf16[16,128,128]{2,1,0:T(8,128)(2,1)S(1)} %get-tuple-element.62.refs_7_), channel_id=1, source_target_pairs={{0,4},{1,5},{2,6},{3,7},{4,0},{5,1},{6,2},{7,3},{8,12},{9,13},{10,... | collective-permute-start | bytes 1572872 | tf_op jit(solution)/shard_map/ppermute | solution.py:285
  79.1 10.0 %collective-permute-start.19 = (f32[16,128,128]{2,1,0:T(8,128)S(1)}, f32[16,128,128]{2,1,0:T(8,128)S(1)}, u32[]{:S(2)}, u32[]{:S(2)}) collective-permute-start(f32[16,128,128]{2,1,0:T(8,128)S(1)} %get-tuple-element.72), channel_id=1, source_target_pairs={{0,1},{1,0},{2,3},{3,2},{4,5},{5,4},{6,7},{7,6},{8,9},{9,8},{10,11... | collective-permute-start | bytes 3145736 | tf_op jit(solution)/shard_map/ppermute | solution.py:285

commit v8 on v6

--- a/solution.py
+++ b/solution.py
@@ -325,7 +325,7 @@
     terms = term_words(source_device, source_block, right_env.shape[0], capacity)
     terms = (terms, swap(terms, core))
     acc, square, held["env"] = local_call(wavefunction, right_env, left_env, hops)
-    hold([(0, x), (0, y), "middle", (1, 0), "env"], terms[1])
+    hold(["middle", (1, 0), (0, y), (0, x), "env"], terms[1])
 
     held[0, xy] = swap(held[0, y], x)
     held[1, y] = swap(held[1, 0], y)

time: 90.8 us -> 90.8 us (level)
  waiting for transfers between devices: 29.5 us -> 27.5 us
  starting transfers between devices: 19.3 us -> 20.6 us
    ppermute x18, waiting for transfers between devices: 29.5 us -> 27.4 us  [swap(): return lax.ppermute(value, 'sector', [(i, i ^ mask) for i in range(owners)])]
    ppermute x18, starting transfers between devices: 19.3 us -> 20.6 us  [swap(): return lax.ppermute(value, 'sector', [(i, i ^ mask) for i in range(owners)])]
  transfers between devices with their start and end apart: 20 -> 20, of which waited for: 13 -> 12; matrix products, arithmetic and copies ran while one was open for 2% -> 2% of each run, Pallas kernels for 23% -> 23%
where the time goes in v8:
time: 90.8 us; the launch traced here: 90.4 us
  waiting for transfers between devices  27.5 us (30%)
  Pallas kernels  25.5 us (28%)
  starting transfers between devices  20.6 us (23%)
  blocking collectives  10.7 us (12%)
  local copies, waits for them, and re-layouts  4.97 us (5%)
    ppermute x18, waiting for transfers between devices, swap(): return lax.ppermute(value, 'sector', [(i, i ^ mask) for i in range(owners)])  27.4 us
    ppermute x18, starting transfers between devices, swap(): return lax.ppermute(value, 'sector', [(i, i ^ mask) for i in range(owners)])  20.6 us
    pallas_call x4, Pallas kernels, hop_call(): pl.pallas_call(functools.partial(hop_kernel, base, count, first, bool(ons...  13.8 us
    all_to_all x1, blocking collectives, spread_everywhere(): sums = lax.all_to_all(sums, 'sector', 0, 0, tiled=True)  10.7 us
    pallas_call x1, Pallas kernels, local_call(): pl.pallas_call(local_kernel, out_shape=(jax.ShapeDtypeStruct((sec, size,...  8.05 us
    unnamed x14, local copies, waits for them, and re-layouts  3.32 us
    pallas_call x5, Pallas kernels, hold_until(): pl.pallas_call(functools.partial(hold_kernel, count, move), out_shape=[ja...  2.37 us
  transfers between devices with their start and end apart: 20, of which 12 were waited for; matrix products, arithmetic and copies ran while one was open for 2% of the time, Pallas kernels for 23%

profile of v8, /device:TPU:0, one launch (start us, length us, event | category | flops | bytes accessed | tf_op | source)
XLA Modules:
  0.0 90.4 jit_solution(3760815284809496175)
XLA Ops:
  0.6 3.0 %collective-permute-start.4 = (bf16[16,128,128]{2,1,0:T(8,128)(2,1)}, bf16[16,128,128]{2,1,0:T(8,128)(2,1)S(1)}, u32[]{:S(2)}, u32[]{:S(2)}) collective-permute-start(bf16[16,128,128]{2,1,0:T(8,128)(2,1)} %psi.1), channel_id=1, source_target_pairs={{0,2},{1,3},{2,0},{3,1},{4,6},{5,7},{6,4},{7,5},{8,10},{9,11},{10,... | collective-permute-start | bytes 1572872 | tf_op jit(solution)/shard_map/ppermute | solution.py:285
  3.6 1.5 %collective-permute-start.3 = (bf16[16,128,128]{2,1,0:T(8,128)(2,1)}, bf16[16,128,128]{2,1,0:T(8,128)(2,1)S(1)}, u32[]{:S(2)}, u32[]{:S(2)}) collective-permute-start(bf16[16,128,128]{2,1,0:T(8,128)(2,1)} %psi.1), channel_id=1, source_target_pairs={{0,4},{1,5},{2,6},{3,7},{4,0},{5,1},{6,2},{7,3},{8,12},{9,13},{10,... | collective-permute-start | bytes 1572872 | tf_op jit(solution)/shard_map/ppermute | solution.py:285
  5.2 1.6 %collective-permute-start.2 = (bf16[16,128,128]{2,1,0:T(8,128)(2,1)}, bf16[16,128,128]{2,1,0:T(8,128)(2,1)}, u32[]{:S(2)}, u32[]{:S(2)}) collective-permute-start(bf16[16,128,128]{2,1,0:T(8,128)(2,1)} %psi.1), channel_id=1, source_target_pairs={{0,8},{1,9},{2,10},{3,11},{4,12},{5,13},{6,14},{7,15},{8,0},{9,1},... | collective-permute-start | bytes 1572872 | tf_op jit(solution)/shard_map/ppermute | solution.py:285
  6.7 0.0 collective-permute-start.1
  6.7 0.8 reshape.95
  7.5 0.8 reshape.96
  8.3 0.2 convert_reduce_fusion
  8.5 0.1 select_reduce_fusion.refs_1_
  8.6 0.6 collective-permute-start
  9.2 1.0 %copy-done = bf16[16,128,128]{2,1,0:T(8,128)(2,1)S(1)} copy-done((bf16[16,128,128]{2,1,0:T(8,128)(2,1)S(1)}, bf16[16,128,128]{2,1,0:T(8,128)(2,1)}, u32[]{:S(2)}) %copy-start) | copy-done | bytes 524312
  10.2 8.1 %local_channels.1 = (f32[16,128,128]{2,1,0:T(8,128)S(1)}, f32[128,128]{1,0:T(8,128)S(1)}, bf16[144,128,128]{2,1,0:T(8,128)(2,1)}) custom-call(bf16[4,4,128,128]{3,2,1,0:T(8,128)(2,1)S(1)} %bitcast.10, bf16[4,32,128,128]{3,2,1,0:T(8,128)(2,1)} %right.1, bf16[4,32,128,128]{3,2,1,0:T(8,128)(2,1)} %left.1), custom_call_target="tpu_custom_call" | custom-call | flops 1 | bytes 1 | tf_op jit(solution)/shard_map/local_channels/pallas_call | solution.py:107
  18.3 0.0 copy-start.4
  18.3 0.0 collective-permute-done.refs_5_.refs_2_
  18.3 0.0 collective-permute-done.4.refs_3_
  18.3 0.0 collective-permute-done.3.refs_2_
  18.3 0.2 collective-permute-done.2.refs_1_
  18.6 0.0 collective-permute-done.1.refs_0_
  18.6 0.0 copy-start.2
  18.6 0.0 copy-start.1
  18.6 0.1 collective-permute-start.5
  18.7 2.9 %collective-permute-start.6 = (bf16[16,128,128]{2,1,0:T(8,128)(2,1)S(1)}, bf16[16,128,128]{2,1,0:T(8,128)(2,1)}, u32[]{:S(2)}, u32[]{:S(2)}) collective-permute-start(bf16[16,128,128]{2,1,0:T(8,128)(2,1)S(1)} %get-tuple-element.40.refs_0_), channel_id=1, source_target_pairs={{0,8},{1,9},{2,10},{3,11},{4,12},{5,13},{6,14},{7,15},{8,0},{9,1},... | collective-permute-start | bytes 1572872 | tf_op jit(solution)/shard_map/ppermute | solution.py:285
  21.6 0.5 collective-permute-start.9
  22.2 0.0 copy-done.4
  22.2 0.5 collective-permute-start.8
  22.7 0.0 collective-permute-start.7
  22.7 11.4 %collective-permute-done.6.refs_1_ = bf16[16,128,128]{2,1,0:T(8,128)(2,1)} collective-permute-done((bf16[16,128,128]{2,1,0:T(8,128)(2,1)S(1)}, bf16[16,128,128]{2,1,0:T(8,128)(2,1)}, u32[]{:S(2)}, u32[]{:S(2)}) %collective-permute-start.6) | collective-permute-done | bytes 524320 | tf_op jit(solution)/shard_map/ppermute | solution.py:285
  34.0 1.1 %hold.6.refs_1_ = bf16[16,128,128]{2,1,0:T(8,128)(2,1)S(1)} custom-call(bf16[16,128,128]{2,1,0:T(8,128)(2,1)S(1)} %get-tuple-element.40.refs_0_, bf16[16,128,128]{2,1,0:T(8,128)(2,1)} %collective-permute-done.6.refs_1_, s32[1]{0:T(128)} %bitcast.5.refs_2_.refs_6_), custom_call_target="tpu_custom_call", output_to_operand_aliasing={{}: (0, {})} | custom-call | flops 1 | bytes 1 | tf_op jit(solution)/shard_map/hold/pallas_call | solution.py:227
  35.2 0.2 collective-permute-done.9.refs_4_
  35.4 0.6 collective-permute-done.8.refs_3_
  36.0 0.0 collective-permute-done.7.refs_2_
  36.0 0.0 collective-permute-done.5.refs_0_
  36.0 0.8 collective-permute-start.12
  36.8 0.0 copy-done.2
  36.8 1.3 %collective-permute-start.11 = (bf16[16,128,128]{2,1,0:T(8,128)(2,1)S(1)}, bf16[16,128,128]{2,1,0:T(8,128)(2,1)}, u32[]{:S(2)}, u32[]{:S(2)}) collective-permute-start(bf16[16,128,128]{2,1,0:T(8,128)(2,1)S(1)} %get-tuple-element.51.refs_6_), channel_id=1, source_target_pairs={{0,2},{1,3},{2,0},{3,1},{4,6},{5,7},{6,4},{7,5},{8,10},{9,11},{10,... | collective-permute-start | bytes 1572872 | tf_op jit(solution)/shard_map/ppermute | solution.py:285
  38.1 1.5 %collective-permute-start.10 = (bf16[16,128,128]{2,1,0:T(8,128)(2,1)S(1)}, bf16[16,128,128]{2,1,0:T(8,128)(2,1)S(1)}, u32[]{:S(2)}, u32[]{:S(2)}) collective-permute-start(bf16[16,128,128]{2,1,0:T(8,128)(2,1)S(1)} %get-tuple-element.51.refs_6_), channel_id=1, source_target_pairs={{0,4},{1,5},{2,6},{3,7},{4,0},{5,1},{6,2},{7,3},{8,12},{9,13},{10,... | collective-permute-start | bytes 1572872 | tf_op jit(solution)/shard_map/ppermute | solution.py:285
  39.6 0.1 concatenate.3.refs_0_
  39.7 0.0 copy-done.1
  39.7 0.0 copy-start.3
  39.7 1.0 %copy-done.3 = bf16[16,128,128]{2,1,0:T(8,128)(2,1)S(1)} copy-done((bf16[16,128,128]{2,1,0:T(8,128)(2,1)S(1)}, bf16[16,128,128]{2,1,0:T(8,128)(2,1)}, u32[]{:S(2)}) %copy-start.3) | copy-done | bytes 524312
  40.8 1.2 %copy-done.5 = f32[16,128,128]{2,1,0:T(8,128)S(1)} copy-done((f32[16,128,128]{2,1,0:T(8,128)S(1)}, f32[16,128,128]{2,1,0:T(8,128)}, u32[]{:S(2)}) %copy-start.5) | copy-done | bytes 1048600
  42.0 7.0 %hops_0.1 = (f32[16,128,128]{2,1,0:T(8,128)S(1)}, f32[16,128,128]{2,1,0:T(8,128)S(1)}, f32[8,128]{1,0:T(8,128)S(1)}, bf16[2,144,128,128]{3,2,1,0:T(8,128)(2,1)S(1)}) custom-call(s32[16]{0:T(128)S(1)} %concatenate.3.refs_0_, s32[256]{0:T(256)S(1)} %select_reduce_fusion.refs_1_, s32[256]{0:T(256)S(1)} %collective-permute-done.refs_5_.refs_2_, ...), custom_call_target="tpu_custom_call" | custom-call | flops 1 | bytes 1 | tf_op jit(solution)/shard_map/hops_0/pallas_call | solution.py:192
  49.0 0.0 collective-permute-done.12.refs_4_
  49.0 0.8 collective-permute-done.11.refs_3_
  49.8 0.6 collective-permute-done.10.refs_2_
  50.4 1.1 %hold.8 = (bf16[16,128,128]{2,1,0:T(8,128)(2,1)S(1)}, bf16[16,128,128]{2,1,0:T(8,128)(2,1)S(1)}, bf16[16,128,128]{2,1,0:T(8,128)(2,1)S(1)}, bf16[16,128,128]{2,1,0:T(8,128)(2,1)}) custom-call(bf16[16,128,128]{2,1,0:T(8,128)(2,1)S(1)} %get-tuple-element.52.refs_0_, ...), custom_call_target="tpu_custom_call", output_to_operand_aliasing={{0}: (0, {}), {1}: (1, {}), {2}: (2, {}), {3}: (3, {})} | custom-call | flops 1 | bytes 1 | tf_op jit(solution)/shard_map/hold/pallas_call | solution.py:227
  51.5 0.2 collective-permute-start.13
  51.8 1.0 %collective-permute-start.15 = (bf16[16,128,128]{2,1,0:T(8,128)(2,1)S(1)}, bf16[16,128,128]{2,1,0:T(8,128)(2,1)S(1)}, u32[]{:S(2)}, u32[]{:S(2)}) collective-permute-start(bf16[16,128,128]{2,1,0:T(8,128)(2,1)S(1)} %get-tuple-element.56.refs_9_), channel_id=1, source_target_pairs={{0,2},{1,3},{2,0},{3,1},{4,6},{5,7},{6,4},{7,5},{8,10},{9,11},{10,... | collective-permute-start | bytes 1572872 | tf_op jit(solution)/shard_map/ppermute | solution.py:285
  52.7 1.3 %collective-permute-start.14 = (bf16[16,128,128]{2,1,0:T(8,128)(2,1)S(1)}, bf16[16,128,128]{2,1,0:T(8,128)(2,1)S(1)}, u32[]{:S(2)}, u32[]{:S(2)}) collective-permute-start(bf16[16,128,128]{2,1,0:T(8,128)(2,1)S(1)} %get-tuple-element.56.refs_9_), channel_id=1, source_target_pairs={{0,4},{1,5},{2,6},{3,7},{4,0},{5,1},{6,2},{7,3},{8,12},{9,13},{10,... | collective-permute-start | bytes 1572872 | tf_op jit(solution)/shard_map/ppermute | solution.py:285
  54.0 2.7 %hops_1.1 = (f32[16,128,128]{2,1,0:T(8,128)S(1)}, f32[16,128,128]{2,1,0:T(8,128)S(1)}, f32[8,128]{1,0:T(8,128)S(1)}) custom-call(s32[16]{0:T(128)S(1)} %concatenate.3.refs_0_, s32[256]{0:T(256)S(1)} %select_reduce_fusion.refs_1_, s32[256]{0:T(256)S(1)} %collective-permute-done.refs_5_.refs_2_, bf16[2,144,128,128]{3,2,1,0:T(8,128)(2,1)S(1)} %get-tuple-element.48.refs_3_, ...), custom_call_target="tpu_custom_call" | custom-call | flops 1 | bytes 1 | tf_op jit(solution)/shard_map/hops_1/pallas_call | solution.py:192
  56.7 6.3 %collective-permute-done.13.refs_0_ = bf16[16,128,128]{2,1,0:T(8,128)(2,1)S(1)} collective-permute-done((bf16[16,128,128]{2,1,0:T(8,128)(2,1)S(1)}, bf16[16,128,128]{2,1,0:T(8,128)(2,1)S(1)}, u32[]{:S(2)}, u32[]{:S(2)}) %collective-permute-start.13) | collective-permute-done | bytes 524320 | tf_op jit(solution)/shard_map/ppermute | solution.py:285
  63.0 0.1 collective-permute-done.15.refs_4_
  63.1 1.1 %collective-permute-done.14.refs_3_ = bf16[16,128,128]{2,1,0:T(8,128)(2,1)S(1)} collective-permute-done((bf16[16,128,128]{2,1,0:T(8,128)(2,1)S(1)}, bf16[16,128,128]{2,1,0:T(8,128)(2,1)S(1)}, u32[]{:S(2)}, u32[]{:S(2)}) %collective-permute-start.14) | collective-permute-done | bytes 524320 | tf_op jit(solution)/shard_map/ppermute | solution.py:285
  64.3 1.9 %collective-permute-start.16 = (bf16[16,128,128]{2,1,0:T(8,128)(2,1)S(1)}, bf16[16,128,128]{2,1,0:T(8,128)(2,1)S(1)}, u32[]{:S(2)}, u32[]{:S(2)}) collective-permute-start(bf16[16,128,128]{2,1,0:T(8,128)(2,1)S(1)} %get-tuple-element.66), channel_id=1, source_target_pairs={{0,8},{1,9},{2,10},{3,11},{4,12},{5,13},{6,14},{7,15},{8,0},{9,1},... | collective-permute-start | bytes 1572872 | tf_op jit(solution)/shard_map/ppermute | solution.py:285
  66.1 0.5 collective-permute-start.17
  66.6 1.3 %collective-permute-start.18 = (bf16[16,128,128]{2,1,0:T(8,128)(2,1)S(1)}, bf16[16,128,128]{2,1,0:T(8,128)(2,1)S(1)}, u32[]{:S(2)}, u32[]{:S(2)}) collective-permute-start(bf16[16,128,128]{2,1,0:T(8,128)(2,1)S(1)} %get-tuple-element.62.refs_7_), channel_id=1, source_target_pairs={{0,4},{1,5},{2,6},{3,7},{4,0},{5,1},{6,2},{7,3},{8,12},{9,13},{10,... | collective-permute-start | bytes 1572872 | tf_op jit(solution)/shard_map/ppermute | solution.py:285
  68.0 2.2 %hops_2.1 = (f32[16,128,128]{2,1,0:T(8,128)S(1)}, f32[16,128,128]{2,1,0:T(8,128)S(1)}, f32[128,128]{1,0:T(8,128)S(1)}) custom-call(s32[16]{0:T(128)S(1)} %concatenate.3.refs_0_, s32[256]{0:T(256)S(1)} %select_reduce_fusion.refs_1_, s32[256]{0:T(256)S(1)} %collective-permute-done.refs_5_.refs_2_, bf16[2,144,128,128]{3,2,1,0:T(8,128)(2,1)S(1)} %get-tuple-element.48.refs_3_, ...), custom_call_target="tpu_custom_call" | custom-call | flops 1 | bytes 1 | tf_op jit(solution)/shard_map/hops_2/pallas_call | solution.py:192
  70.2 4.7 %collective-permute-done.16.refs_6_ = bf16[16,128,128]{2,1,0:T(8,128)(2,1)S(1)} collective-permute-done((bf16[16,128,128]{2,1,0:T(8,128)(2,1)S(1)}, bf16[16,128,128]{2,1,0:T(8,128)(2,1)S(1)}, u32[]{:S(2)}, u32[]{:S(2)}) %collective-permute-start.16) | collective-permute-done | bytes 524320 | tf_op jit(solution)/shard_map/ppermute | solution.py:285
  74.9 1.1 %collective-permute-done.17.refs_7_ = bf16[16,128,128]{2,1,0:T(8,128)(2,1)S(1)} collective-permute-done((bf16[16,128,128]{2,1,0:T(8,128)(2,1)S(1)}, bf16[16,128,128]{2,1,0:T(8,128)(2,1)S(1)}, u32[]{:S(2)}, u32[]{:S(2)}) %collective-permute-start.17) | collective-permute-done | bytes 524320 | tf_op jit(solution)/shard_map/ppermute | solution.py:285
  76.0 0.3 collective-permute-done.18.refs_8_
  76.3 2.0 %hops_3.1 = (f32[16,128,128]{2,1,0:T(8,128)S(1)}, f32[16,128,128]{2,1,0:T(8,128)S(1)}, f32[32,128]{1,0:T(8,128)S(1)}) custom-call(s32[16]{0:T(128)S(1)} %concatenate.3.refs_0_, s32[256]{0:T(256)S(1)} %select_reduce_fusion.refs_1_, s32[256]{0:T(256)S(1)} %collective-permute-done.refs_5_.refs_2_, bf16[2,144,128,128]{3,2,1,0:T(8,128)(2,1)S(1)} %get-tuple-element.48.refs_3_, ...), custom_call_target="tpu_custom_call" | custom-call | flops 1 | bytes 1 | tf_op jit(solution)/shard_map/hops_3/pallas_call | solution.py:192
  78.3 0.1 collective-permute-start.19
  78.4 10.7 %all_to_all.11 = f32[32,1,128]{2,1,0:T(1,128)S(1)} all-to-all(f32[32,1,128]{2,1,0:T(1,128)S(1)} %bitcast.12), channel_id=1, replica_groups=mesh['groups'=1,'sector'=32] {'sector'}, dimensions={0} | all-to-all | bytes 32768 | tf_op jit(solution)/shard_map/all_to_all | solution.py:356
  89.1 0.0 collective-permute-done.19.theirs
  89.1 1.3 %finish.1 = (bf16[16,128,128]{2,1,0:T(8,128)(2,1)}, bf16[16,128,128]{2,1,0:T(8,128)(2,1)}, f32[1]{0:T(128)}) custom-call(f32[32,128]{1,0:T(8,128)S(1)} %bitcast.11, bf16[16,128,128]{2,1,0:T(8,128)(2,1)S(1)} %copy-done.1, f32[16,128,128]{2,1,0:T(8,128)S(1)} %get-tuple-element.71.mine, f32[16,128,128]{2,1,0:T(8,128)S(1)} %collective-permute-done.19.theirs), custom_call_target="tpu_custom_call" | custom-call | tf_op jit(solution)/shard_map/finish/pallas_call | solution.py:253
  (8 shorter events, 0.1 us)
Async XLA Ops:
  0.6 17.7 %collective-permute-start.4 = (bf16[16,128,128]{2,1,0:T(8,128)(2,1)}, bf16[16,128,128]{2,1,0:T(8,128)(2,1)S(1)}, u32[]{:S(2)}, u32[]{:S(2)}) collective-permute-start(bf16[16,128,128]{2,1,0:T(8,128)(2,1)} %psi.1), channel_id=1, source_target_pairs={{0,2},{1,3},{2,0},{3,1},{4,6},{5,7},{6,4},{7,5},{8,10},{9,11},{10,... | collective-permute-start | bytes 1572872 | tf_op jit(solution)/shard_map/ppermute | solution.py:285
  3.6 14.7 %collective-permute-start.3 = (bf16[16,128,128]{2,1,0:T(8,128)(2,1)}, bf16[16,128,128]{2,1,0:T(8,128)(2,1)S(1)}, u32[]{:S(2)}, u32[]{:S(2)}) collective-permute-start(bf16[16,128,128]{2,1,0:T(8,128)(2,1)} %psi.1), channel_id=1, source_target_pairs={{0,4},{1,5},{2,6},{3,7},{4,0},{5,1},{6,2},{7,3},{8,12},{9,13},{10,... | collective-permute-start | bytes 1572872 | tf_op jit(solution)/shard_map/ppermute | solution.py:285
  5.2 13.4 %collective-permute-start.2 = (bf16[16,128,128]{2,1,0:T(8,128)(2,1)}, bf16[16,128,128]{2,1,0:T(8,128)(2,1)}, u32[]{:S(2)}, u32[]{:S(2)}) collective-permute-start(bf16[16,128,128]{2,1,0:T(8,128)(2,1)} %psi.1), channel_id=1, source_target_pairs={{0,8},{1,9},{2,10},{3,11},{4,12},{5,13},{6,14},{7,15},{8,0},{9,1},... | collective-permute-start | bytes 1572872 | tf_op jit(solution)/shard_map/ppermute | solution.py:285
  6.7 11.8 %collective-permute-start.1 = (bf16[16,128,128]{2,1,0:T(8,128)(2,1)}, bf16[16,128,128]{2,1,0:T(8,128)(2,1)S(1)}, u32[]{:S(2)}, u32[]{:S(2)}) collective-permute-start(bf16[16,128,128]{2,1,0:T(8,128)(2,1)} %psi.1), channel_id=1, source_target_pairs={{0,1},{1,0},{2,3},{3,2},{4,5},{5,4},{6,7},{7,6},{8,16},{9,17},{10,... | collective-permute-start | bytes 1572872 | tf_op jit(solution)/shard_map/ppermute | solution.py:292
  8.6 9.7 %collective-permute-start = (s32[256]{0:T(256)S(1)}, s32[256]{0:T(256)S(1)}, u32[]{:S(2)}, u32[]{:S(2)}) collective-permute-start(s32[256]{0:T(256)S(1)} %select_reduce_fusion.refs_1_), channel_id=1, source_target_pairs={{0,1},{1,0},{2,3},{3,2},{4,5},{5,4},{6,7},{7,6},{8,9},{9,8},{10,11... | collective-permute-start | bytes 3080 | tf_op jit(solution)/shard_map/ppermute | solution.py:285
  9.2 1.0 %copy-start = (bf16[16,128,128]{2,1,0:T(8,128)(2,1)S(1)}, bf16[16,128,128]{2,1,0:T(8,128)(2,1)}, u32[]{:S(2)}) copy-start(bf16[16,128,128]{2,1,0:T(8,128)(2,1)} %psi.1) | copy-start | bytes 1572868
  18.3 3.9 %copy-start.4 = (f32[16,128,128]{2,1,0:T(8,128)}, f32[16,128,128]{2,1,0:T(8,128)S(1)}, u32[]{:S(2)}) copy-start(f32[16,128,128]{2,1,0:T(8,128)S(1)} %get-tuple-element.44.refs_5_) | copy-start | bytes 3145732
  18.6 18.2 %copy-start.2 = (bf16[16,128,128]{2,1,0:T(8,128)(2,1)}, bf16[16,128,128]{2,1,0:T(8,128)(2,1)S(1)}, u32[]{:S(2)}) copy-start(bf16[16,128,128]{2,1,0:T(8,128)(2,1)S(1)} %get-tuple-element.42.refs_8_) | copy-start | bytes 1572868
  18.6 21.1 %copy-start.1 = (bf16[16,128,128]{2,1,0:T(8,128)(2,1)S(1)}, bf16[16,128,128]{2,1,0:T(8,128)(2,1)}, u32[]{:S(2)}) copy-start(bf16[16,128,128]{2,1,0:T(8,128)(2,1)} %psi.1) | copy-start | bytes 1572868
  18.6 17.3 %collective-permute-start.5 = (bf16[144,128,128]{2,1,0:T(8,128)(2,1)}, bf16[144,128,128]{2,1,0:T(8,128)(2,1)}, u32[]{:S(2)}, u32[]{:S(2)}) collective-permute-start(bf16[144,128,128]{2,1,0:T(8,128)(2,1)} %get-tuple-element.39.refs_3_), channel_id=1, source_target_pairs={{0,1},{1,0},{2,3},{3,2},{4,5},{5,4},{6,7},{7,6},{8,9},{9,8},{10,11... | collective-permute-start | bytes 14155784 | tf_op jit(solution)/shard_map/ppermute | solution.py:285
  18.7 15.3 %collective-permute-start.6 = (bf16[16,128,128]{2,1,0:T(8,128)(2,1)S(1)}, bf16[16,128,128]{2,1,0:T(8,128)(2,1)}, u32[]{:S(2)}, u32[]{:S(2)}) collective-permute-start(bf16[16,128,128]{2,1,0:T(8,128)(2,1)S(1)} %get-tuple-element.40.refs_0_), channel_id=1, source_target_pairs={{0,8},{1,9},{2,10},{3,11},{4,12},{5,13},{6,14},{7,15},{8,0},{9,1},... | collective-permute-start | bytes 1572872 | tf_op jit(solution)/shard_map/ppermute | solution.py:285
  21.6 13.8 %collective-permute-start.9 = (bf16[16,128,128]{2,1,0:T(8,128)(2,1)S(1)}, bf16[16,128,128]{2,1,0:T(8,128)(2,1)S(1)}, u32[]{:S(2)}, u32[]{:S(2)}) collective-permute-start(bf16[16,128,128]{2,1,0:T(8,128)(2,1)S(1)} %get-tuple-element.42.refs_8_), channel_id=1, source_target_pairs={{0,2},{1,3},{2,0},{3,1},{4,6},{5,7},{6,4},{7,5},{8,10},{9,11},{10,... | collective-permute-start | bytes 1572872 | tf_op jit(solution)/shard_map/ppermute | solution.py:285
  22.2 13.8 %collective-permute-start.8 = (bf16[16,128,128]{2,1,0:T(8,128)(2,1)}, bf16[16,128,128]{2,1,0:T(8,128)(2,1)}, u32[]{:S(2)}, u32[]{:S(2)}) collective-permute-start(bf16[16,128,128]{2,1,0:T(8,128)(2,1)} %get-tuple-element.41.refs_9_), channel_id=1, source_target_pairs={{0,4},{1,5},{2,6},{3,7},{4,0},{5,1},{6,2},{7,3},{8,12},{9,13},{10,... | collective-permute-start | bytes 1572872 | tf_op jit(solution)/shard_map/ppermute | solution.py:285
  22.7 13.3 %collective-permute-start.7 = (bf16[16,128,128]{2,1,0:T(8,128)(2,1)}, bf16[16,128,128]{2,1,0:T(8,128)(2,1)S(1)}, u32[]{:S(2)}, u32[]{:S(2)}) collective-permute-start(bf16[16,128,128]{2,1,0:T(8,128)(2,1)} %get-tuple-element.41.refs_9_), channel_id=1, source_target_pairs={{0,1},{1,0},{2,3},{3,2},{4,5},{5,4},{6,7},{7,6},{8,16},{9,17},{10,... | collective-permute-start | bytes 1572872 | tf_op jit(solution)/shard_map/ppermute | solution.py:292
  36.0 13.0 %collective-permute-start.12 = (bf16[16,128,128]{2,1,0:T(8,128)(2,1)S(1)}, bf16[16,128,128]{2,1,0:T(8,128)(2,1)}, u32[]{:S(2)}, u32[]{:S(2)}) collective-permute-start(bf16[16,128,128]{2,1,0:T(8,128)(2,1)S(1)} %get-tuple-element.52.refs_0_), channel_id=1, source_target_pairs={{0,8},{1,9},{2,10},{3,11},{4,12},{5,13},{6,14},{7,15},{8,0},{9,1},... | collective-permute-start | bytes 1572872 | tf_op jit(solution)/shard_map/ppermute | solution.py:285
  36.8 13.0 %collective-permute-start.11 = (bf16[16,128,128]{2,1,0:T(8,128)(2,1)S(1)}, bf16[16,128,128]{2,1,0:T(8,128)(2,1)}, u32[]{:S(2)}, u32[]{:S(2)}) collective-permute-start(bf16[16,128,128]{2,1,0:T(8,128)(2,1)S(1)} %get-tuple-element.51.refs_6_), channel_id=1, source_target_pairs={{0,2},{1,3},{2,0},{3,1},{4,6},{5,7},{6,4},{7,5},{8,10},{9,11},{10,... | collective-permute-start | bytes 1572872 | tf_op jit(solution)/shard_map/ppermute | solution.py:285
  38.1 12.3 %collective-permute-start.10 = (bf16[16,128,128]{2,1,0:T(8,128)(2,1)S(1)}, bf16[16,128,128]{2,1,0:T(8,128)(2,1)S(1)}, u32[]{:S(2)}, u32[]{:S(2)}) collective-permute-start(bf16[16,128,128]{2,1,0:T(8,128)(2,1)S(1)} %get-tuple-element.51.refs_6_), channel_id=1, source_target_pairs={{0,4},{1,5},{2,6},{3,7},{4,0},{5,1},{6,2},{7,3},{8,12},{9,13},{10,... | collective-permute-start | bytes 1572872 | tf_op jit(solution)/shard_map/ppermute | solution.py:285
  39.7 1.0 %copy-start.3 = (bf16[16,128,128]{2,1,0:T(8,128)(2,1)S(1)}, bf16[16,128,128]{2,1,0:T(8,128)(2,1)}, u32[]{:S(2)}) copy-start(bf16[16,128,128]{2,1,0:T(8,128)(2,1)} %copy-done.2) | copy-start | bytes 1572868
  40.8 1.2 %copy-start.5 = (f32[16,128,128]{2,1,0:T(8,128)S(1)}, f32[16,128,128]{2,1,0:T(8,128)}, u32[]{:S(2)}) copy-start(f32[16,128,128]{2,1,0:T(8,128)} %copy-done.4) | copy-start | bytes 3145732
  42.0 12.0 %copy-start.6 = (f32[16]{0:T(128)S(1)}, f32[16]{0:T(128)}, u32[]{:S(2)}) copy-start(f32[16]{0:T(128)} %refs_10_.1) | copy-start | bytes 196
  51.5 11.5 %collective-permute-start.13 = (bf16[16,128,128]{2,1,0:T(8,128)(2,1)S(1)}, bf16[16,128,128]{2,1,0:T(8,128)(2,1)S(1)}, u32[]{:S(2)}, u32[]{:S(2)}) collective-permute-start(bf16[16,128,128]{2,1,0:T(8,128)(2,1)S(1)} %get-tuple-element.59), channel_id=1, source_target_pairs={{0,8},{1,9},{2,10},{3,11},{4,12},{5,13},{6,14},{7,15},{8,0},{9,1},... | collective-permute-start | bytes 1572872 | tf_op jit(solution)/shard_map/ppermute | solution.py:285
  51.8 11.4 %collective-permute-start.15 = (bf16[16,128,128]{2,1,0:T(8,128)(2,1)S(1)}, bf16[16,128,128]{2,1,0:T(8,128)(2,1)S(1)}, u32[]{:S(2)}, u32[]{:S(2)}) collective-permute-start(bf16[16,128,128]{2,1,0:T(8,128)(2,1)S(1)} %get-tuple-element.56.refs_9_), channel_id=1, source_target_pairs={{0,2},{1,3},{2,0},{3,1},{4,6},{5,7},{6,4},{7,5},{8,10},{9,11},{10,... | collective-permute-start | bytes 1572872 | tf_op jit(solution)/shard_map/ppermute | solution.py:285
  52.7 11.5 %collective-permute-start.14 = (bf16[16,128,128]{2,1,0:T(8,128)(2,1)S(1)}, bf16[16,128,128]{2,1,0:T(8,128)(2,1)S(1)}, u32[]{:S(2)}, u32[]{:S(2)}) collective-permute-start(bf16[16,128,128]{2,1,0:T(8,128)(2,1)S(1)} %get-tuple-element.56.refs_9_), channel_id=1, source_target_pairs={{0,4},{1,5},{2,6},{3,7},{4,0},{5,1},{6,2},{7,3},{8,12},{9,13},{10,... | collective-permute-start | bytes 1572872 | tf_op jit(solution)/shard_map/ppermute | solution.py:285
  64.3 10.6 %collective-permute-start.16 = (bf16[16,128,128]{2,1,0:T(8,128)(2,1)S(1)}, bf16[16,128,128]{2,1,0:T(8,128)(2,1)S(1)}, u32[]{:S(2)}, u32[]{:S(2)}) collective-permute-start(bf16[16,128,128]{2,1,0:T(8,128)(2,1)S(1)} %get-tuple-element.66), channel_id=1, source_target_pairs={{0,8},{1,9},{2,10},{3,11},{4,12},{5,13},{6,14},{7,15},{8,0},{9,1},... | collective-permute-start | bytes 1572872 | tf_op jit(solution)/shard_map/ppermute | solution.py:285
  66.1 9.9 %collective-permute-start.17 = (bf16[16,128,128]{2,1,0:T(8,128)(2,1)S(1)}, bf16[16,128,128]{2,1,0:T(8,128)(2,1)S(1)}, u32[]{:S(2)}, u32[]{:S(2)}) collective-permute-start(bf16[16,128,128]{2,1,0:T(8,128)(2,1)S(1)} %get-tuple-element.67), channel_id=1, source_target_pairs={{0,2},{1,3},{2,0},{3,1},{4,6},{5,7},{6,4},{7,5},{8,10},{9,11},{10,... | collective-permute-start | bytes 1572872 | tf_op jit(solution)/shard_map/ppermute | solution.py:285
  66.6 9.6 %collective-permute-start.18 = (bf16[16,128,128]{2,1,0:T(8,128)(2,1)S(1)}, bf16[16,128,128]{2,1,0:T(8,128)(2,1)S(1)}, u32[]{:S(2)}, u32[]{:S(2)}) collective-permute-start(bf16[16,128,128]{2,1,0:T(8,128)(2,1)S(1)} %get-tuple-element.62.refs_7_), channel_id=1, source_target_pairs={{0,4},{1,5},{2,6},{3,7},{4,0},{5,1},{6,2},{7,3},{8,12},{9,13},{10,... | collective-permute-start | bytes 1572872 | tf_op jit(solution)/shard_map/ppermute | solution.py:285
  78.3 10.8 %collective-permute-start.19 = (f32[16,128,128]{2,1,0:T(8,128)S(1)}, f32[16,128,128]{2,1,0:T(8,128)S(1)}, u32[]{:S(2)}, u32[]{:S(2)}) collective-permute-start(f32[16,128,128]{2,1,0:T(8,128)S(1)} %get-tuple-element.72), channel_id=1, source_target_pairs={{0,1},{1,0},{2,3},{3,2},{4,5},{5,4},{6,7},{7,6},{8,9},{9,8},{10,11... | collective-permute-start | bytes 3145736 | tf_op jit(solution)/shard_map/ppermute | solution.py:285
